TPU v7x, 32 devices: a whole 2x2x4 slice. The times are simulated.
32 devices in a mesh: ep: 32 (over z, y, x, core).
Axes of the slice: x: 2, y: 2, z: 4, core: 2. Of those that a mesh axis runs over, the one named last changes fastest.
Arguments:
- tokens: bfloat16 [2, 512, 3584], P(None, 'ep'), may hold values from -6 to 6
- expert_ids: int32 [2, 512, 8], P(None, 'ep'), may hold values from 0 to 31, all different within a row; in each aligned block of 16 rows (0 to 15, 16 to 31, ..., all dimensions but the last counted through in order) at most 8 rows name the same one
- combine_weights: float32 [2, 512, 8], P(None, 'ep'), may hold values from 0.05 to 0.5
- w_gate: bfloat16 [32, 3584, 1024], P('ep'), may hold values from -0.09375 to 0.09375
- w_up: bfloat16 [32, 3584, 1024], P('ep'), may hold values from -0.09375 to 0.09375
- w_down: bfloat16 [32, 1024, 3584], P('ep'), may hold values from -0.1875 to 0.1875
- shared_weights: bfloat16 [3, 3584, 4096], P(None, None, 'ep'), as said below
Outputs:
- moe_out: bfloat16 [2, 512, 3584], P(None, 'ep')
Inputs may be any that keep to these rules, and one draw needn't show every extreme that they name: `expert_ids`: in each step the 16 rows of one device name any one expert at most 8 times; the 8 experts of a token differ. `shared_weights`: the array is 4 equal copies of one block of 1024 columns, laid end to end along the last dimension.
All inputs are finite; a program needn't handle non-finite values.
Results may differ from a plain program's by a relative error of at most 0.0055.
Values may be sent and summed in bfloat16 or wider, within the bound.
No kernel may reach another device: no remote copies, remote signals or barrier semaphores. Data moves between devices by JAX's collectives and lax.ppermute only.
A program may use at most 128 MiB of HBM per device.

v0:
```python
import jax
import jax.numpy as jnp
from jax import lax
from jax.sharding import PartitionSpec as P


def partner_2(block, axis, apart):
    count = lax.axis_size(axis)
    route = []
    for low in range(count):
        high = low | 1 << apart
        if high != low and high < count:
            route += [(low, high), (high, low)]
    return lax.ppermute(block, axis, route)


def expert_rows(token_rows, gate_mat, up_mat, down_mat):
    gate_val = jnp.dot(token_rows, gate_mat, preferred_element_type=jnp.float32)
    up_val = jnp.dot(token_rows, up_mat, preferred_element_type=jnp.float32)
    hidden = (jax.nn.silu(gate_val) * up_val).astype(jnp.bfloat16)
    return jnp.dot(hidden, down_mat, preferred_element_type=jnp.float32).astype(jnp.bfloat16)


def route_tables(step_ids, step_weights, experts, capacity):
    row_count, top_count = step_ids.shape
    pair_count = row_count * top_count
    flat_ids = step_ids.reshape(pair_count)
    onehot = (flat_ids[:, None] == jnp.arange(experts, dtype=jnp.int32)[None, :]).astype(
        jnp.float32
    )
    earlier = (jnp.arange(pair_count)[:, None] > jnp.arange(pair_count)[None, :]).astype(
        jnp.float32
    )
    counts = jnp.dot(earlier, onehot, precision=lax.Precision.HIGHEST)
    slot_index = jnp.sum(counts * onehot, axis=1).astype(jnp.int32)
    position = flat_ids * capacity + slot_index
    placing = (
        position[:, None] == jnp.arange(experts * capacity, dtype=jnp.int32)[None, :]
    ).astype(jnp.float32)
    owner = (
        (jnp.arange(pair_count) // top_count)[:, None] == jnp.arange(row_count)[None, :]
    ).astype(jnp.float32)
    dispatch = jnp.dot(placing.T, owner, precision=lax.Precision.HIGHEST).astype(jnp.bfloat16)
    combine = jnp.dot(
        (owner * step_weights.reshape(pair_count)[:, None]).T,
        placing,
        precision=lax.Precision.HIGHEST,
    )
    return (dispatch, combine)


def join_halves(mine, partner, upper_side, axis_no):
    return jnp.where(
        upper_side,
        jnp.concatenate([partner, mine], axis=axis_no),
        jnp.concatenate([mine, partner], axis=axis_no),
    )


def shared_expert(tokens, shared_weights):
    my_index = lax.axis_index("ep")
    step_count, row_count, model_width = tokens.shape
    gathered = tokens
    for level in range(3):
        partner = partner_2(gathered, "ep", level)
        gathered = join_halves(gathered, partner, my_index >> level & 1 == 1, 1)
    flat_rows = gathered.reshape(-1, model_width)
    gate_val = jnp.dot(flat_rows, shared_weights[0], preferred_element_type=jnp.float32)
    up_val = jnp.dot(flat_rows, shared_weights[1], preferred_element_type=jnp.float32)
    hidden = (jax.nn.silu(gate_val) * up_val).astype(jnp.bfloat16)
    partial_value = lax.dot_general(
        hidden, shared_weights[2], (((1,), (1,)), ((), ())), preferred_element_type=jnp.float32
    )
    partial_value = partial_value.reshape(step_count, 8 * row_count, model_width)
    for level in (2, 1, 0):
        half_rows = partial_value.shape[1] // 2
        upper_side = my_index >> level & 1 == 1
        lower_part = partial_value[:, :half_rows]
        upper_part = partial_value[:, half_rows:]
        kept_rows = jnp.where(upper_side, upper_part, lower_part)
        sent_rows = jnp.where(upper_side, lower_part, upper_part)
        partial_value = kept_rows + partner_2(sent_rows, "ep", level)
    return partial_value


def shards(tokens, expert_ids, combine_weights, w_gate, w_up, w_down, shared_weights):
    step_count, row_count, model_width = tokens.shape
    top_count = expert_ids.shape[2]
    device_count = lax.axis_size("ep")
    experts = w_gate.shape[0] * device_count
    capacity = max(2, row_count * top_count * 2 // experts)
    tables = [
        route_tables(expert_ids[s], combine_weights[s], experts, capacity)
        for s in range(step_count)
    ]
    outgoing = jnp.stack(
        [
            jnp.dot(tables[s][0], tokens[s], preferred_element_type=jnp.float32)
            .astype(jnp.bfloat16)
            .reshape(experts, capacity, model_width)
            for s in range(step_count)
        ]
    )
    received = lax.all_to_all(outgoing, "ep", split_axis=1, concat_axis=1, tiled=True)
    returned = lax.all_to_all(
        expert_rows(received.reshape(-1, model_width), w_gate[0], w_up[0], w_down[0]).reshape(
            received.shape
        ),
        "ep",
        split_axis=1,
        concat_axis=1,
        tiled=True,
    )
    shared = shared_expert(tokens, shared_weights)
    routed = jnp.stack(
        [
            jnp.dot(
                tables[s][1],
                returned[s].reshape(experts * capacity, model_width).astype(jnp.float32),
                precision=lax.Precision.HIGHEST,
            )
            for s in range(step_count)
        ]
    )
    return (shared + routed).astype(jnp.bfloat16)


def solution(mesh):
    placed = (
        P(None, "ep", None),
        P(None, "ep", None),
        P(None, "ep", None),
        P("ep", None, None),
        P("ep", None, None),
        P("ep", None, None),
        P(None, None, "ep"),
    )
    return jax.shard_map(
        shards, mesh=mesh, in_specs=placed, out_specs=P(None, "ep", None), check_vma=False
    )
```

profile of v0, /device:TPU:0, one launch (start us, length us, event | category | flops | bytes accessed | tf_op | source)
XLA Modules:
  0.0 242.6 jit_solution(11706215771409528933)
XLA Ops:
  0.0 0.7 fusion.53
  2.0 1.6 fusion.10
  3.5 0.7 fusion.9
  4.2 2.2 pad_maximum_fusion
  6.4 7.4 %all-to-all-start = ((bf16[2,32,8,3584]{3,2,0,1:T(8,128)(2,1)}), bf16[2,32,8,3584]{3,2,0,1:T(8,128)(2,1)}, u32[]{:S(2)}, u32[]{:S(2)}) async-start(bf16[2,32,8,3584]{3,2,0,1:T(8,128)(2,1)} %pad_maximum_fusion), calls=%async_computation | async-start | bytes 7340032 | tf_op jit(solution)/shard_map/all_to_all | solution.py:104
  14.1 1.3 collective-permute-done
  15.5 1.8 collective-permute-start.1
  17.3 40.9 %collective-permute-done.1 = bf16[2,32,3584]{2,1,0:T(8,128)(2,1)S(1)} collective-permute-done((bf16[2,32,3584]{2,1,0:T(8,128)(2,1)S(1)}, bf16[2,32,3584]{2,1,0:T(8,128)(2,1)S(1)}, u32[]{:S(2)}, u32[]{:S(2)}) %collective-permute-start.1) | collective-permute-done | bytes 458784 | tf_op jit(solution)/shard_map/ppermute | solution.py:14
  58.3 2.3 collective-permute-start.2
  60.6 28.2 %collective-permute-done.2 = bf16[2,64,3584]{2,1,0:T(8,128)(2,1)S(1)} collective-permute-done((bf16[2,64,3584]{2,1,0:T(8,128)(2,1)S(1)}, bf16[2,64,3584]{2,1,0:T(8,128)(2,1)S(1)}, u32[]{:S(2)}, u32[]{:S(2)}) %collective-permute-start.2) | collective-permute-done | bytes 917536 | tf_op jit(solution)/shard_map/ppermute | solution.py:14
  88.8 0.4 maximum_select_fusion
  89.2 0.6 fusion.19
  89.8 0.6 multiply_convert_fusion.1
  90.5 2.4 %fusion.15 = f32[2,128,3584]{2,1,0:T(8,128)} fusion(bf16[2,128,128]{2,1,0:T(8,128)(2,1)S(1)} %bitcast.69, bf16[3,3584,128]{2,1,0:T(8,128)(2,1)S(1)} %copy-done.3), kind=kOutput, calls=%fused_computation.27 | convolution fusion | flops 234881024 | bytes 4653056 | tf_op jit(solution)/shard_map/dot_general | solution.py:71
  92.9 3.8 %all-to-all-done = bf16[2,32,8,3584]{3,2,0,1:T(8,128)(2,1)} async-done(((bf16[2,32,8,3584]{3,2,0,1:T(8,128)(2,1)}), bf16[2,32,8,3584]{3,2,0,1:T(8,128)(2,1)}, u32[]{:S(2)}, u32[]{:S(2)}) %all-to-all-start) | async-done | bytes 3670048 | tf_op jit(solution)/shard_map/all_to_all | solution.py:104
  96.7 2.3 copy.28
  99.0 1.8 copy-done.1
  100.8 6.2 %fusion.2 = f32[512,1024]{1,0:T(8,128)S(1)} fusion(bf16[512,3584]{1,0:T(8,128)(2,1)S(1)} %bitcast.64, bf16[1,3584,1024]{2,1,0:T(8,128)(2,1)} %param.11), kind=kOutput, calls=%fused_computation.2 | convolution fusion | flops 3758096384 | bytes 13107200 | tf_op jit(solution)/shard_map/dot_general | solution.py:19
  107.1 16.1 %fusion.6 = bf16[512,3584]{1,0:T(8,128)(2,1)} fusion(bf16[1,1024,3584]{2,1,0:T(8,128)(2,1)} %param.12, f32[512,1024]{1,0:T(8,128)S(1)} %fusion.2, bf16[512,3584]{1,0:T(8,128)(2,1)} %bitcast.65, bf16[1,3584,1024]{2,1,0:T(8,128)(2,1)} %param.10), kind=kOutput, calls=%fused_computation.6 | convolution fusion | flops 7521173504 | bytes 24117248 | tf_op jit(solution)/shard_map/dot_general | solution.py:21
  123.1 4.4 %copy.29 = bf16[2,32,8,3584]{3,2,0,1:T(8,128)(2,1)} copy(bf16[2,32,8,3584]{3,2,1,0:T(8,128)(2,1)} %bitcast.66) | data formatting | bytes 7340032 | tf_op jit(solution)/shard_map/reshape | solution.py:106
  127.5 4.0 %all-to-all-start.1 = ((bf16[2,32,8,3584]{3,2,0,1:T(8,128)(2,1)}), bf16[2,32,8,3584]{3,2,0,1:T(8,128)(2,1)}, u32[]{:S(2)}, u32[]{:S(2)}) async-start(bf16[2,32,8,3584]{3,2,0,1:T(8,128)(2,1)} %copy.29), calls=%async_computation.1 | async-start | bytes 7340032 | tf_op jit(solution)/shard_map/all_to_all | solution.py:105
  131.6 2.4 slice_select_fusion
  134.0 1.6 collective-permute-start.3
  135.6 77.2 %collective-permute-done.3 = f32[2,64,3584]{2,1,0:T(8,128)S(1)} collective-permute-done((f32[2,64,3584]{2,1,0:T(8,128)S(1)}, f32[2,64,3584]{2,1,0:T(8,128)S(1)}, u32[]{:S(2)}, u32[]{:S(2)}) %collective-permute-start.3) | collective-permute-done | bytes 1835040 | tf_op jit(solution)/shard_map/ppermute | solution.py:14
  213.1 1.5 collective-permute-start.4
  215.0 0.3 fusion.27
  215.3 20.2 %collective-permute-done.4 = f32[2,32,3584]{2,1,0:T(8,128)} collective-permute-done((f32[2,32,3584]{2,1,0:T(8,128)S(1)}, f32[2,32,3584]{2,1,0:T(8,128)}, u32[]{:S(2)}, u32[]{:S(2)}) %collective-permute-start.4) | collective-permute-done | bytes 917536 | tf_op jit(solution)/shard_map/ppermute | solution.py:14
  235.5 1.3 select_add_fusion.1
  236.9 0.3 fusion.28
  237.2 2.3 convolution_bitcast_fusion
  239.5 2.3 convolution_bitcast_fusion.1
  241.9 0.8 fusion.26
  (33 shorter events, 2.5 us)
Async XLA Ops:
  0.0 3.5 %copy-start.2 = (bf16[2,16,3584]{2,1,0:T(8,128)(2,1)S(1)}, bf16[2,16,3584]{2,1,0:T(8,128)(2,1)}, u32[]{:S(2)}) copy-start(bf16[2,16,3584]{2,1,0:T(8,128)(2,1)} %param.7) | copy-start | bytes 688132
  6.4 90.3 %all-to-all-start = ((bf16[2,32,8,3584]{3,2,0,1:T(8,128)(2,1)}), bf16[2,32,8,3584]{3,2,0,1:T(8,128)(2,1)}, u32[]{:S(2)}, u32[]{:S(2)}) async-start(bf16[2,32,8,3584]{3,2,0,1:T(8,128)(2,1)} %pad_maximum_fusion), calls=%async_computation | async-start | bytes 7340032 | tf_op jit(solution)/shard_map/all_to_all | solution.py:104
  13.9 1.6 collective-permute-start
  15.5 42.6 %collective-permute-start.1 = (bf16[2,32,3584]{2,1,0:T(8,128)(2,1)S(1)}, bf16[2,32,3584]{2,1,0:T(8,128)(2,1)S(1)}, u32[]{:S(2)}, u32[]{:S(2)}) collective-permute-start(bf16[2,32,3584]{2,1,0:T(8,128)(2,1)S(1)} %maximum_select_fusion.2), channel_id=1, source_target_pairs={{0,2},{2,0},{1,3},{3,1},{4,6},{6,4},{5,7},{7,5},{8,10},{10,8},{9,1... | collective-permute-start | bytes 1376264 | tf_op jit(solution)/shard_map/ppermute | solution.py:14
  58.3 30.5 %collective-permute-start.2 = (bf16[2,64,3584]{2,1,0:T(8,128)(2,1)S(1)}, bf16[2,64,3584]{2,1,0:T(8,128)(2,1)S(1)}, u32[]{:S(2)}, u32[]{:S(2)}) collective-permute-start(bf16[2,64,3584]{2,1,0:T(8,128)(2,1)S(1)} %maximum_select_fusion.1), channel_id=1, source_target_pairs={{0,4},{4,0},{1,5},{5,1},{2,6},{6,2},{3,7},{7,3},{8,12},{12,8},{9,1... | collective-permute-start | bytes 2752520 | tf_op jit(solution)/shard_map/ppermute | solution.py:14
  60.6 28.6 %copy-start.3 = (bf16[3,3584,128]{2,1,0:T(8,128)(2,1)S(1)}, bf16[3,3584,128]{2,1,0:T(8,128)(2,1)}, u32[]{:S(2)}) copy-start(bf16[3,3584,128]{2,1,0:T(8,128)(2,1)} %param.13) | copy-start | bytes 8257540
  99.0 1.8 copy-start.1
  127.5 109.7 %all-to-all-start.1 = ((bf16[2,32,8,3584]{3,2,0,1:T(8,128)(2,1)}), bf16[2,32,8,3584]{3,2,0,1:T(8,128)(2,1)}, u32[]{:S(2)}, u32[]{:S(2)}) async-start(bf16[2,32,8,3584]{3,2,0,1:T(8,128)(2,1)} %copy.29), calls=%async_computation.1 | async-start | bytes 7340032 | tf_op jit(solution)/shard_map/all_to_all | solution.py:105
  131.5 81.2 %copy-start = (f32[2,128,3584]{2,1,0:T(8,128)S(1)}, f32[2,128,3584]{2,1,0:T(8,128)}, u32[]{:S(2)}) copy-start(f32[2,128,3584]{2,1,0:T(8,128)} %fusion.15) | copy-start | bytes 11010052
  134.0 78.8 %collective-permute-start.3 = (f32[2,64,3584]{2,1,0:T(8,128)S(1)}, f32[2,64,3584]{2,1,0:T(8,128)S(1)}, u32[]{:S(2)}, u32[]{:S(2)}) collective-permute-start(f32[2,64,3584]{2,1,0:T(8,128)S(1)} %slice_select_fusion), channel_id=1, source_target_pairs={{0,4},{4,0},{1,5},{5,1},{2,6},{6,2},{3,7},{7,3},{8,12},{12,8},{9,1... | collective-permute-start | bytes 5505032 | tf_op jit(solution)/shard_map/ppermute | solution.py:14
  213.0 1.6 copy-start.4
  213.1 22.3 %collective-permute-start.4 = (f32[2,32,3584]{2,1,0:T(8,128)S(1)}, f32[2,32,3584]{2,1,0:T(8,128)}, u32[]{:S(2)}, u32[]{:S(2)}) collective-permute-start(f32[2,32,3584]{2,1,0:T(8,128)S(1)} %slice_select_fusion.1), channel_id=1, source_target_pairs={{0,2},{2,0},{1,3},{3,1},{4,6},{6,4},{5,7},{7,5},{8,10},{10,8},{9,1... | collective-permute-start | bytes 2752520 | tf_op jit(solution)/shard_map/ppermute | solution.py:14
  236.8 5.0 %collective-permute-start.5 = (f32[2,16,3584]{2,1,0:T(8,128)S(1)}, f32[2,16,3584]{2,1,0:T(8,128)S(1)}, u32[]{:S(2)}, u32[]{:S(2)}) collective-permute-start(f32[2,16,3584]{2,1,0:T(8,128)S(1)} %slice_select_fusion.2), channel_id=1, source_target_pairs={{0,1},{1,0},{2,3},{3,2},{4,5},{5,4},{6,7},{7,6},{8,9},{9,8},{10,11... | collective-permute-start | bytes 1376264 | tf_op jit(solution)/shard_map/ppermute | solution.py:14
where the time goes:
time: 243 us
  waiting for transfers between devices  172 us (71%)
  matrix products  34.2 us (14%)
  starting transfers between devices  19 us (8%)
  local copies, waits for them, and re-layouts  9.89 us (4%)
  other arithmetic  7.75 us (3%)
    ppermute x6, waiting for transfers between devices, partner_2(): return lax.ppermute(block, axis, route)  168 us
    dot_general x1, matrix products, expert_rows(): jnp.dot(hidden, down_mat, preferred_element_type=jnp.float32)  16.1 us
    ppermute x6, starting transfers between devices, partner_2(): return lax.ppermute(block, axis, route)  7.54 us
    all_to_all x1, starting transfers between devices, shards(): lax.all_to_all(outgoing, 'ep', split_axis=1, concat_axis=1, tiled=True)  7.41 us
    dot_general x1, matrix products, expert_rows(): up_val = jnp.dot(token_rows, up_mat, preferred_element_type=jnp.float32)  6.2 us
  transfers between devices with their start and end apart: 8, of which 6 were waited for; matrix products, arithmetic and copies ran while one was open for 6% of the time, Pallas kernels for 0%

commit v1 on v0

v1 whole, which is shorter than its diff:
```python
import functools

import jax
import jax.numpy as jnp
from jax import lax
from jax.experimental import pallas as pl
from jax.experimental.pallas import tpu as pltpu
from jax.sharding import PartitionSpec as P

AXIS = "ep"
GROUP = 8


def swap(block, mask_even, mask_odd):
    count = lax.axis_size(AXIS)
    route = [(i, i ^ (mask_odd if i & 1 else mask_even)) for i in range(count)]
    return lax.ppermute(block, AXIS, route)


def first_hop(block):
    return swap(block, 2, 4)


def second_hop(block):
    return swap(block, 4, 2)


def across(block, k):
    return swap(block, GROUP * k, GROUP * k)


def other_core(block):
    return swap(block, 1, 1)


def routing_columns(expert_ids, combine_weights, experts):
    step_count, row_count, _ = expert_ids.shape
    named = expert_ids[..., None] == jnp.arange(experts, dtype=jnp.int32)
    present = jnp.any(named, axis=2)
    weight = jnp.sum(jnp.where(named, combine_weights[..., None], 0.0), axis=2)
    earlier = (jnp.arange(row_count)[:, None] > jnp.arange(row_count)[None, :])[None, :, :, None]
    before = jnp.sum(jnp.where(earlier & present[:, None], 1.0, 0.0), axis=2)
    slot = jnp.where(present, before, -1.0)
    high = lax.reduce_precision(weight, 8, 7)
    low = weight - high
    columns = jnp.concatenate([slot, high, low], axis=2).astype(jnp.bfloat16)
    pad = -columns.shape[2] % 128
    return jnp.pad(columns, ((0, 0), (0, 0), (0, pad)))


def ffn_kernel(parts, me_ref, x_ref, gate_ref, up_ref, down_ref, out_ref, hidden):
    first_parts, width, experts = parts
    step = pl.program_id(0)
    tile = gate_ref.shape[1]

    @pl.when(step < first_parts)
    def _():
        rows = x_ref[:, :width]
        gate_val = jnp.dot(rows, gate_ref[...], preferred_element_type=jnp.float32)
        up_val = jnp.dot(rows, up_ref[...], preferred_element_type=jnp.float32)
        value = gate_val / (1.0 + jnp.exp(-gate_val)) * up_val
        hidden[:, pl.ds(pl.multiple_of(step * tile, tile), tile)] = value.astype(jnp.bfloat16)

    @pl.when(step >= first_parts)
    def _():
        columns = x_ref[:, width:].astype(jnp.float32)
        lane = lax.broadcasted_iota(jnp.int32, columns.shape, 1)
        mine = (lane == me_ref[0] + experts) | (lane == me_ref[0] + 2 * experts)
        weight = jnp.sum(jnp.where(mine, columns, 0.0), axis=1, keepdims=True)
        value = jnp.dot(hidden[...], down_ref[...], preferred_element_type=jnp.float32)
        out_ref[...] = (value * weight).astype(jnp.bfloat16)


def ffn(x, me, w_gate, w_up, w_down, experts):
    rows, full = x.shape
    _, width, units = w_gate.shape
    tile_j, tile_n = 256, 512
    first_parts, second_parts = units // tile_j, width // tile_n
    grid_spec = pltpu.PrefetchScalarGridSpec(
        num_scalar_prefetch=1,
        grid=(first_parts + second_parts,),
        in_specs=[
            pl.BlockSpec((rows, full), lambda i, m: (0, 0)),
            pl.BlockSpec((None, width, tile_j), lambda i, m: (0, 0, jnp.minimum(i, first_parts - 1))),
            pl.BlockSpec((None, width, tile_j), lambda i, m: (0, 0, jnp.minimum(i, first_parts - 1))),
            pl.BlockSpec((None, units, tile_n), lambda i, m: (0, 0, jnp.maximum(i - first_parts, 0))),
        ],
        out_specs=pl.BlockSpec((rows, tile_n), lambda i, m: (0, jnp.maximum(i - first_parts, 0))),
        scratch_shapes=[pltpu.VMEM((rows, units), jnp.bfloat16)],
    )
    return pl.pallas_call(
        functools.partial(ffn_kernel, (first_parts, width, experts)),
        grid_spec=grid_spec,
        out_shape=jax.ShapeDtypeStruct((rows, width), jnp.bfloat16),
        compiler_params=pltpu.CompilerParams(vmem_limit_bytes=32 * 1024 * 1024),
        cost_estimate=pl.CostEstimate(
            flops=6 * rows * width * units, bytes_accessed=6 * width * units, transcendentals=rows * units
        ),
        name="expert_ffn",
    )(me, x, w_gate, w_up, w_down)


def placing(columns, expert, row_count, capacity):
    rows = columns.shape[0]
    slots = rows // row_count * capacity
    slot = lax.dynamic_slice_in_dim(columns, expert, 1, axis=1).astype(jnp.int32)
    base = (jnp.arange(rows, dtype=jnp.int32) // row_count * capacity)[:, None]
    target = jnp.where(slot >= 0, base + slot, -1)
    return (target == jnp.arange(slots, dtype=jnp.int32)[None, :]).astype(jnp.bfloat16)


def shards(tokens, expert_ids, combine_weights, w_gate, w_up, w_down, shared_weights):
    step_count, row_count, width = tokens.shape
    top_count = expert_ids.shape[2]
    devices = lax.axis_size(AXIS)
    experts = w_gate.shape[0] * devices
    capacity = max(2, row_count * top_count * 2 // experts)
    planes = devices // GROUP
    me = lax.axis_index(AXIS)
    block = step_count * row_count

    columns = routing_columns(expert_ids, combine_weights, experts)
    own = jnp.concatenate([tokens, columns], axis=2).reshape(block, -1)

    shared_other = other_core(shared_weights)

    def spread(rows):
        rows = jnp.concatenate([rows, first_hop(rows)], axis=0)
        return jnp.concatenate([rows, second_hop(rows)], axis=0)

    gathered = [None] * planes
    far = [own] + [across(own, k) for k in range(1, planes)]
    gathered0 = spread(own)
    gathered1 = spread(far[1])
    rest = jnp.stack(far[2:], axis=0).reshape(-1, own.shape[1])
    gathered_rest = spread(rest)

    def experts_of(rows):
        place = jnp.concatenate(
            [placing(rows[:, width:], me, row_count, capacity), placing(rows[:, width:], me ^ 1, row_count, capacity)],
            axis=1,
        )
        chosen = lax.dot_general(
            place, rows, (((0,), (0,)), ((), ())), preferred_element_type=jnp.float32
        ).astype(jnp.bfloat16)
        half = chosen.shape[0] // 2
        received = other_core(chosen[half:])
        result = ffn(
            jnp.concatenate([chosen[:half], received], axis=0), me[None], w_gate, w_up, w_down, experts
        )
        returned = other_core(result[half:])
        return jnp.dot(
            place, jnp.concatenate([result[:half], returned], axis=0), preferred_element_type=jnp.float32
        )

    def shared_expert(rows):
        hidden = []
        for part in (shared_weights, shared_other):
            gate_val = jnp.dot(rows, part[0], preferred_element_type=jnp.float32)
            up_val = jnp.dot(rows, part[1], preferred_element_type=jnp.float32)
            hidden.append((jax.nn.silu(gate_val) * up_val).astype(jnp.bfloat16))
        return sum(
            lax.dot_general(h, part[2], (((1,), (1,)), ((), ())), preferred_element_type=jnp.float32)
            for h, part in zip(hidden, (shared_weights, shared_other))
        )

    def collect(partial):
        half = partial.shape[0] // 2
        partial = partial[:half] + second_hop(partial[half:].astype(jnp.bfloat16)).astype(jnp.float32)
        half = half // 2
        return partial[:half] + first_hop(partial[half:].astype(jnp.bfloat16)).astype(jnp.float32)

    first = experts_of(jnp.concatenate([gathered0, gathered1], axis=0))
    partial0 = first[: GROUP // 2 * block] + shared_expert(gathered0[:, :width])
    partial1 = first[GROUP // 2 * block :]
    partial_rest = experts_of(gathered_rest)

    total1 = across(collect(partial1).astype(jnp.bfloat16), 1)
    summed_rest = collect(partial_rest).astype(jnp.bfloat16)
    parts = [total1] + [
        across(summed_rest[(k - 2) * block : (k - 1) * block], k) for k in range(2, planes)
    ]
    total = collect(partial0)
    for part in parts:
        total = total + part.astype(jnp.float32)
    return total.astype(jnp.bfloat16).reshape(step_count, row_count, width)


def solution(mesh):
    placed = (
        P(None, AXIS, None),
        P(None, AXIS, None),
        P(None, AXIS, None),
        P(AXIS, None, None),
        P(AXIS, None, None),
        P(AXIS, None, None),
        P(None, None, AXIS),
    )
    return jax.shard_map(
        shards, mesh=mesh, in_specs=placed, out_specs=P(None, AXIS, None), check_vma=False
    )
```

time: 243 us -> 164 us (0.67)
  waiting for transfers between devices: 172 us -> 82.5 us
  Pallas kernels: 0 us -> 26.3 us
  matrix products: 34.2 us -> 15.4 us
  starting transfers between devices: 19 us -> 25.1 us
  other arithmetic: 7.75 us -> 5.27 us
    ppermute x6 -> x23, waiting for transfers between devices: 168 us -> 82.5 us  [swap(): return lax.ppermute(block, AXIS, route)]
    pallas_call x0 -> x2, Pallas kernels: none -> 26.3 us  [ffn(): pl.pallas_call(functools.partial(ffn_kernel, (first_parts, width, experts...]
    dot_general x15 -> x8, matrix products: 34.2 us -> 15.4 us  [the longest x2 6.97 us: shared_expert(): lax.dot_general(h, part[2], (((1,), (1,)), ((), ())), preferred_element_t...]
    ppermute x6 -> x23, starting transfers between devices: 7.54 us -> 25.1 us  [swap(): return lax.ppermute(block, AXIS, route)]
    all_to_all x2 -> x0, starting transfers between devices: 11.4 us -> none  [the longest x1 7.41 us: shards(): lax.all_to_all(outgoing, 'ep', split_axis=1, concat_axis=1, tiled=True)]
    reshape x1 -> x0, local copies, waits for them, and re-layouts: 4.37 us -> none  [shards(): expert_rows(received.reshape(-1, model_width), w_gate[0], w_up[0], w_down...]
    all_to_all x2 -> x0, waiting for transfers between devices: 3.83 us -> none  [the longest x1 3.83 us: shards(): lax.all_to_all(outgoing, 'ep', split_axis=1, concat_axis=1, tiled=True)]
    unnamed x10 -> x19, local copies, waits for them, and re-layouts: 1.85 us -> 4.81 us
  transfers between devices with their start and end apart: 8 -> 23, of which waited for: 6 -> 12; matrix products, arithmetic and copies ran while one was open for 6% -> 14% of each run, Pallas kernels for 0% -> 16%
where the time goes in v1:
time: 164 us; the launch traced here: 163 us
  waiting for transfers between devices  82.5 us (50%)
  Pallas kernels  26.3 us (16%)
  starting transfers between devices  25.1 us (15%)
  matrix products  15.4 us (9%)
  local copies, waits for them, and re-layouts  8.39 us (5%)
  other arithmetic  5.27 us (3%)
    ppermute x23, waiting for transfers between devices, swap(): return lax.ppermute(block, AXIS, route)  82.5 us
    pallas_call x2, Pallas kernels, ffn(): pl.pallas_call(functools.partial(ffn_kernel, (first_parts, width, experts...  26.3 us
    ppermute x23, starting transfers between devices, swap(): return lax.ppermute(block, AXIS, route)  25.1 us
    dot_general x2, matrix products, shared_expert(): lax.dot_general(h, part[2], (((1,), (1,)), ((), ())), preferred_element_t...  6.97 us
    unnamed x19, local copies, waits for them, and re-layouts  4.81 us
    dot_general x2, matrix products, experts_of(): jnp.dot(place, jnp.concatenate([result[:half], returned], axis=0), prefer...  3.66 us
    dot_general x2, matrix products, shared_expert(): up_val = jnp.dot(rows, part[1], preferred_element_type=jnp.float32)  3.3 us
  transfers between devices with their start and end apart: 23, of which 12 were waited for; matrix products, arithmetic and copies ran while one was open for 14% of the time, Pallas kernels for 16%

profile of v1, /device:TPU:0, one launch (start us, length us, event | category | flops | bytes accessed | tf_op | source)
XLA Modules:
  0.0 163.3 jit_solution(8282987112193966188)
XLA Ops:
  3.0 3.0 %collective-permute-start = (bf16[32,3712]{1,0:T(8,128)(2,1)S(1)}, bf16[32,3712]{1,0:T(8,128)(2,1)S(1)}, u32[]{:S(2)}, u32[]{:S(2)}) collective-permute-start(bf16[32,3712]{1,0:T(8,128)(2,1)S(1)} %bitcast.43), channel_id=1, source_target_pairs={{0,2},{1,5},{2,0},{3,7},{4,6},{5,1},{6,4},{7,3},{8,10},{9,13},{10,... | collective-permute-start | bytes 712712 | tf_op jit(solution)/shard_map/ppermute | solution.py:17
  6.1 1.6 collective-permute-start.2
  7.6 2.5 %collective-permute-start.14 = (bf16[32,3712]{1,0:T(8,128)(2,1)S(1)}, bf16[32,3712]{1,0:T(8,128)(2,1)S(1)}, u32[]{:S(2)}, u32[]{:S(2)}) collective-permute-start(bf16[32,3712]{1,0:T(8,128)(2,1)S(1)} %bitcast.45), channel_id=1, source_target_pairs={{0,24},{1,25},{2,26},{3,27},{4,28},{5,29},{6,30},{7,31},{8,16},{9,... | collective-permute-start | bytes 712712 | tf_op jit(solution)/shard_map/ppermute | solution.py:17
  10.3 2.0 %collective-permute-start.1 = (bf16[64,3712]{1,0:T(8,128)(2,1)S(1)}, bf16[64,3712]{1,0:T(8,128)(2,1)S(1)}, u32[]{:S(2)}, u32[]{:S(2)}) collective-permute-start(bf16[64,3712]{1,0:T(8,128)(2,1)S(1)} %pad_maximum_fusion.5), channel_id=1, source_target_pairs={{0,4},{1,3},{2,6},{3,1},{4,0},{5,7},{6,2},{7,5},{8,12},{9,11},{10,... | collective-permute-start | bytes 1425416 | tf_op jit(solution)/shard_map/ppermute | solution.py:17
  12.3 9.7 %collective-permute-done.14 = bf16[32,3712]{1,0:T(8,128)(2,1)S(1)} collective-permute-done((bf16[32,3712]{1,0:T(8,128)(2,1)S(1)}, bf16[32,3712]{1,0:T(8,128)(2,1)S(1)}, u32[]{:S(2)}, u32[]{:S(2)}) %collective-permute-start.14) | collective-permute-done | bytes 237600 | tf_op jit(solution)/shard_map/ppermute | solution.py:17
  22.0 8.8 %collective-permute-done.13 = bf16[32,3712]{1,0:T(8,128)(2,1)S(1)} collective-permute-done((bf16[32,3712]{1,0:T(8,128)(2,1)S(1)}, bf16[32,3712]{1,0:T(8,128)(2,1)S(1)}, u32[]{:S(2)}, u32[]{:S(2)}) %collective-permute-start.13) | collective-permute-done | bytes 237600 | tf_op jit(solution)/shard_map/ppermute | solution.py:17
  30.8 1.6 collective-permute-start.15
  32.9 9.1 %collective-permute-done.3 = bf16[32,3712]{1,0:T(8,128)(2,1)S(1)} collective-permute-done((bf16[32,3712]{1,0:T(8,128)(2,1)S(1)}, bf16[32,3712]{1,0:T(8,128)(2,1)S(1)}, u32[]{:S(2)}, u32[]{:S(2)}) %collective-permute-start.3) | collective-permute-done | bytes 237600 | tf_op jit(solution)/shard_map/ppermute | solution.py:17
  42.7 1.6 collective-permute-start.16
  44.4 1.7 %fusion.18 = f32[128,128]{1,0:T(8,128)S(1)} fusion(bf16[3,3584,128]{2,1,0:T(8,128)(2,1)} %param.13, bf16[64,3712]{1,0:T(8,128)(2,1)S(1)} %collective-permute-done.1, bf16[32,3712]{1,0:T(8,128)(2,1)S(1)} %collective-permute-done, bf16[32,3712]{1,0:T(8,128)(2,1)S(1)} %bitcast.49), kind=kOutput, calls=%fused_computation.38 | convolution fusion | flops 120193024 | bytes 1933312 | tf_op jit(solution)/shard_map/dot_general | solution.py:160
  46.2 4.6 %collective-permute-done.4 = bf16[64,3712]{1,0:T(8,128)(2,1)S(1)} collective-permute-done((bf16[64,3712]{1,0:T(8,128)(2,1)S(1)}, bf16[64,3712]{1,0:T(8,128)(2,1)S(1)}, u32[]{:S(2)}, u32[]{:S(2)}) %collective-permute-start.4) | collective-permute-done | bytes 475168 | tf_op jit(solution)/shard_map/ppermute | solution.py:17
  50.9 10.1 %collective-permute-done.16 = bf16[128,3712]{1,0:T(8,128)(2,1)S(1)} collective-permute-done((bf16[128,3712]{1,0:T(8,128)(2,1)S(1)}, bf16[128,3712]{1,0:T(8,128)(2,1)S(1)}, u32[]{:S(2)}, u32[]{:S(2)}) %collective-permute-start.16) | collective-permute-done | bytes 950304 | tf_op jit(solution)/shard_map/ppermute | solution.py:17
  66.6 13.2 %expert_ffn.2 = bf16[256,3584]{1,0:T(8,128)(2,1)S(1)} custom-call(s32[1]{0:T(128)} %bitcast.1.me_ref, bf16[256,3712]{1,0:T(8,128)(2,1)S(1)} %pad_maximum_fusion.x_ref, bf16[1,3584,1024]{2,1,0:T(8,128)(2,1)S(1)} %bitcast.36, bf16[1,3584,1024]{2,1,0:T(8,128)(2,1)S(1)} %bitcast.38, bf16[1,1024,3584]{2,1,0:T(8,128)(2,1)} %down_ref.3), custom_call_target="tpu_custom_call" | custom-call | flops 5637144576 | bytes 22020096 | tf_op jit(solution)/shard_map/expert_ffn/pallas_call | solution.py:91
  81.0 13.2 %expert_ffn.3 = bf16[256,3584]{1,0:T(8,128)(2,1)S(1)} custom-call(s32[1]{0:T(128)} %bitcast.1.me_ref, bf16[256,3712]{1,0:T(8,128)(2,1)S(1)} %pad_maximum_fusion.1.x_ref, bf16[1,3584,1024]{2,1,0:T(8,128)(2,1)S(1)} %bitcast.36, bf16[1,3584,1024]{2,1,0:T(8,128)(2,1)S(1)} %bitcast.38, bf16[1,1024,3584]{2,1,0:T(8,128)(2,1)} %down_ref.3), custom_call_target="tpu_custom_call" | custom-call | flops 5637144576 | bytes 22020096 | tf_op jit(solution)/shard_map/expert_ffn/pallas_call | solution.py:91
  94.2 1.1 fusion.66
  95.7 3.5 %fusion.16 = f32[128,3584]{1,0:T(8,128)} fusion(bf16[3,3584,128]{2,1,0:T(8,128)(2,1)} %param.13, f32[128,128]{1,0:T(8,128)S(1)} %fusion.18, bf16[64,3712]{1,0:T(8,128)(2,1)S(1)} %collective-permute-done.1, bf16[32,3712]{1,0:T(8,128)(2,1)S(1)} %collective-permute-done, bf16[32,3712]{1,0:T(8,128)(2,1)S(1)} %bitcast.50), kind=kOutput, calls=%fused_computation.36 | convolution fusion | flops 237731840 | bytes 4685824 | tf_op jit(solution)/shard_map/dot_general | solution.py:163
  99.2 1.6 fusion.14
  100.8 1.8 %fusion.5 = f32[256,3584]{1,0:T(8,128)S(1)} fusion(bf16[128,3584]{1,0:T(8,128)(2,1)} %collective-permute-done.6, bf16[128,3584]{1,0:T(8,128)(2,1)S(1)} %get-tuple-element.15, pred[256,128]{1,0:T(32,128)(4,1)S(1)} %iota_compare_fusion.2, pred[256,128]{1,0:T(32,128)(4,1)S(1)} %iota_compare_fusion.3), kind=kOutput, calls=%fused_computation.13 | convolution fusion | flops 473497600 | bytes 5570560 | tf_op jit(solution)/shard_map/dot_general | solution.py:152
  102.6 1.8 %copy-done = f32[256,3584]{1,0:T(8,128)} copy-done((f32[256,3584]{1,0:T(8,128)}, f32[256,3584]{1,0:T(8,128)S(1)}, u32[]{:S(2)}) %copy-start) | copy-done | bytes 3670040
  105.7 3.5 %slice_add_fusion.1 = f32[128,3584]{1,0:T(8,128)S(1)} fusion(f32[256,3584]{1,0:T(8,128)} %copy-done, f32[128,3584]{1,0:T(8,128)} %fusion.16, bf16[3,3584,128]{2,1,0:T(8,128)(2,1)} %collective-permute-done.7, f32[128,128]{1,0:T(8,128)S(1)} %fusion.14, bf16[64,3712]{1,0:T(8,128)(2,1)} %copy-done.1, bf16[32,3712]{1,0:T(8,128)(2,1)S(1)} %collective-permute-done, ...), kind=kOutput, calls=%fused_computation.12 | convolution fusion | flops 238649344 | bytes 8355840 | tf_op jit(solution)/shard_map/dot_general | solution.py:163
  109.3 1.6 collective-permute-start.8
  110.9 1.8 %fusion.9 = f32[256,3584]{1,0:T(8,128)S(1)} fusion(bf16[128,3584]{1,0:T(8,128)(2,1)} %collective-permute-done.18, bf16[128,3584]{1,0:T(8,128)(2,1)S(1)} %get-tuple-element.13, pred[256,128]{1,0:T(32,128)(4,1)S(1)} %iota_compare_fusion, pred[256,128]{1,0:T(32,128)(4,1)S(1)} %iota_compare_fusion.1), kind=kOutput, calls=%fused_computation.17 | convolution fusion | flops 473497600 | bytes 5570560 | tf_op jit(solution)/shard_map/dot_general | solution.py:152
  114.0 1.4 slice_add_fusion.3
  115.4 1.6 collective-permute-start.11
  117.0 2.9 %collective-permute-done.8 = bf16[64,3584]{1,0:T(8,128)(2,1)S(1)} collective-permute-done((bf16[64,3584]{1,0:T(8,128)(2,1)S(1)}, bf16[64,3584]{1,0:T(8,128)(2,1)S(1)}, u32[]{:S(2)}, u32[]{:S(2)}) %collective-permute-start.8) | collective-permute-done | bytes 458784 | tf_op jit(solution)/shard_map/ppermute | solution.py:17
  120.1 1.9 %collective-permute-start.9 = (bf16[32,3584]{1,0:T(8,128)(2,1)S(1)}, bf16[32,3584]{1,0:T(8,128)(2,1)S(1)}, u32[]{:S(2)}, u32[]{:S(2)}) collective-permute-start(bf16[32,3584]{1,0:T(8,128)(2,1)S(1)} %slice.224), channel_id=1, source_target_pairs={{0,2},{1,5},{2,0},{3,7},{4,6},{5,1},{6,4},{7,3},{8,10},{9,13},{10,... | collective-permute-start | bytes 688136 | tf_op jit(solution)/shard_map/ppermute | solution.py:17
  122.0 11.6 %collective-permute-done.19 = bf16[128,3584]{1,0:T(8,128)(2,1)S(1)} collective-permute-done((bf16[128,3584]{1,0:T(8,128)(2,1)S(1)}, bf16[128,3584]{1,0:T(8,128)(2,1)S(1)}, u32[]{:S(2)}, u32[]{:S(2)}) %collective-permute-start.19) | collective-permute-done | bytes 917536 | tf_op jit(solution)/shard_map/ppermute | solution.py:17
  133.8 1.6 collective-permute-start.20
  135.5 6.9 %collective-permute-done.20 = bf16[64,3584]{1,0:T(8,128)(2,1)S(1)} collective-permute-done((bf16[64,3584]{1,0:T(8,128)(2,1)S(1)}, bf16[64,3584]{1,0:T(8,128)(2,1)S(1)}, u32[]{:S(2)}, u32[]{:S(2)}) %collective-permute-start.20) | collective-permute-done | bytes 458784 | tf_op jit(solution)/shard_map/ppermute | solution.py:17
  142.5 2.7 %collective-permute-start.22 = (bf16[32,3584]{1,0:T(8,128)(2,1)S(1)}, bf16[32,3584]{1,0:T(8,128)(2,1)S(1)}, u32[]{:S(2)}, u32[]{:S(2)}) collective-permute-start(bf16[32,3584]{1,0:T(8,128)(2,1)S(1)} %get-tuple-element.18), channel_id=1, source_target_pairs={{0,24},{1,25},{2,26},{3,27},{4,28},{5,29},{6,30},{7,31},{8,16},{9,... | collective-permute-start | bytes 688136 | tf_op jit(solution)/shard_map/ppermute | solution.py:17
  145.2 7.6 %collective-permute-done.22 = bf16[32,3584]{1,0:T(8,128)(2,1)S(1)} collective-permute-done((bf16[32,3584]{1,0:T(8,128)(2,1)S(1)}, bf16[32,3584]{1,0:T(8,128)(2,1)S(1)}, u32[]{:S(2)}, u32[]{:S(2)}) %collective-permute-start.22) | collective-permute-done | bytes 229408 | tf_op jit(solution)/shard_map/ppermute | solution.py:17
  152.8 9.7 %collective-permute-done.21 = bf16[32,3584]{1,0:T(8,128)(2,1)S(1)} collective-permute-done((bf16[32,3584]{1,0:T(8,128)(2,1)S(1)}, bf16[32,3584]{1,0:T(8,128)(2,1)S(1)}, u32[]{:S(2)}, u32[]{:S(2)}) %collective-permute-start.21) | collective-permute-done | bytes 229408 | tf_op jit(solution)/shard_map/ppermute | solution.py:17
  (84 shorter events, 15.9 us)
Async XLA Ops:
  3.0 7.2 %collective-permute-start = (bf16[32,3712]{1,0:T(8,128)(2,1)S(1)}, bf16[32,3712]{1,0:T(8,128)(2,1)S(1)}, u32[]{:S(2)}, u32[]{:S(2)}) collective-permute-start(bf16[32,3712]{1,0:T(8,128)(2,1)S(1)} %bitcast.43), channel_id=1, source_target_pairs={{0,2},{1,5},{2,0},{3,7},{4,6},{5,1},{6,4},{7,3},{8,10},{9,13},{10,... | collective-permute-start | bytes 712712 | tf_op jit(solution)/shard_map/ppermute | solution.py:17
  6.1 26.3 %collective-permute-start.2 = (bf16[32,3712]{1,0:T(8,128)(2,1)S(1)}, bf16[32,3712]{1,0:T(8,128)(2,1)S(1)}, u32[]{:S(2)}, u32[]{:S(2)}) collective-permute-start(bf16[32,3712]{1,0:T(8,128)(2,1)S(1)} %bitcast.44), channel_id=1, source_target_pairs={{0,8},{1,9},{2,10},{3,11},{4,12},{5,13},{6,14},{7,15},{8,0},{9,1},... | collective-permute-start | bytes 712712 | tf_op jit(solution)/shard_map/ppermute | solution.py:17
  7.6 14.3 %collective-permute-start.14 = (bf16[32,3712]{1,0:T(8,128)(2,1)S(1)}, bf16[32,3712]{1,0:T(8,128)(2,1)S(1)}, u32[]{:S(2)}, u32[]{:S(2)}) collective-permute-start(bf16[32,3712]{1,0:T(8,128)(2,1)S(1)} %bitcast.45), channel_id=1, source_target_pairs={{0,24},{1,25},{2,26},{3,27},{4,28},{5,29},{6,30},{7,31},{8,16},{9,... | collective-permute-start | bytes 712712 | tf_op jit(solution)/shard_map/ppermute | solution.py:17
  10.1 20.6 %collective-permute-start.13 = (bf16[32,3712]{1,0:T(8,128)(2,1)S(1)}, bf16[32,3712]{1,0:T(8,128)(2,1)S(1)}, u32[]{:S(2)}, u32[]{:S(2)}) collective-permute-start(bf16[32,3712]{1,0:T(8,128)(2,1)S(1)} %bitcast.46), channel_id=1, source_target_pairs={{0,16},{1,17},{2,18},{3,19},{4,20},{5,21},{6,22},{7,23},{8,24},{9,... | collective-permute-start | bytes 712712 | tf_op jit(solution)/shard_map/ppermute | solution.py:17
  10.2 89.0 %collective-permute-start.7 = (bf16[3,3584,128]{2,1,0:T(8,128)(2,1)}, bf16[3,3584,128]{2,1,0:T(8,128)(2,1)}, u32[]{:S(2)}, u32[]{:S(2)}) collective-permute-start(bf16[3,3584,128]{2,1,0:T(8,128)(2,1)} %param.13), channel_id=1, source_target_pairs={{0,1},{1,0},{2,3},{3,2},{4,5},{5,4},{6,7},{7,6},{8,9},{9,8},{10,11... | collective-permute-start | bytes 8257544 | tf_op jit(solution)/shard_map/ppermute | solution.py:17
  10.3 34.0 %collective-permute-start.1 = (bf16[64,3712]{1,0:T(8,128)(2,1)S(1)}, bf16[64,3712]{1,0:T(8,128)(2,1)S(1)}, u32[]{:S(2)}, u32[]{:S(2)}) collective-permute-start(bf16[64,3712]{1,0:T(8,128)(2,1)S(1)} %pad_maximum_fusion.5), channel_id=1, source_target_pairs={{0,4},{1,3},{2,6},{3,1},{4,0},{5,7},{6,2},{7,5},{8,12},{9,11},{10,... | collective-permute-start | bytes 1425416 | tf_op jit(solution)/shard_map/ppermute | solution.py:17
  30.8 11.9 %collective-permute-start.15 = (bf16[64,3712]{1,0:T(8,128)(2,1)S(1)}, bf16[64,3712]{1,0:T(8,128)(2,1)S(1)}, u32[]{:S(2)}, u32[]{:S(2)}) collective-permute-start(bf16[64,3712]{1,0:T(8,128)(2,1)S(1)} %bitcast.39), channel_id=1, source_target_pairs={{0,2},{1,5},{2,0},{3,7},{4,6},{5,1},{6,4},{7,3},{8,10},{9,13},{10,... | collective-permute-start | bytes 1425416 | tf_op jit(solution)/shard_map/ppermute | solution.py:17
  32.4 9.7 %collective-permute-start.3 = (bf16[32,3712]{1,0:T(8,128)(2,1)S(1)}, bf16[32,3712]{1,0:T(8,128)(2,1)S(1)}, u32[]{:S(2)}, u32[]{:S(2)}) collective-permute-start(bf16[32,3712]{1,0:T(8,128)(2,1)S(1)} %collective-permute-done.2), channel_id=1, source_target_pairs={{0,2},{1,5},{2,0},{3,7},{4,6},{5,1},{6,4},{7,3},{8,10},{9,13},{10,... | collective-permute-start | bytes 712712 | tf_op jit(solution)/shard_map/ppermute | solution.py:17
  42.1 8.7 %collective-permute-start.4 = (bf16[64,3712]{1,0:T(8,128)(2,1)S(1)}, bf16[64,3712]{1,0:T(8,128)(2,1)S(1)}, u32[]{:S(2)}, u32[]{:S(2)}) collective-permute-start(bf16[64,3712]{1,0:T(8,128)(2,1)S(1)} %pad_maximum_fusion.6), channel_id=1, source_target_pairs={{0,4},{1,3},{2,6},{3,1},{4,0},{5,7},{6,2},{7,5},{8,12},{9,11},{10,... | collective-permute-start | bytes 1425416 | tf_op jit(solution)/shard_map/ppermute | solution.py:17
  42.7 18.3 %collective-permute-start.16 = (bf16[128,3712]{1,0:T(8,128)(2,1)S(1)}, bf16[128,3712]{1,0:T(8,128)(2,1)S(1)}, u32[]{:S(2)}, u32[]{:S(2)}) collective-permute-start(bf16[128,3712]{1,0:T(8,128)(2,1)S(1)} %pad_maximum_fusion.2), channel_id=1, source_target_pairs={{0,4},{1,3},{2,6},{3,1},{4,0},{5,7},{6,2},{7,5},{8,12},{9,11},{10,... | collective-permute-start | bytes 2850824 | tf_op jit(solution)/shard_map/ppermute | solution.py:17
  44.3 54.9 %copy-start.1 = (bf16[64,3712]{1,0:T(8,128)(2,1)}, bf16[64,3712]{1,0:T(8,128)(2,1)S(1)}, u32[]{:S(2)}) copy-start(bf16[64,3712]{1,0:T(8,128)(2,1)S(1)} %collective-permute-done.1) | copy-start | bytes 1425412
  44.4 20.8 %slice-start.2 = ((s8[7340032]{0:T(1024)(128)(4,1)}), s8[4194304]{0:T(1024)(128)(4,1)S(1)}, s32[]{:S(2)}) async-start(s8[7340032]{0:T(1024)(128)(4,1)} %bitcast.37), calls=%async_computation.2 | async-start | bytes 8388608
  62.3 2.9 %slice-start.3 = ((s8[7340032]{0:T(1024)(128)(4,1)}), s8[3145728]{0:T(1024)(128)(4,1)S(1)}, s32[]{:S(2)}) async-start(s8[7340032]{0:T(1024)(128)(4,1)} %bitcast.37), calls=%async_computation.3 | async-start | bytes 6291456
  62.5 2.6 %collective-permute-start.5 = (bf16[128,3712]{1,0:T(8,128)(2,1)S(1)}, bf16[128,3712]{1,0:T(8,128)(2,1)S(1)}, u32[]{:S(2)}, u32[]{:S(2)}) collective-permute-start(bf16[128,3712]{1,0:T(8,128)(2,1)S(1)} %get-tuple-element.12), channel_id=1, source_target_pairs={{0,1},{1,0},{2,3},{3,2},{4,5},{5,4},{6,7},{7,6},{8,9},{9,8},{10,11... | collective-permute-start | bytes 2850824 | tf_op jit(solution)/shard_map/ppermute | solution.py:17
  62.8 2.8 %slice-start = ((s8[7340032]{0:T(1024)(128)(4,1)}), s8[4194304]{0:T(1024)(128)(4,1)S(1)}, s32[]{:S(2)}) async-start(s8[7340032]{0:T(1024)(128)(4,1)} %bitcast.35), calls=%async_computation | async-start | bytes 8388608
  63.5 3.0 %slice-start.1 = ((s8[7340032]{0:T(1024)(128)(4,1)}), s8[3145728]{0:T(1024)(128)(4,1)S(1)}, s32[]{:S(2)}) async-start(s8[7340032]{0:T(1024)(128)(4,1)} %bitcast.35), calls=%async_computation.1 | async-start | bytes 6291456
  63.7 17.2 %collective-permute-start.17 = (bf16[128,3712]{1,0:T(8,128)(2,1)S(1)}, bf16[128,3712]{1,0:T(8,128)(2,1)S(1)}, u32[]{:S(2)}, u32[]{:S(2)}) collective-permute-start(bf16[128,3712]{1,0:T(8,128)(2,1)S(1)} %get-tuple-element.10), channel_id=1, source_target_pairs={{0,1},{1,0},{2,3},{3,2},{4,5},{5,4},{6,7},{7,6},{8,9},{9,8},{10,11... | collective-permute-start | bytes 2850824 | tf_op jit(solution)/shard_map/ppermute | solution.py:17
  80.8 20.0 %collective-permute-start.6 = (bf16[128,3584]{1,0:T(8,128)(2,1)}, bf16[128,3584]{1,0:T(8,128)(2,1)}, u32[]{:S(2)}, u32[]{:S(2)}) collective-permute-start(bf16[128,3584]{1,0:T(8,128)(2,1)} %get-tuple-element.16), channel_id=1, source_target_pairs={{0,1},{1,0},{2,3},{3,2},{4,5},{5,4},{6,7},{7,6},{8,9},{9,8},{10,11... | collective-permute-start | bytes 2752520 | tf_op jit(solution)/shard_map/ppermute | solution.py:17
  95.3 15.6 %collective-permute-start.18 = (bf16[128,3584]{1,0:T(8,128)(2,1)}, bf16[128,3584]{1,0:T(8,128)(2,1)}, u32[]{:S(2)}, u32[]{:S(2)}) collective-permute-start(bf16[128,3584]{1,0:T(8,128)(2,1)} %get-tuple-element.14), channel_id=1, source_target_pairs={{0,1},{1,0},{2,3},{3,2},{4,5},{5,4},{6,7},{7,6},{8,9},{9,8},{10,11... | collective-permute-start | bytes 2752520 | tf_op jit(solution)/shard_map/ppermute | solution.py:17
  102.6 1.8 %copy-start = (f32[256,3584]{1,0:T(8,128)}, f32[256,3584]{1,0:T(8,128)S(1)}, u32[]{:S(2)}) copy-start(f32[256,3584]{1,0:T(8,128)S(1)} %fusion.5) | copy-start | bytes 11010052
  105.2 8.8 %collective-permute-start.10 = (bf16[64,3584]{1,0:T(8,128)(2,1)}, bf16[64,3584]{1,0:T(8,128)(2,1)}, u32[]{:S(2)}, u32[]{:S(2)}) collective-permute-start(bf16[64,3584]{1,0:T(8,128)(2,1)} %slice.221), channel_id=1, source_target_pairs={{0,4},{1,3},{2,6},{3,1},{4,0},{5,7},{6,2},{7,5},{8,12},{9,11},{10,... | collective-permute-start | bytes 1376264 | tf_op jit(solution)/shard_map/ppermute | solution.py:17
  109.3 10.6 %collective-permute-start.8 = (bf16[64,3584]{1,0:T(8,128)(2,1)S(1)}, bf16[64,3584]{1,0:T(8,128)(2,1)S(1)}, u32[]{:S(2)}, u32[]{:S(2)}) collective-permute-start(bf16[64,3584]{1,0:T(8,128)(2,1)S(1)} %slice.222), channel_id=1, source_target_pairs={{0,4},{1,3},{2,6},{3,1},{4,0},{5,7},{6,2},{7,5},{8,12},{9,11},{10,... | collective-permute-start | bytes 1376264 | tf_op jit(solution)/shard_map/ppermute | solution.py:17
  112.8 20.7 %collective-permute-start.19 = (bf16[128,3584]{1,0:T(8,128)(2,1)S(1)}, bf16[128,3584]{1,0:T(8,128)(2,1)S(1)}, u32[]{:S(2)}, u32[]{:S(2)}) collective-permute-start(bf16[128,3584]{1,0:T(8,128)(2,1)S(1)} %slice.219), channel_id=1, source_target_pairs={{0,4},{1,3},{2,6},{3,1},{4,0},{5,7},{6,2},{7,5},{8,12},{9,11},{10,... | collective-permute-start | bytes 2752520 | tf_op jit(solution)/shard_map/ppermute | solution.py:17
  115.4 19.9 %collective-permute-start.11 = (bf16[32,3584]{1,0:T(8,128)(2,1)S(1)}, bf16[32,3584]{1,0:T(8,128)(2,1)S(1)}, u32[]{:S(2)}, u32[]{:S(2)}) collective-permute-start(bf16[32,3584]{1,0:T(8,128)(2,1)S(1)} %slice.223), channel_id=1, source_target_pairs={{0,2},{1,5},{2,0},{3,7},{4,6},{5,1},{6,4},{7,3},{8,10},{9,13},{10,... | collective-permute-start | bytes 688136 | tf_op jit(solution)/shard_map/ppermute | solution.py:17
  120.1 25.1 %collective-permute-start.9 = (bf16[32,3584]{1,0:T(8,128)(2,1)S(1)}, bf16[32,3584]{1,0:T(8,128)(2,1)S(1)}, u32[]{:S(2)}, u32[]{:S(2)}) collective-permute-start(bf16[32,3584]{1,0:T(8,128)(2,1)S(1)} %slice.224), channel_id=1, source_target_pairs={{0,2},{1,5},{2,0},{3,7},{4,6},{5,1},{6,4},{7,3},{8,10},{9,13},{10,... | collective-permute-start | bytes 688136 | tf_op jit(solution)/shard_map/ppermute | solution.py:17
  133.8 8.5 %collective-permute-start.20 = (bf16[64,3584]{1,0:T(8,128)(2,1)S(1)}, bf16[64,3584]{1,0:T(8,128)(2,1)S(1)}, u32[]{:S(2)}, u32[]{:S(2)}) collective-permute-start(bf16[64,3584]{1,0:T(8,128)(2,1)S(1)} %slice.220), channel_id=1, source_target_pairs={{0,2},{1,5},{2,0},{3,7},{4,6},{5,1},{6,4},{7,3},{8,10},{9,13},{10,... | collective-permute-start | bytes 1376264 | tf_op jit(solution)/shard_map/ppermute | solution.py:17
  135.4 9.8 %collective-permute-start.12 = (bf16[32,3584]{1,0:T(8,128)(2,1)S(1)}, bf16[32,3584]{1,0:T(8,128)(2,1)S(1)}, u32[]{:S(2)}, u32[]{:S(2)}) collective-permute-start(bf16[32,3584]{1,0:T(8,128)(2,1)S(1)} %fusion.25), channel_id=1, source_target_pairs={{0,8},{1,9},{2,10},{3,11},{4,12},{5,13},{6,14},{7,15},{8,0},{9,1},... | collective-permute-start | bytes 688136 | tf_op jit(solution)/shard_map/ppermute | solution.py:17
  142.5 10.3 %collective-permute-start.22 = (bf16[32,3584]{1,0:T(8,128)(2,1)S(1)}, bf16[32,3584]{1,0:T(8,128)(2,1)S(1)}, u32[]{:S(2)}, u32[]{:S(2)}) collective-permute-start(bf16[32,3584]{1,0:T(8,128)(2,1)S(1)} %get-tuple-element.18), channel_id=1, source_target_pairs={{0,24},{1,25},{2,26},{3,27},{4,28},{5,29},{6,30},{7,31},{8,16},{9,... | collective-permute-start | bytes 688136 | tf_op jit(solution)/shard_map/ppermute | solution.py:17
  145.2 17.3 %collective-permute-start.21 = (bf16[32,3584]{1,0:T(8,128)(2,1)S(1)}, bf16[32,3584]{1,0:T(8,128)(2,1)S(1)}, u32[]{:S(2)}, u32[]{:S(2)}) collective-permute-start(bf16[32,3584]{1,0:T(8,128)(2,1)S(1)} %get-tuple-element.17), channel_id=1, source_target_pairs={{0,16},{1,17},{2,18},{3,19},{4,20},{5,21},{6,22},{7,23},{8,24},{9,... | collective-permute-start | bytes 688136 | tf_op jit(solution)/shard_map/ppermute | solution.py:17

commit v2 on v1

v2 whole, which is shorter than its diff:
```python
import functools

import jax
import jax.numpy as jnp
from jax import lax
from jax.experimental import pallas as pl
from jax.experimental.pallas import tpu as pltpu
from jax.sharding import PartitionSpec as P

AXIS = "ep"
GROUP = 8
WHOLE = pl.BlockSpec(memory_space=pltpu.VMEM)
ANYWHERE = pl.BlockSpec(memory_space=pl.ANY)
SCALAR = pl.BlockSpec(memory_space=pltpu.SMEM)
F32, BF16 = jnp.float32, jnp.bfloat16


def swap(block, mask_even, mask_odd):
    count = lax.axis_size(AXIS)
    route = [(i, i ^ (mask_odd if i & 1 else mask_even)) for i in range(count)]
    return lax.ppermute(block, AXIS, route)


def first_hop(block):
    return swap(block, 2, 4)


def second_hop(block):
    return swap(block, 4, 2)


def across(block, k):
    return swap(block, GROUP * k, GROUP * k)


def other_core(block):
    return swap(block, 1, 1)


def far_off(array):
    return pltpu.with_memory_space_constraint(array, pltpu.HBM)


def near(array):
    return pltpu.with_memory_space_constraint(array, pltpu.VMEM)


class Line:
    def __init__(self):
        self.last = []

    def __call__(self, kernel, name, outs, scalars, arrays, scratch=(), alias=None, stored=(), inside=True, mib=8):
        count, waits = len(scalars) + len(arrays) + len(stored), len(self.last)

        def body(*refs):
            kernel(*refs[:count], *refs[count + waits :])

        result = pl.pallas_call(
            body,
            in_specs=[SCALAR] * len(scalars) + [WHOLE] * len(arrays) + [ANYWHERE] * (len(stored) + waits),
            out_specs=[WHOLE] * len(outs),
            out_shape=[(pltpu.VMEM if inside else jax.ShapeDtypeStruct)(shape, dtype) for shape, dtype in outs],
            scratch_shapes=scratch,
            input_output_aliases=alias or {},
            compiler_params=pltpu.CompilerParams(vmem_limit_bytes=mib * 1024 * 1024),
            cost_estimate=pl.CostEstimate(flops=1, bytes_accessed=1, transcendentals=0),
            name=name,
        )(*scalars, *[near(a) for a in arrays], *[far_off(a) for a in stored], *self.last)
        self.last = [result[0]]
        return result


def own_kernel(sizes, me_ref, choice_ref, tokens_ref, own_ref, held, sems):
    width, row_count, experts = sizes
    rows, full = own_ref.shape
    copy = pltpu.make_async_copy(tokens_ref, held, sems.at[0])
    copy.start()
    choice = choice_ref[...]
    top_count = choice.shape[1] // 2
    ids, weights = choice[:, :top_count].astype(jnp.int32), choice[:, top_count:]
    lane = lax.broadcasted_iota(jnp.int32, (rows, full - width), 1)
    present = jnp.zeros((rows, full - width), F32)
    weight = jnp.zeros((rows, full - width), F32)
    for k in range(ids.shape[1]):
        named = lax.rem(lane, experts) == ids[:, k : k + 1]
        present = jnp.where(named, 1.0, present)
        weight = jnp.where(named, weights[:, k : k + 1], weight)
    row = lax.broadcasted_iota(jnp.int32, (rows, rows), 0)
    column = lax.broadcasted_iota(jnp.int32, (rows, rows), 1)
    earlier = (row > column) & (row // row_count == column // row_count)
    before = jnp.dot(jnp.where(earlier, 1.0, 0.0).astype(BF16), present.astype(BF16), preferred_element_type=F32)
    slot = jnp.where(present > 0.0, before, -1.0)
    high = weight.astype(BF16).astype(F32)
    value = jnp.where(lane < experts, slot, jnp.where(lane < 2 * experts, high, weight - high))
    own_ref[:, width:] = value.astype(BF16)
    copy.wait()
    for s in range(held.shape[0]):
        own_ref[s * row_count : (s + 1) * row_count, :width] = held[s]


def load_kernel(weights_ref, held_ref, sems):
    pieces = sems.shape[0]
    rows = weights_ref.shape[1] // pieces
    copies = []
    for i in range(pieces):
        part = (slice(None), pl.ds(i * rows, rows))
        copies.append(pltpu.make_async_copy(weights_ref.at[part], held_ref.at[part], sems.at[i]))
    for copy in copies:
        copy.start()
    for copy in copies:
        copy.wait()


def pick(columns, lane_index):
    lane = lax.broadcasted_iota(jnp.int32, columns.shape, 1)
    return jnp.sum(jnp.where(lane == lane_index, columns, 0.0), axis=1, keepdims=True)


def placing(columns, expert, first_row, slots, row_count, capacity):
    rows = columns.shape[0]
    slot = pick(columns, expert).astype(jnp.int32)
    row = lax.broadcasted_iota(jnp.int32, (rows, 1), 0) + first_row
    target = jnp.where(slot >= 0, row // row_count * capacity + slot, -1)
    lane = lax.broadcasted_iota(jnp.int32, (rows, slots), 1)
    return jnp.where(lane == target, 1.0, 0.0).astype(BF16)


def gate_kernel(given_ref, out_ref):
    pass


def pack_kernel(*refs):
    *parts, out = refs
    start = 0
    for part in parts:
        rows = part.shape[0]
        out[start : start + rows, :] = part[...]
        start += rows


def dispatch_kernel(sizes, me_ref, a_ref, b_ref, own_ref, other_ref):
    width, row_count, capacity = sizes
    slots = own_ref.shape[0]
    rows = a_ref.shape[0]
    for out, expert in ((own_ref, me_ref[0]), (other_ref, me_ref[0] ^ 1)):
        place = [
            placing(ref[:, width:].astype(F32), expert, first, slots, row_count, capacity)
            for ref, first in ((a_ref, 0), (b_ref, rows))
        ]
        place = jnp.concatenate(place, axis=0).T
        for ref, first in ((a_ref, 0), (b_ref, rows)):
            half = slots // 2
            lower = first // row_count * capacity
            out[lower : lower + half, :] = jnp.dot(
                place[lower : lower + half, first : first + rows], ref[...], preferred_element_type=F32
            ).astype(BF16)


def expert_kernel(experts, me_ref, own_ref, got_ref, gate_ref, up_ref, down_ref, mine_ref, sent_ref, rows_ref, hidden):
    _, width, units = gate_ref.shape
    slots = own_ref.shape[0]
    rows_ref[:slots, :] = own_ref[...]
    rows_ref[slots:, :] = got_ref[...]
    columns = rows_ref[:, width:].astype(F32)
    weight = pick(columns, me_ref[0] + experts) + pick(columns, me_ref[0] + 2 * experts)
    tile = 256
    for j in range(0, units, tile):
        rows = rows_ref[:, :width]
        gate_val = jnp.dot(rows, gate_ref[0, :, j : j + tile], preferred_element_type=F32)
        up_val = jnp.dot(rows, up_ref[0, :, j : j + tile], preferred_element_type=F32)
        hidden[:, j : j + tile] = (gate_val / (1.0 + jnp.exp(-gate_val)) * up_val).astype(BF16)
    tile = 512
    for n in range(0, width, tile):
        value = jnp.dot(hidden[...], down_ref[0, :, n : n + tile], preferred_element_type=F32)
        value = (value * weight).astype(BF16)
        mine_ref[:, n : n + tile] = value[:slots]
        sent_ref[:, n : n + tile] = value[slots:]


def shared_kernel(a_ref, b_ref, first_ref, second_ref, out_ref):
    width = first_ref.shape[1]
    rows = a_ref.shape[0]
    for half, ref in enumerate((a_ref, b_ref)):
        hidden = []
        for part in (first_ref, second_ref):
            gate_val = jnp.dot(ref[:, :width], part[0], preferred_element_type=F32)
            up_val = jnp.dot(ref[:, :width], part[1], preferred_element_type=F32)
            hidden.append((gate_val / (1.0 + jnp.exp(-gate_val)) * up_val).astype(BF16))
        tile = 512
        for n in range(0, width, tile):
            value = 0.0
            for h, part in zip(hidden, (first_ref, second_ref)):
                value += lax.dot_general(
                    h, part[2, n : n + tile, :], (((1,), (1,)), ((), ())), preferred_element_type=F32
                )
            out_ref[half * rows : (half + 1) * rows, n : n + tile] = value


def combine_kernel(sizes, me_ref, a_ref, b_ref, mine_ref, back_ref, *refs):
    width, row_count, capacity = sizes
    *extra, keep_ref, send_ref = refs
    slots = mine_ref.shape[0]
    rows = a_ref.shape[0]
    half = slots // 2
    for ref, out, first in ((a_ref, keep_ref, 0), (b_ref, send_ref, rows)):
        columns = ref[:, width:].astype(F32)
        lower = first // row_count * capacity
        here = [
            placing(columns, e, 0, half, row_count, capacity) for e in (me_ref[0], me_ref[0] ^ 1)
        ]
        tile = 512
        for n in range(0, width, tile):
            value = sum(
                jnp.dot(p, part[lower : lower + half, n : n + tile], preferred_element_type=F32)
                for p, part in zip(here, (mine_ref, back_ref))
            )
            for part in extra:
                value += part[first : first + rows, n : n + tile]
            out[:, n : n + tile] = value.astype(out.dtype)


def middle_kernel(keep_ref, got_ref, *refs):
    *early, rest_ref, send_ref = refs
    half = rest_ref.shape[0]
    rest = keep_ref[:half, :] + got_ref[:half, :].astype(F32)
    for part in early:
        rest = rest + part[...].astype(F32)
    rest_ref[...] = rest
    send_ref[...] = (keep_ref[half:, :] + got_ref[half:, :].astype(F32)).astype(BF16)


def sum_kernel(*refs):
    *parts, out = refs
    total = parts[0][...]
    for part in parts[1:]:
        total = total + part[...].astype(F32)
    out[...] = total.astype(BF16).reshape(out.shape)


def shards(tokens, expert_ids, combine_weights, w_gate, w_up, w_down, shared_weights):
    step_count, row_count, width = tokens.shape
    top_count = expert_ids.shape[2]
    devices = lax.axis_size(AXIS)
    experts = w_gate.shape[0] * devices
    capacity = max(2, row_count * top_count * 2 // experts)
    planes = devices // GROUP
    units = w_gate.shape[2]
    index = lax.axis_index(AXIS)[None].astype(jnp.int32)
    block = step_count * row_count
    rows = GROUP // 2 * block
    slots = rows // row_count * capacity
    full = width + (3 * experts + 127) // 128 * 128
    sizes = (width, row_count, capacity)
    line = Line()

    choice = jnp.concatenate([expert_ids.astype(F32), combine_weights], axis=2)
    own, = line(
        functools.partial(own_kernel, (width, row_count, experts)),
        "own",
        [((block, full), BF16)],
        [index],
        [choice.reshape(block, 2 * top_count)],
        stored=[tokens],
        scratch=[pltpu.VMEM(tokens.shape, BF16), pltpu.SemaphoreType.DMA((1,))],
    )
    shared_other = other_core(shared_weights)
    far = {0: own, 1: across(own, 1), 2: across(own, 2)}
    held = {}
    hop, both, wide, leaving, chosen, mine, back, part, last, arrived = ({} for _ in range(10))

    def load(name, weights):
        held[name], = line(
            load_kernel,
            "load",
            [(weights.shape, BF16)],
            [],
            [],
            stored=[weights],
            scratch=[pltpu.SemaphoreType.DMA((4,))],
        )

    def enter(k):
        if k > 0:
            far[k], = line(gate_kernel, "enter", [((block, full), BF16)], [], [far[k]], alias={0: 0})
        if k >= 2 and k + 1 < planes:
            if k & 1 == 0:
                far[k + 1] = across(far[k], 1)
        hop[k] = first_hop(far[k])

    def pack(k):
        both[k], = line(pack_kernel, "pack", [((2 * block, full), BF16)], [], [far[k], hop[k]])
        wide[k] = second_hop(both[k])

    def dispatch(k):
        chosen[k], out = line(
            functools.partial(dispatch_kernel, sizes), "dispatch", [((slots, full), BF16)] * 2, [index], [both[k], wide[k]]
        )
        leaving[k] = other_core(out)

    def expert(k):
        mine[k], out = line(
            functools.partial(expert_kernel, experts),
            "expert",
            [((slots, width), BF16)] * 2,
            [index],
            [chosen[k], leaving[k], held["gate"], held["up"], held["down"]],
            scratch=[pltpu.VMEM((2 * slots, full), BF16), pltpu.VMEM((2 * slots, units), BF16)],
        )
        back[k] = other_core(out)

    def shared():
        part["shared"], = line(
            shared_kernel, "shared", [((rows, width), F32)], [], [both[0], wide[0], shared_weights, shared_other]
        )

    def combine(k):
        extra = [part["shared"]] if k == 0 else []
        keep, send = line(
            functools.partial(combine_kernel, sizes),
            "combine",
            [((2 * block, width), F32), ((2 * block, width), BF16)],
            [index],
            [both[k], wide[k], mine[k], back[k], *extra],
        )
        part[k] = (keep, second_hop(send))

    def middle(k, early=()):
        keep, send = line(
            middle_kernel,
            "middle",
            [((block, width), F32), ((block, width), BF16)],
            [],
            [*part[k], *[arrived.pop(j) for j in early]],
        )
        last[k] = (keep, first_hop(send))

    def leave(k):
        out, = line(sum_kernel, "leave", [((block, width), BF16)], [], list(last[k]))
        arrived[k] = across(out, k)

    def final():
        out, = line(
            sum_kernel,
            "final",
            [((step_count, row_count, width), BF16)],
            [],
            [*last[0], *[arrived[k] for k in arrived]],
            inside=False,
        )
        return out

    enter(0)
    pack(0)
    load("gate", w_gate)
    enter(1)
    if planes == 4:
        enter(2)
        dispatch(0)
        pack(1)
        load("up", w_up)
        pack(2)
        enter(3)
        load("down", w_down)
        dispatch(1)
        pack(3)
        dispatch(2)
        expert(1)
        expert(2)
        combine(2)
        dispatch(3)
        combine(1)
        expert(3)
        middle(2)
        combine(3)
        middle(1)
        leave(2)
        expert(0)
        shared()
        middle(3)
        leave(1)
        combine(0)
        leave(3)
        middle(0, early=(2, 1))
    else:
        load("gate", w_gate)
        load("up", w_up)
        load("down", w_down)
        pack(1)
        for k in range(2, planes):
            if k not in far:
                far[k] = across(own, k)
            enter(k)
            pack(k)
        for k in range(planes):
            dispatch(k)
            expert(k)
        shared()
        for k in reversed(range(planes)):
            combine(k)
            middle(k)
            if k > 0:
                leave(k)
    return final()


def solution(mesh):
    placed = (
        P(None, AXIS, None),
        P(None, AXIS, None),
        P(None, AXIS, None),
        P(AXIS, None, None),
        P(AXIS, None, None),
        P(AXIS, None, None),
        P(None, None, AXIS),
    )
    return jax.shard_map(
        shards, mesh=mesh, in_specs=placed, out_specs=P(None, AXIS, None), check_vma=False
    )
```

time: 164 us -> 112 us (0.68)
  waiting for transfers between devices: 82.5 us -> 43.7 us
  matrix products: 15.4 us -> 0 us
  local copies, waits for them, and re-layouts: 8.39 us -> 0.08 us
  starting transfers between devices: 25.1 us -> 32.9 us
  Pallas kernels: 26.3 us -> 33.4 us
  other arithmetic: 5.27 us -> 1.4 us
    ppermute x23 -> x31, waiting for transfers between devices: 82.5 us -> 43.7 us  [swap(): return lax.ppermute(block, AXIS, route)]
    dot_general x8 -> x0, matrix products: 15.4 us -> none  [the longest x2 6.97 us: shared_expert(): lax.dot_general(h, part[2], (((1,), (1,)), ((), ())), preferred_element_t...]
    ppermute x23 -> x31, starting transfers between devices: 25.1 us -> 32.9 us  [swap(): return lax.ppermute(block, AXIS, route)]
    pallas_call x2 -> x32, Pallas kernels: 26.3 us -> 33.4 us  [__call__(): pl.pallas_call(body, in_specs=[SCALAR] * len(scalars) + [WHOLE] * len(arr...]
    unnamed x19 -> x2, local copies, waits for them, and re-layouts: 4.81 us -> 0.01 us
    slice x12 -> x0, local copies, waits for them, and re-layouts: 3.53 us -> none  [the longest x2 2.17 us: experts_of(): result[:half]]
  transfers between devices with their start and end apart: 23 -> 31, of which waited for: 12 -> 13; matrix products, arithmetic and copies ran while one was open for 14% -> 0% of each run, Pallas kernels for 16% -> 28%
where the time goes in v2:
time: 112 us
  waiting for transfers between devices  43.7 us (39%)
  Pallas kernels  33.4 us (30%)
  starting transfers between devices  32.9 us (29%)
  other arithmetic  1.4 us (1%)
    ppermute x31, waiting for transfers between devices, swap(): return lax.ppermute(block, AXIS, route)  43.7 us
    pallas_call x32, Pallas kernels, __call__(): pl.pallas_call(body, in_specs=[SCALAR] * len(scalars) + [WHOLE] * len(arr...  33.4 us
    ppermute x31, starting transfers between devices, swap(): return lax.ppermute(block, AXIS, route)  32.9 us
  transfers between devices with their start and end apart: 31, of which 13 were waited for; matrix products, arithmetic and copies ran while one was open for 0% of the time, Pallas kernels for 28%

profile of v2, /device:TPU:0, one launch (start us, length us, event | category | flops | bytes accessed | tf_op | source)
XLA Modules:
  0.0 111.8 jit_solution(15233893300556437021)
XLA Ops:
  2.4 3.0 %collective-permute-start = (bf16[32,3712]{1,0:T(8,128)(2,1)S(1)}, bf16[32,3712]{1,0:T(8,128)(2,1)S(1)}, u32[]{:S(2)}, u32[]{:S(2)}) collective-permute-start(bf16[32,3712]{1,0:T(8,128)(2,1)S(1)} %own.1.refs_0_.refs_2_), channel_id=1, source_target_pairs={{0,2},{1,5},{2,0},{3,7},{4,6},{5,1},{6,4},{7,3},{8,10},{9,13},{10,... | collective-permute-start | bytes 712712 | tf_op jit(solution)/shard_map/ppermute | solution.py:21
  5.5 1.6 %collective-permute-start.3 = (bf16[32,3712]{1,0:T(8,128)(2,1)S(1)}, bf16[32,3712]{1,0:T(8,128)(2,1)S(1)}, u32[]{:S(2)}, u32[]{:S(2)}) collective-permute-start(bf16[32,3712]{1,0:T(8,128)(2,1)S(1)} %own.1.refs_0_.refs_2_), channel_id=1, source_target_pairs={{0,8},{1,9},{2,10},{3,11},{4,12},{5,13},{6,14},{7,15},{8,0},{9,1},... | collective-permute-start | bytes 712712 | tf_op jit(solution)/shard_map/ppermute | solution.py:21
  7.0 2.5 %collective-permute-done.refs_1_ = bf16[32,3712]{1,0:T(8,128)(2,1)S(1)} collective-permute-done((bf16[32,3712]{1,0:T(8,128)(2,1)S(1)}, bf16[32,3712]{1,0:T(8,128)(2,1)S(1)}, u32[]{:S(2)}, u32[]{:S(2)}) %collective-permute-start) | collective-permute-done | bytes 237600 | tf_op jit(solution)/shard_map/ppermute | solution.py:21
  9.6 2.1 %collective-permute-start.1 = (bf16[64,3712]{1,0:T(8,128)(2,1)S(1)}, bf16[64,3712]{1,0:T(8,128)(2,1)S(1)}, u32[]{:S(2)}, u32[]{:S(2)}) collective-permute-start(bf16[64,3712]{1,0:T(8,128)(2,1)S(1)} %pack.4.refs_1_.refs_0_), channel_id=1, source_target_pairs={{0,4},{1,3},{2,6},{3,1},{4,0},{5,7},{6,2},{7,5},{8,12},{9,11},{10,... | collective-permute-start | bytes 1425416 | tf_op jit(solution)/shard_map/ppermute | solution.py:21
  11.7 2.6 %collective-permute-start.2 = (bf16[32,3712]{1,0:T(8,128)(2,1)S(1)}, bf16[32,3712]{1,0:T(8,128)(2,1)S(1)}, u32[]{:S(2)}, u32[]{:S(2)}) collective-permute-start(bf16[32,3712]{1,0:T(8,128)(2,1)S(1)} %own.1.refs_0_.refs_2_), channel_id=1, source_target_pairs={{0,16},{1,17},{2,18},{3,19},{4,20},{5,21},{6,22},{7,23},{8,24},{9,... | collective-permute-start | bytes 712712 | tf_op jit(solution)/shard_map/ppermute | solution.py:21
  14.3 3.2 %load.3.refs_1_.refs_3_ = bf16[1,3584,1024]{2,1,0:T(8,128)(2,1)S(1)} custom-call(bf16[1,3584,1024]{2,1,0:T(8,128)(2,1)} %refs_0_.3, bf16[64,3712]{1,0:T(8,128)(2,1)S(1)} %pack.4.refs_1_.refs_0_), custom_call_target="tpu_custom_call" | custom-call | flops 1 | bytes 1 | tf_op jit(solution)/shard_map/load/pallas_call | solution.py:58
  17.5 1.6 %collective-permute-start.5 = (bf16[32,3712]{1,0:T(8,128)(2,1)S(1)}, bf16[32,3712]{1,0:T(8,128)(2,1)S(1)}, u32[]{:S(2)}, u32[]{:S(2)}) collective-permute-start(bf16[32,3712]{1,0:T(8,128)(2,1)S(1)} %enter.3.refs_1_.refs_0_), channel_id=1, source_target_pairs={{0,2},{1,5},{2,0},{3,7},{4,6},{5,1},{6,4},{7,3},{8,10},{9,13},{10,... | collective-permute-start | bytes 712712 | tf_op jit(solution)/shard_map/ppermute | solution.py:21
  19.1 5.0 %collective-permute-done.2.refs_0_ = bf16[32,3712]{1,0:T(8,128)(2,1)S(1)} collective-permute-done((bf16[32,3712]{1,0:T(8,128)(2,1)S(1)}, bf16[32,3712]{1,0:T(8,128)(2,1)S(1)}, u32[]{:S(2)}, u32[]{:S(2)}) %collective-permute-start.2) | collective-permute-done | bytes 237600 | tf_op jit(solution)/shard_map/ppermute | solution.py:21
  25.2 1.6 %collective-permute-start.10 = (bf16[64,3712]{1,0:T(8,128)(2,1)S(1)}, bf16[64,3712]{1,0:T(8,128)(2,1)S(1)}, u32[]{:S(2)}, u32[]{:S(2)}) collective-permute-start(bf16[64,3712]{1,0:T(8,128)(2,1)S(1)} %pack.5.refs_1_), channel_id=1, source_target_pairs={{0,4},{1,3},{2,6},{3,1},{4,0},{5,7},{6,2},{7,5},{8,12},{9,11},{10,... | collective-permute-start | bytes 1425416 | tf_op jit(solution)/shard_map/ppermute | solution.py:21
  27.5 3.2 %load.4.refs_2_.refs_4_ = bf16[1,3584,1024]{2,1,0:T(8,128)(2,1)S(1)} custom-call(bf16[1,3584,1024]{2,1,0:T(8,128)(2,1)} %refs_0_.4, bf16[64,3712]{1,0:T(8,128)(2,1)S(1)} %pack.5.refs_1_), custom_call_target="tpu_custom_call" | custom-call | flops 1 | bytes 1 | tf_op jit(solution)/shard_map/load/pallas_call | solution.py:58
  30.8 1.7 %collective-permute-done.7.refs_1_ = bf16[32,3712]{1,0:T(8,128)(2,1)S(1)} collective-permute-done((bf16[32,3712]{1,0:T(8,128)(2,1)S(1)}, bf16[32,3712]{1,0:T(8,128)(2,1)S(1)}, u32[]{:S(2)}, u32[]{:S(2)}) %collective-permute-start.7) | collective-permute-done | bytes 237600 | tf_op jit(solution)/shard_map/ppermute | solution.py:21
  32.5 1.8 %collective-permute-start.8 = (bf16[64,3712]{1,0:T(8,128)(2,1)S(1)}, bf16[64,3712]{1,0:T(8,128)(2,1)S(1)}, u32[]{:S(2)}, u32[]{:S(2)}) collective-permute-start(bf16[64,3712]{1,0:T(8,128)(2,1)S(1)} %pack.6.refs_1_), channel_id=1, source_target_pairs={{0,4},{1,3},{2,6},{3,1},{4,0},{5,7},{6,2},{7,5},{8,12},{9,11},{10,... | collective-permute-start | bytes 1425416 | tf_op jit(solution)/shard_map/ppermute | solution.py:21
  35.0 3.2 %load.5.refs_3_.refs_5_ = bf16[1,1024,3584]{2,1,0:T(8,128)(2,1)S(1)} custom-call(bf16[1,1024,3584]{2,1,0:T(8,128)(2,1)} %refs_0_.5, bf16[32,3712]{1,0:T(8,128)(2,1)S(1)} %enter.5.refs_1_.refs_0_), custom_call_target="tpu_custom_call" | custom-call | flops 1 | bytes 1 | tf_op jit(solution)/shard_map/load/pallas_call | solution.py:58
  38.9 4.0 %collective-permute-done.9.refs_1_ = bf16[32,3712]{1,0:T(8,128)(2,1)S(1)} collective-permute-done((bf16[32,3712]{1,0:T(8,128)(2,1)S(1)}, bf16[32,3712]{1,0:T(8,128)(2,1)S(1)}, u32[]{:S(2)}, u32[]{:S(2)}) %collective-permute-start.9) | collective-permute-done | bytes 237600 | tf_op jit(solution)/shard_map/ppermute | solution.py:21
  44.5 1.6 %collective-permute-start.15 = (bf16[64,3712]{1,0:T(8,128)(2,1)S(1)}, bf16[64,3712]{1,0:T(8,128)(2,1)S(1)}, u32[]{:S(2)}, u32[]{:S(2)}) collective-permute-start(bf16[64,3712]{1,0:T(8,128)(2,1)S(1)} %pack.7.refs_3_.refs_1_), channel_id=1, source_target_pairs={{0,4},{1,3},{2,6},{3,1},{4,0},{5,7},{6,2},{7,5},{8,12},{9,11},{10,... | collective-permute-start | bytes 1425416 | tf_op jit(solution)/shard_map/ppermute | solution.py:21
  46.2 3.3 %expert.4 = (bf16[64,3584]{1,0:T(8,128)(2,1)S(1)}, bf16[64,3584]{1,0:T(8,128)(2,1)S(1)}) custom-call(s32[1]{0:T(128)} %bitcast.refs_0_, bf16[64,3712]{1,0:T(8,128)(2,1)S(1)} %get-tuple-element.39.refs_2_.refs_1_, bf16[64,3712]{1,0:T(8,128)(2,1)S(1)} %collective-permute-done.12.refs_2_, bf16[1,3584,1024]{2,1,0:T(8,128)(2,1)S(1)} %load.3.refs_1_.refs_3_, ...), custom_call_target="tpu_custom_call" | custom-call | flops 1 | bytes 1 | tf_op jit(solution)/shard_map/expert/pallas_call | solution.py:58
  49.5 3.3 %expert.5 = (bf16[64,3584]{1,0:T(8,128)(2,1)S(1)}, bf16[64,3584]{1,0:T(8,128)(2,1)S(1)}) custom-call(s32[1]{0:T(128)} %bitcast.refs_0_, bf16[64,3712]{1,0:T(8,128)(2,1)S(1)} %get-tuple-element.40.refs_6_.refs_1_, bf16[64,3712]{1,0:T(8,128)(2,1)S(1)} %collective-permute-done.11.refs_2_, bf16[1,3584,1024]{2,1,0:T(8,128)(2,1)S(1)} %load.3.refs_1_.refs_3_, ...), custom_call_target="tpu_custom_call" | custom-call | flops 1 | bytes 1 | tf_op jit(solution)/shard_map/expert/pallas_call | solution.py:58
  52.9 1.8 %collective-permute-done.13.refs_4_ = bf16[64,3584]{1,0:T(8,128)(2,1)S(1)} collective-permute-done((bf16[64,3584]{1,0:T(8,128)(2,1)S(1)}, bf16[64,3584]{1,0:T(8,128)(2,1)S(1)}, u32[]{:S(2)}, u32[]{:S(2)}) %collective-permute-start.13) | collective-permute-done | bytes 458784 | tf_op jit(solution)/shard_map/ppermute | solution.py:21
  57.2 1.4 %collective-permute-done.17.refs_4_ = bf16[64,3584]{1,0:T(8,128)(2,1)S(1)} collective-permute-done((bf16[64,3584]{1,0:T(8,128)(2,1)S(1)}, bf16[64,3584]{1,0:T(8,128)(2,1)S(1)}, u32[]{:S(2)}, u32[]{:S(2)}) %collective-permute-start.17) | collective-permute-done | bytes 458784 | tf_op jit(solution)/shard_map/ppermute | solution.py:21
  59.3 3.5 %expert.6 = (bf16[64,3584]{1,0:T(8,128)(2,1)S(1)}, bf16[64,3584]{1,0:T(8,128)(2,1)S(1)}) custom-call(s32[1]{0:T(128)} %bitcast.refs_0_, bf16[64,3712]{1,0:T(8,128)(2,1)S(1)} %get-tuple-element.48.refs_5_.refs_1_, bf16[64,3712]{1,0:T(8,128)(2,1)S(1)} %collective-permute-done.16.refs_2_, bf16[1,3584,1024]{2,1,0:T(8,128)(2,1)S(1)} %load.3.refs_1_.refs_3_, ...), custom_call_target="tpu_custom_call" | custom-call | flops 1 | bytes 1 | tf_op jit(solution)/shard_map/expert/pallas_call | solution.py:58
  63.7 1.4 %collective-permute-done.14.refs_1_ = bf16[64,3584]{1,0:T(8,128)(2,1)S(1)} collective-permute-done((bf16[64,3584]{1,0:T(8,128)(2,1)S(1)}, bf16[64,3584]{1,0:T(8,128)(2,1)S(1)}, u32[]{:S(2)}, u32[]{:S(2)}) %collective-permute-start.14) | collective-permute-done | bytes 458784 | tf_op jit(solution)/shard_map/ppermute | solution.py:21
  67.8 6.2 %collective-permute-done.19.refs_1_ = bf16[64,3584]{1,0:T(8,128)(2,1)S(1)} collective-permute-done((bf16[64,3584]{1,0:T(8,128)(2,1)S(1)}, bf16[64,3584]{1,0:T(8,128)(2,1)S(1)}, u32[]{:S(2)}, u32[]{:S(2)}) %collective-permute-start.19) | collective-permute-done | bytes 458784 | tf_op jit(solution)/shard_map/ppermute | solution.py:21
  74.2 3.3 %expert.7 = (bf16[64,3584]{1,0:T(8,128)(2,1)S(1)}, bf16[64,3584]{1,0:T(8,128)(2,1)S(1)}) custom-call(s32[1]{0:T(128)} %bitcast.refs_0_, bf16[64,3712]{1,0:T(8,128)(2,1)S(1)} %get-tuple-element.37.refs_2_.refs_1_, bf16[64,3712]{1,0:T(8,128)(2,1)S(1)} %collective-permute-done.4.refs_2_, bf16[1,3584,1024]{2,1,0:T(8,128)(2,1)S(1)} %load.3.refs_1_.refs_3_, ...), custom_call_target="tpu_custom_call" | custom-call | flops 1 | bytes 1 | tf_op jit(solution)/shard_map/expert/pallas_call | solution.py:58
  78.3 2.6 %shared.1.refs_2_.refs_5_ = f32[128,3584]{1,0:T(8,128)S(1)} custom-call(bf16[64,3712]{1,0:T(8,128)(2,1)S(1)} %pack.4.refs_1_.refs_0_, bf16[64,3712]{1,0:T(8,128)(2,1)S(1)} %collective-permute-done.1.refs_2_.refs_1_, bf16[3,3584,128]{2,1,0:T(8,128)(2,1)S(1)} %copy-done, bf16[3,3584,128]{2,1,0:T(8,128)(2,1)S(1)} %collective-permute-done.22.refs_3_, ...), custom_call_target="tpu_custom_call" | custom-call | flops 1 | bytes 1 | tf_op jit(solution)/shard_map/shared/pallas_call | solution.py:58
  81.0 2.6 %collective-permute-done.23.refs_1_ = bf16[32,3584]{1,0:T(8,128)(2,1)S(1)} collective-permute-done((bf16[32,3584]{1,0:T(8,128)(2,1)S(1)}, bf16[32,3584]{1,0:T(8,128)(2,1)S(1)}, u32[]{:S(2)}, u32[]{:S(2)}) %collective-permute-start.23) | collective-permute-done | bytes 229408 | tf_op jit(solution)/shard_map/ppermute | solution.py:21
  85.1 1.4 %collective-permute-start.28 = (bf16[32,3584]{1,0:T(8,128)(2,1)S(1)}, bf16[32,3584]{1,0:T(8,128)(2,1)S(1)}, u32[]{:S(2)}, u32[]{:S(2)}) collective-permute-start(bf16[32,3584]{1,0:T(8,128)(2,1)S(1)} %get-tuple-element.66), channel_id=1, source_target_pairs={{0,2},{1,5},{2,0},{3,7},{4,6},{5,1},{6,4},{7,3},{8,10},{9,13},{10,... | collective-permute-start | bytes 688136 | tf_op jit(solution)/shard_map/ppermute | solution.py:21
  86.5 1.6 %collective-permute-start.26 = (bf16[32,3584]{1,0:T(8,128)(2,1)S(1)}, bf16[32,3584]{1,0:T(8,128)(2,1)S(1)}, u32[]{:S(2)}, u32[]{:S(2)}) collective-permute-start(bf16[32,3584]{1,0:T(8,128)(2,1)S(1)} %leave.3.refs_6_), channel_id=1, source_target_pairs={{0,16},{1,17},{2,18},{3,19},{4,20},{5,21},{6,22},{7,23},{8,24},{9,... | collective-permute-start | bytes 688136 | tf_op jit(solution)/shard_map/ppermute | solution.py:21
  88.1 2.4 %collective-permute-start.27 = (bf16[32,3584]{1,0:T(8,128)(2,1)S(1)}, bf16[32,3584]{1,0:T(8,128)(2,1)S(1)}, u32[]{:S(2)}, u32[]{:S(2)}) collective-permute-start(bf16[32,3584]{1,0:T(8,128)(2,1)S(1)} %leave.4.refs_6_), channel_id=1, source_target_pairs={{0,8},{1,9},{2,10},{3,11},{4,12},{5,13},{6,14},{7,15},{8,0},{9,1},... | collective-permute-start | bytes 688136 | tf_op jit(solution)/shard_map/ppermute | solution.py:21
  90.5 3.2 %collective-permute-done.28.refs_1_ = bf16[32,3584]{1,0:T(8,128)(2,1)S(1)} collective-permute-done((bf16[32,3584]{1,0:T(8,128)(2,1)S(1)}, bf16[32,3584]{1,0:T(8,128)(2,1)S(1)}, u32[]{:S(2)}, u32[]{:S(2)}) %collective-permute-start.28) | collective-permute-done | bytes 229408 | tf_op jit(solution)/shard_map/ppermute | solution.py:21
  93.7 3.4 %collective-permute-start.30 = (bf16[32,3584]{1,0:T(8,128)(2,1)S(1)}, bf16[32,3584]{1,0:T(8,128)(2,1)S(1)}, u32[]{:S(2)}, u32[]{:S(2)}) collective-permute-start(bf16[32,3584]{1,0:T(8,128)(2,1)S(1)} %leave.5.refs_4_), channel_id=1, source_target_pairs={{0,24},{1,25},{2,26},{3,27},{4,28},{5,29},{6,30},{7,31},{8,16},{9,... | collective-permute-start | bytes 688136 | tf_op jit(solution)/shard_map/ppermute | solution.py:21
  97.2 7.6 %collective-permute-done.26.refs_2_ = bf16[32,3584]{1,0:T(8,128)(2,1)S(1)} collective-permute-done((bf16[32,3584]{1,0:T(8,128)(2,1)S(1)}, bf16[32,3584]{1,0:T(8,128)(2,1)S(1)}, u32[]{:S(2)}, u32[]{:S(2)}) %collective-permute-start.26) | collective-permute-done | bytes 229408 | tf_op jit(solution)/shard_map/ppermute | solution.py:21
  105.6 5.4 %collective-permute-done.29.refs_1_ = bf16[32,3584]{1,0:T(8,128)(2,1)S(1)} collective-permute-done((bf16[32,3584]{1,0:T(8,128)(2,1)S(1)}, bf16[32,3584]{1,0:T(8,128)(2,1)S(1)}, u32[]{:S(2)}, u32[]{:S(2)}) %collective-permute-start.29) | collective-permute-done | bytes 229408 | tf_op jit(solution)/shard_map/ppermute | solution.py:21
  (67 shorter events, 18.3 us)
Async XLA Ops:
  2.4 7.1 %collective-permute-start = (bf16[32,3712]{1,0:T(8,128)(2,1)S(1)}, bf16[32,3712]{1,0:T(8,128)(2,1)S(1)}, u32[]{:S(2)}, u32[]{:S(2)}) collective-permute-start(bf16[32,3712]{1,0:T(8,128)(2,1)S(1)} %own.1.refs_0_.refs_2_), channel_id=1, source_target_pairs={{0,2},{1,5},{2,0},{3,7},{4,6},{5,1},{6,4},{7,3},{8,10},{9,13},{10,... | collective-permute-start | bytes 712712 | tf_op jit(solution)/shard_map/ppermute | solution.py:21
  5.5 12.0 %collective-permute-start.3 = (bf16[32,3712]{1,0:T(8,128)(2,1)S(1)}, bf16[32,3712]{1,0:T(8,128)(2,1)S(1)}, u32[]{:S(2)}, u32[]{:S(2)}) collective-permute-start(bf16[32,3712]{1,0:T(8,128)(2,1)S(1)} %own.1.refs_0_.refs_2_), channel_id=1, source_target_pairs={{0,8},{1,9},{2,10},{3,11},{4,12},{5,13},{6,14},{7,15},{8,0},{9,1},... | collective-permute-start | bytes 712712 | tf_op jit(solution)/shard_map/ppermute | solution.py:21
  9.6 14.9 %collective-permute-start.1 = (bf16[64,3712]{1,0:T(8,128)(2,1)S(1)}, bf16[64,3712]{1,0:T(8,128)(2,1)S(1)}, u32[]{:S(2)}, u32[]{:S(2)}) collective-permute-start(bf16[64,3712]{1,0:T(8,128)(2,1)S(1)} %pack.4.refs_1_.refs_0_), channel_id=1, source_target_pairs={{0,4},{1,3},{2,6},{3,1},{4,0},{5,7},{6,2},{7,5},{8,12},{9,11},{10,... | collective-permute-start | bytes 1425416 | tf_op jit(solution)/shard_map/ppermute | solution.py:21
  11.7 12.3 %collective-permute-start.2 = (bf16[32,3712]{1,0:T(8,128)(2,1)S(1)}, bf16[32,3712]{1,0:T(8,128)(2,1)S(1)}, u32[]{:S(2)}, u32[]{:S(2)}) collective-permute-start(bf16[32,3712]{1,0:T(8,128)(2,1)S(1)} %own.1.refs_0_.refs_2_), channel_id=1, source_target_pairs={{0,16},{1,17},{2,18},{3,19},{4,20},{5,21},{6,22},{7,23},{8,24},{9,... | collective-permute-start | bytes 712712 | tf_op jit(solution)/shard_map/ppermute | solution.py:21
  17.5 7.7 %collective-permute-start.5 = (bf16[32,3712]{1,0:T(8,128)(2,1)S(1)}, bf16[32,3712]{1,0:T(8,128)(2,1)S(1)}, u32[]{:S(2)}, u32[]{:S(2)}) collective-permute-start(bf16[32,3712]{1,0:T(8,128)(2,1)S(1)} %enter.3.refs_1_.refs_0_), channel_id=1, source_target_pairs={{0,2},{1,5},{2,0},{3,7},{4,6},{5,1},{6,4},{7,3},{8,10},{9,13},{10,... | collective-permute-start | bytes 712712 | tf_op jit(solution)/shard_map/ppermute | solution.py:21
  24.0 8.4 %collective-permute-start.7 = (bf16[32,3712]{1,0:T(8,128)(2,1)S(1)}, bf16[32,3712]{1,0:T(8,128)(2,1)S(1)}, u32[]{:S(2)}, u32[]{:S(2)}) collective-permute-start(bf16[32,3712]{1,0:T(8,128)(2,1)S(1)} %enter.4.refs_3_.refs_0_), channel_id=1, source_target_pairs={{0,2},{1,5},{2,0},{3,7},{4,6},{5,1},{6,4},{7,3},{8,10},{9,13},{10,... | collective-permute-start | bytes 712712 | tf_op jit(solution)/shard_map/ppermute | solution.py:21
  25.2 12.9 %collective-permute-start.10 = (bf16[64,3712]{1,0:T(8,128)(2,1)S(1)}, bf16[64,3712]{1,0:T(8,128)(2,1)S(1)}, u32[]{:S(2)}, u32[]{:S(2)}) collective-permute-start(bf16[64,3712]{1,0:T(8,128)(2,1)S(1)} %pack.5.refs_1_), channel_id=1, source_target_pairs={{0,4},{1,3},{2,6},{3,1},{4,0},{5,7},{6,2},{7,5},{8,12},{9,11},{10,... | collective-permute-start | bytes 1425416 | tf_op jit(solution)/shard_map/ppermute | solution.py:21
  26.9 7.4 %collective-permute-start.6 = (bf16[32,3712]{1,0:T(8,128)(2,1)S(1)}, bf16[32,3712]{1,0:T(8,128)(2,1)S(1)}, u32[]{:S(2)}, u32[]{:S(2)}) collective-permute-start(bf16[32,3712]{1,0:T(8,128)(2,1)S(1)} %enter.4.refs_3_.refs_0_), channel_id=1, source_target_pairs={{0,8},{1,9},{2,10},{3,11},{4,12},{5,13},{6,14},{7,15},{8,0},{9,1},... | collective-permute-start | bytes 712712 | tf_op jit(solution)/shard_map/ppermute | solution.py:21
  30.7 3.6 %copy-start = (bf16[3,3584,128]{2,1,0:T(8,128)(2,1)S(1)}, bf16[3,3584,128]{2,1,0:T(8,128)(2,1)}, u32[]{:S(2)}) copy-start(bf16[3,3584,128]{2,1,0:T(8,128)(2,1)} %refs_2_.3) | copy-start | bytes 8257540
  32.5 11.3 %collective-permute-start.8 = (bf16[64,3712]{1,0:T(8,128)(2,1)S(1)}, bf16[64,3712]{1,0:T(8,128)(2,1)S(1)}, u32[]{:S(2)}, u32[]{:S(2)}) collective-permute-start(bf16[64,3712]{1,0:T(8,128)(2,1)S(1)} %pack.6.refs_1_), channel_id=1, source_target_pairs={{0,4},{1,3},{2,6},{3,1},{4,0},{5,7},{6,2},{7,5},{8,12},{9,11},{10,... | collective-permute-start | bytes 1425416 | tf_op jit(solution)/shard_map/ppermute | solution.py:21
  34.3 44.0 %collective-permute-start.22 = (bf16[3,3584,128]{2,1,0:T(8,128)(2,1)S(1)}, bf16[3,3584,128]{2,1,0:T(8,128)(2,1)S(1)}, u32[]{:S(2)}, u32[]{:S(2)}) collective-permute-start(bf16[3,3584,128]{2,1,0:T(8,128)(2,1)S(1)} %copy-done), channel_id=1, source_target_pairs={{0,1},{1,0},{2,3},{3,2},{4,5},{5,4},{6,7},{7,6},{8,9},{9,8},{10,11... | collective-permute-start | bytes 8257544 | tf_op jit(solution)/shard_map/ppermute | solution.py:21
  34.3 8.5 %collective-permute-start.9 = (bf16[32,3712]{1,0:T(8,128)(2,1)S(1)}, bf16[32,3712]{1,0:T(8,128)(2,1)S(1)}, u32[]{:S(2)}, u32[]{:S(2)}) collective-permute-start(bf16[32,3712]{1,0:T(8,128)(2,1)S(1)} %enter.5.refs_1_.refs_0_), channel_id=1, source_target_pairs={{0,2},{1,5},{2,0},{3,7},{4,6},{5,1},{6,4},{7,3},{8,10},{9,13},{10,... | collective-permute-start | bytes 712712 | tf_op jit(solution)/shard_map/ppermute | solution.py:21
  38.8 7.3 %collective-permute-start.12 = (bf16[64,3712]{1,0:T(8,128)(2,1)S(1)}, bf16[64,3712]{1,0:T(8,128)(2,1)S(1)}, u32[]{:S(2)}, u32[]{:S(2)}) collective-permute-start(bf16[64,3712]{1,0:T(8,128)(2,1)S(1)} %get-tuple-element.42), channel_id=1, source_target_pairs={{0,1},{1,0},{2,3},{3,2},{4,5},{5,4},{6,7},{7,6},{8,9},{9,8},{10,11... | collective-permute-start | bytes 1425416 | tf_op jit(solution)/shard_map/ppermute | solution.py:21
  44.4 5.0 %collective-permute-start.11 = (bf16[64,3712]{1,0:T(8,128)(2,1)S(1)}, bf16[64,3712]{1,0:T(8,128)(2,1)S(1)}, u32[]{:S(2)}, u32[]{:S(2)}) collective-permute-start(bf16[64,3712]{1,0:T(8,128)(2,1)S(1)} %get-tuple-element.41), channel_id=1, source_target_pairs={{0,1},{1,0},{2,3},{3,2},{4,5},{5,4},{6,7},{7,6},{8,9},{9,8},{10,11... | collective-permute-start | bytes 1425416 | tf_op jit(solution)/shard_map/ppermute | solution.py:21
  44.5 10.9 %collective-permute-start.15 = (bf16[64,3712]{1,0:T(8,128)(2,1)S(1)}, bf16[64,3712]{1,0:T(8,128)(2,1)S(1)}, u32[]{:S(2)}, u32[]{:S(2)}) collective-permute-start(bf16[64,3712]{1,0:T(8,128)(2,1)S(1)} %pack.7.refs_3_.refs_1_), channel_id=1, source_target_pairs={{0,4},{1,3},{2,6},{3,1},{4,0},{5,7},{6,2},{7,5},{8,12},{9,11},{10,... | collective-permute-start | bytes 1425416 | tf_op jit(solution)/shard_map/ppermute | solution.py:21
  52.8 1.9 %collective-permute-start.13 = (bf16[64,3584]{1,0:T(8,128)(2,1)S(1)}, bf16[64,3584]{1,0:T(8,128)(2,1)S(1)}, u32[]{:S(2)}, u32[]{:S(2)}) collective-permute-start(bf16[64,3584]{1,0:T(8,128)(2,1)S(1)} %get-tuple-element.45), channel_id=1, source_target_pairs={{0,1},{1,0},{2,3},{3,2},{4,5},{5,4},{6,7},{7,6},{8,9},{9,8},{10,11... | collective-permute-start | bytes 1376264 | tf_op jit(solution)/shard_map/ppermute | solution.py:21
  56.1 3.3 %collective-permute-start.16 = (bf16[64,3712]{1,0:T(8,128)(2,1)S(1)}, bf16[64,3712]{1,0:T(8,128)(2,1)S(1)}, u32[]{:S(2)}, u32[]{:S(2)}) collective-permute-start(bf16[64,3712]{1,0:T(8,128)(2,1)S(1)} %get-tuple-element.49), channel_id=1, source_target_pairs={{0,1},{1,0},{2,3},{3,2},{4,5},{5,4},{6,7},{7,6},{8,9},{9,8},{10,11... | collective-permute-start | bytes 1425416 | tf_op jit(solution)/shard_map/ppermute | solution.py:21
  56.3 2.3 %collective-permute-start.17 = (bf16[64,3584]{1,0:T(8,128)(2,1)S(1)}, bf16[64,3584]{1,0:T(8,128)(2,1)S(1)}, u32[]{:S(2)}, u32[]{:S(2)}) collective-permute-start(bf16[64,3584]{1,0:T(8,128)(2,1)S(1)} %get-tuple-element.50), channel_id=1, source_target_pairs={{0,1},{1,0},{2,3},{3,2},{4,5},{5,4},{6,7},{7,6},{8,9},{9,8},{10,11... | collective-permute-start | bytes 1376264 | tf_op jit(solution)/shard_map/ppermute | solution.py:21
  56.6 8.5 %collective-permute-start.14 = (bf16[64,3584]{1,0:T(8,128)(2,1)S(1)}, bf16[64,3584]{1,0:T(8,128)(2,1)S(1)}, u32[]{:S(2)}, u32[]{:S(2)}) collective-permute-start(bf16[64,3584]{1,0:T(8,128)(2,1)S(1)} %get-tuple-element.47), channel_id=1, source_target_pairs={{0,4},{1,3},{2,6},{3,1},{4,0},{5,7},{6,2},{7,5},{8,12},{9,11},{10,... | collective-permute-start | bytes 1376264 | tf_op jit(solution)/shard_map/ppermute | solution.py:21
  57.1 17.1 %collective-permute-start.4 = (bf16[64,3712]{1,0:T(8,128)(2,1)S(1)}, bf16[64,3712]{1,0:T(8,128)(2,1)S(1)}, u32[]{:S(2)}, u32[]{:S(2)}) collective-permute-start(bf16[64,3712]{1,0:T(8,128)(2,1)S(1)} %get-tuple-element.38), channel_id=1, source_target_pairs={{0,1},{1,0},{2,3},{3,2},{4,5},{5,4},{6,7},{7,6},{8,9},{9,8},{10,11... | collective-permute-start | bytes 1425416 | tf_op jit(solution)/shard_map/ppermute | solution.py:21
  62.8 3.1 %collective-permute-start.20 = (bf16[64,3584]{1,0:T(8,128)(2,1)S(1)}, bf16[64,3584]{1,0:T(8,128)(2,1)S(1)}, u32[]{:S(2)}, u32[]{:S(2)}) collective-permute-start(bf16[64,3584]{1,0:T(8,128)(2,1)S(1)} %get-tuple-element.56), channel_id=1, source_target_pairs={{0,1},{1,0},{2,3},{3,2},{4,5},{5,4},{6,7},{7,6},{8,9},{9,8},{10,11... | collective-permute-start | bytes 1376264 | tf_op jit(solution)/shard_map/ppermute | solution.py:21
  63.1 10.9 %collective-permute-start.19 = (bf16[64,3584]{1,0:T(8,128)(2,1)S(1)}, bf16[64,3584]{1,0:T(8,128)(2,1)S(1)}, u32[]{:S(2)}, u32[]{:S(2)}) collective-permute-start(bf16[64,3584]{1,0:T(8,128)(2,1)S(1)} %get-tuple-element.55), channel_id=1, source_target_pairs={{0,4},{1,3},{2,6},{3,1},{4,0},{5,7},{6,2},{7,5},{8,12},{9,11},{10,... | collective-permute-start | bytes 1376264 | tf_op jit(solution)/shard_map/ppermute | solution.py:21
  65.2 8.9 %collective-permute-start.18 = (bf16[32,3584]{1,0:T(8,128)(2,1)S(1)}, bf16[32,3584]{1,0:T(8,128)(2,1)S(1)}, u32[]{:S(2)}, u32[]{:S(2)}) collective-permute-start(bf16[32,3584]{1,0:T(8,128)(2,1)S(1)} %get-tuple-element.54), channel_id=1, source_target_pairs={{0,2},{1,5},{2,0},{3,7},{4,6},{5,1},{6,4},{7,3},{8,10},{9,13},{10,... | collective-permute-start | bytes 688136 | tf_op jit(solution)/shard_map/ppermute | solution.py:21
  66.6 14.3 %collective-permute-start.24 = (bf16[64,3584]{1,0:T(8,128)(2,1)S(1)}, bf16[64,3584]{1,0:T(8,128)(2,1)S(1)}, u32[]{:S(2)}, u32[]{:S(2)}) collective-permute-start(bf16[64,3584]{1,0:T(8,128)(2,1)S(1)} %get-tuple-element.62), channel_id=1, source_target_pairs={{0,4},{1,3},{2,6},{3,1},{4,0},{5,7},{6,2},{7,5},{8,12},{9,11},{10,... | collective-permute-start | bytes 1376264 | tf_op jit(solution)/shard_map/ppermute | solution.py:21
  77.5 6.2 %collective-permute-start.21 = (bf16[64,3584]{1,0:T(8,128)(2,1)S(1)}, bf16[64,3584]{1,0:T(8,128)(2,1)S(1)}, u32[]{:S(2)}, u32[]{:S(2)}) collective-permute-start(bf16[64,3584]{1,0:T(8,128)(2,1)S(1)} %get-tuple-element.60), channel_id=1, source_target_pairs={{0,1},{1,0},{2,3},{3,2},{4,5},{5,4},{6,7},{7,6},{8,9},{9,8},{10,11... | collective-permute-start | bytes 1376264 | tf_op jit(solution)/shard_map/ppermute | solution.py:21
  77.6 6.1 %collective-permute-start.23 = (bf16[32,3584]{1,0:T(8,128)(2,1)S(1)}, bf16[32,3584]{1,0:T(8,128)(2,1)S(1)}, u32[]{:S(2)}, u32[]{:S(2)}) collective-permute-start(bf16[32,3584]{1,0:T(8,128)(2,1)S(1)} %get-tuple-element.61), channel_id=1, source_target_pairs={{0,2},{1,5},{2,0},{3,7},{4,6},{5,1},{6,4},{7,3},{8,10},{9,13},{10,... | collective-permute-start | bytes 688136 | tf_op jit(solution)/shard_map/ppermute | solution.py:21
  84.4 20.4 %collective-permute-start.25 = (bf16[64,3584]{1,0:T(8,128)(2,1)S(1)}, bf16[64,3584]{1,0:T(8,128)(2,1)S(1)}, u32[]{:S(2)}, u32[]{:S(2)}) collective-permute-start(bf16[64,3584]{1,0:T(8,128)(2,1)S(1)} %get-tuple-element.65), channel_id=1, source_target_pairs={{0,4},{1,3},{2,6},{3,1},{4,0},{5,7},{6,2},{7,5},{8,12},{9,11},{10,... | collective-permute-start | bytes 1376264 | tf_op jit(solution)/shard_map/ppermute | solution.py:21
  85.1 8.5 %collective-permute-start.28 = (bf16[32,3584]{1,0:T(8,128)(2,1)S(1)}, bf16[32,3584]{1,0:T(8,128)(2,1)S(1)}, u32[]{:S(2)}, u32[]{:S(2)}) collective-permute-start(bf16[32,3584]{1,0:T(8,128)(2,1)S(1)} %get-tuple-element.66), channel_id=1, source_target_pairs={{0,2},{1,5},{2,0},{3,7},{4,6},{5,1},{6,4},{7,3},{8,10},{9,13},{10,... | collective-permute-start | bytes 688136 | tf_op jit(solution)/shard_map/ppermute | solution.py:21
  86.5 18.3 %collective-permute-start.26 = (bf16[32,3584]{1,0:T(8,128)(2,1)S(1)}, bf16[32,3584]{1,0:T(8,128)(2,1)S(1)}, u32[]{:S(2)}, u32[]{:S(2)}) collective-permute-start(bf16[32,3584]{1,0:T(8,128)(2,1)S(1)} %leave.3.refs_6_), channel_id=1, source_target_pairs={{0,16},{1,17},{2,18},{3,19},{4,20},{5,21},{6,22},{7,23},{8,24},{9,... | collective-permute-start | bytes 688136 | tf_op jit(solution)/shard_map/ppermute | solution.py:21
  88.1 16.7 %collective-permute-start.27 = (bf16[32,3584]{1,0:T(8,128)(2,1)S(1)}, bf16[32,3584]{1,0:T(8,128)(2,1)S(1)}, u32[]{:S(2)}, u32[]{:S(2)}) collective-permute-start(bf16[32,3584]{1,0:T(8,128)(2,1)S(1)} %leave.4.refs_6_), channel_id=1, source_target_pairs={{0,8},{1,9},{2,10},{3,11},{4,12},{5,13},{6,14},{7,15},{8,0},{9,1},... | collective-permute-start | bytes 688136 | tf_op jit(solution)/shard_map/ppermute | solution.py:21
  93.7 11.9 %collective-permute-start.30 = (bf16[32,3584]{1,0:T(8,128)(2,1)S(1)}, bf16[32,3584]{1,0:T(8,128)(2,1)S(1)}, u32[]{:S(2)}, u32[]{:S(2)}) collective-permute-start(bf16[32,3584]{1,0:T(8,128)(2,1)S(1)} %leave.5.refs_4_), channel_id=1, source_target_pairs={{0,24},{1,25},{2,26},{3,27},{4,28},{5,29},{6,30},{7,31},{8,16},{9,... | collective-permute-start | bytes 688136 | tf_op jit(solution)/shard_map/ppermute | solution.py:21
  105.0 6.1 %collective-permute-start.29 = (bf16[32,3584]{1,0:T(8,128)(2,1)S(1)}, bf16[32,3584]{1,0:T(8,128)(2,1)S(1)}, u32[]{:S(2)}, u32[]{:S(2)}) collective-permute-start(bf16[32,3584]{1,0:T(8,128)(2,1)S(1)} %get-tuple-element.68), channel_id=1, source_target_pairs={{0,2},{1,5},{2,0},{3,7},{4,6},{5,1},{6,4},{7,3},{8,10},{9,13},{10,... | collective-permute-start | bytes 688136 | tf_op jit(solution)/shard_map/ppermute | solution.py:21

commit v3 on v2

v3 whole, which is shorter than its diff:
```python
import functools

import jax
import jax.numpy as jnp
from jax import lax
from jax.experimental import pallas as pl
from jax.experimental.pallas import tpu as pltpu
from jax.sharding import PartitionSpec as P

AXIS = "ep"
GROUP = 8
WHOLE = pl.BlockSpec(memory_space=pltpu.VMEM)
ANYWHERE = pl.BlockSpec(memory_space=pl.ANY)
SCALAR = pl.BlockSpec(memory_space=pltpu.SMEM)
F32, BF16 = jnp.float32, jnp.bfloat16


def swap(block, mask_even, mask_odd):
    count = lax.axis_size(AXIS)
    route = [(i, i ^ (mask_odd if i & 1 else mask_even)) for i in range(count)]
    return lax.ppermute(block, AXIS, route)


def first_hop(block):
    return swap(block, 2, 4)


def second_hop(block):
    return swap(block, 4, 2)


def across(block, k):
    return swap(block, GROUP * k, GROUP * k)


def other_core(block):
    return swap(block, 1, 1)


def far_off(array):
    return pltpu.with_memory_space_constraint(array, pltpu.HBM)


def near(array):
    return pltpu.with_memory_space_constraint(array, pltpu.VMEM)


ORDER = (
    "E0", "K0", "L0", "E1", "E2", "K1", "S0", "K2", "E3", "D0:w1", "K3:w0", "D1:w0", "D2", "X1",
    "D3", "X3", "X2", "C0", "C1", "X0", "M0", "C2:w2", "V0:w2:h2", "M1:w0", "C3:h0", "M2", "V1",
    "M3:g0", "V2:w3", "V3:w3",
)
GATHER_GROUPS = ((0,), (1,), (2,), (3,))
REDUCE_GROUPS = ((3,), (2,), (1,), (0,))


def any_groups(planes):
    gather = tuple((k,) for k in range(planes))
    reduce = tuple((k,) for k in reversed(range(planes)))
    steps = ["E0", "K0", "L0"]
    for k in range(1, planes):
        steps += [f"E{k}", f"K{k}"]
    steps += ["S0"]
    for i, (k,) in enumerate(reduce):
        steps += [f"D{k}", f"X{k}", f"C{i}", f"M{i}", f"V{i}"]
    return gather, reduce, steps


class Line:
    def __init__(self):
        self.last = []
        self.also = []

    def __call__(self, kernel, name, outs, scalars, arrays, scratch=(), alias=None, stored=(), inside=True, mib=8):
        count, waits = len(scalars) + len(arrays) + len(stored), len(self.last) + len(self.also)

        def body(*refs):
            kernel(*refs[:count], *refs[count + waits :])

        result = pl.pallas_call(
            body,
            in_specs=[SCALAR] * len(scalars) + [WHOLE] * len(arrays) + [ANYWHERE] * (len(stored) + waits),
            out_specs=[WHOLE] * len(outs),
            out_shape=[(pltpu.VMEM if inside else jax.ShapeDtypeStruct)(shape, dtype) for shape, dtype in outs],
            scratch_shapes=scratch,
            input_output_aliases=alias or {},
            compiler_params=pltpu.CompilerParams(vmem_limit_bytes=mib * 1024 * 1024),
            cost_estimate=pl.CostEstimate(flops=1, bytes_accessed=1, transcendentals=0),
            name=name,
        )(*scalars, *[near(a) for a in arrays], *[far_off(a) for a in stored], *self.last, *self.also)
        self.last, self.also = [result[0]], []
        return result


def own_kernel(sizes, me_ref, tokens_ref, ids_ref, weights_ref, own_ref, held, ids_held, weights_held, sems):
    width, row_count, experts = sizes
    extra = own_ref.shape[1] - width
    pairs = ((ids_ref, ids_held), (weights_ref, weights_held), (tokens_ref, held))
    copies = [pltpu.make_async_copy(source, target, sems.at[i]) for i, (source, target) in enumerate(pairs)]
    for copy in copies:
        copy.start()
    column = lax.broadcasted_iota(jnp.int32, (extra, row_count), 0)
    row = lax.broadcasted_iota(jnp.int32, (row_count, row_count), 0)
    other = lax.broadcasted_iota(jnp.int32, (row_count, row_count), 1)
    earlier = jnp.where(row < other, 1.0, 0.0).astype(BF16)
    same = jnp.where(row == other, 1.0, 0.0).astype(BF16)
    copies[0].wait()
    copies[1].wait()
    for s in range(held.shape[0]):
        present = jnp.zeros((extra, row_count), F32)
        weight = jnp.zeros((extra, row_count), F32)
        for k in range(ids_held.shape[1]):
            named = lax.rem(column, experts) == ids_held[s, k : k + 1, :]
            present = jnp.where(named, 1.0, present)
            weight = jnp.where(named, weights_held[s, k : k + 1, :], weight)
        before = jnp.dot(present.astype(BF16), earlier, preferred_element_type=F32)
        slot = jnp.where(present > 0.0, before, -1.0)
        high = weight.astype(BF16).astype(F32)
        value = jnp.where(column < experts, slot, jnp.where(column < 2 * experts, high, weight - high))
        turned = lax.dot_general(
            same, value.astype(BF16), (((1,), (1,)), ((), ())), preferred_element_type=F32
        )
        own_ref[s * row_count : (s + 1) * row_count, width:] = turned.astype(BF16)
    copies[2].wait()
    for s in range(held.shape[0]):
        own_ref[s * row_count : (s + 1) * row_count, :width] = held[s]


def loading(weights_ref, held_ref, sems):
    pieces = sems.shape[0]
    rows = weights_ref.shape[1] // pieces
    copies = []
    for i in range(pieces):
        part = (slice(None), pl.ds(i * rows, rows))
        copies.append(pltpu.make_async_copy(weights_ref.at[part], held_ref.at[part], sems.at[i]))
    return copies


def load_kernel(weights_ref, held_ref, sems):
    copies = loading(weights_ref, held_ref, sems)
    for copy in copies:
        copy.start()
    for copy in copies:
        copy.wait()


def pick(columns, lane_index):
    lane = lax.broadcasted_iota(jnp.int32, columns.shape, 1)
    return jnp.sum(jnp.where(lane == lane_index, columns, 0.0), axis=1, keepdims=True)


def placing(columns, expert, first_row, slots, row_count, capacity):
    rows = columns.shape[0]
    slot = pick(columns, expert).astype(jnp.int32)
    row = lax.broadcasted_iota(jnp.int32, (rows, 1), 0) + first_row
    target = jnp.where(slot >= 0, row // row_count * capacity + slot, -1)
    lane = lax.broadcasted_iota(jnp.int32, (rows, slots), 1)
    return jnp.where(lane == target, 1.0, 0.0).astype(BF16)


def gate_kernel(given_ref, out_ref):
    pass


def pack_kernel(*refs):
    *parts, out = refs
    start = 0
    for part in parts:
        rows = part.shape[0]
        out[start : start + rows, :] = part[...]
        start += rows


def dispatch_kernel(sizes, me_ref, *refs):
    (width, row_count, capacity, block), places = sizes
    *refs, own_ref, other_ref = refs
    parts = [(refs[i // 2], at) for i, at in enumerate(places)]
    slots = own_ref.shape[0]
    quarter = slots // 4
    for out, expert in ((own_ref, me_ref[0]), (other_ref, me_ref[0] ^ 1)):
        place = [
            placing(ref[at : at + block, width:].astype(F32), expert, 0, 128, row_count, capacity) for ref, at in parts
        ]
        place = jnp.concatenate(place, axis=0).T
        for i, (ref, at) in enumerate(parts):
            out[i * quarter : (i + 1) * quarter, :] = jnp.dot(
                place[:quarter, i * block : (i + 1) * block], ref[at : at + block, :], preferred_element_type=F32
            ).astype(BF16)


def expert_kernel(experts, me_ref, own_ref, got_ref, gate_ref, up_ref, down_ref, *refs):
    if len(refs) > 4:
        mine_ref, sent_ref, held_ref, rows_ref, hidden, sems = refs
        copies = loading(down_ref, held_ref, sems)
        down_ref = held_ref
    else:
        mine_ref, sent_ref, rows_ref, hidden = refs
        copies = []
    for copy in copies:
        copy.start()
    _, width, units = gate_ref.shape
    slots = own_ref.shape[0]
    rows_ref[:slots, :] = own_ref[...]
    rows_ref[slots:, :] = got_ref[...]
    columns = rows_ref[:, width:].astype(F32)
    weight = pick(columns, me_ref[0] + experts) + pick(columns, me_ref[0] + 2 * experts)
    tile = 256
    for j in range(0, units, tile):
        rows = rows_ref[:, :width]
        gate_val = jnp.dot(rows, gate_ref[0, :, j : j + tile], preferred_element_type=F32)
        up_val = jnp.dot(rows, up_ref[0, :, j : j + tile], preferred_element_type=F32)
        hidden[:, j : j + tile] = (gate_val / (1.0 + jnp.exp(-gate_val)) * up_val).astype(BF16)
    for copy in copies:
        copy.wait()
    tile = 512
    for n in range(0, width, tile):
        value = jnp.dot(hidden[...], down_ref[0, :, n : n + tile], preferred_element_type=F32)
        value = (value * weight).astype(BF16)
        mine_ref[:, n : n + tile] = value[:slots]
        sent_ref[:, n : n + tile] = value[slots:]


def shared_kernel(sizes, *refs):
    (width, _, _, block), places = sizes
    *refs, first_ref, second_ref, up_ref, out_ref, held_ref, rows_ref, sems = refs
    copies = loading(up_ref, held_ref, sems)
    for copy in copies:
        copy.start()
    for i, at in enumerate(places):
        ref = refs[i // 2]
        rows_ref[i * block : (i + 1) * block, :] = ref[at : at + block, :width]
    hidden = []
    for part in (first_ref, second_ref):
        gate_val = jnp.dot(rows_ref[...], part[0], preferred_element_type=F32)
        up_val = jnp.dot(rows_ref[...], part[1], preferred_element_type=F32)
        hidden.append((gate_val / (1.0 + jnp.exp(-gate_val)) * up_val).astype(BF16))
    tile = 512
    for n in range(0, width, tile):
        value = 0.0
        for h, part in zip(hidden, (first_ref, second_ref)):
            value += lax.dot_general(
                h, part[2, n : n + tile, :], (((1,), (1,)), ((), ())), preferred_element_type=F32
            )
        out_ref[:, n : n + tile] = value
    for copy in copies:
        copy.wait()


def combine_kernel(sizes, me_ref, *refs):
    (width, row_count, capacity, block), all_places, shared_at = sizes
    *refs, keep_ref, send_ref = refs
    count = len(all_places)
    tile = 512
    for c, places in enumerate(all_places):
        *parts, mine_ref, back_ref = refs[4 * c : 4 * c + 4]
        quarter = mine_ref.shape[0] // 4
        for i, at in enumerate(places):
            columns = parts[i // 2][at : at + block, width:].astype(F32)
            here = [placing(columns, e, 0, quarter, row_count, capacity) for e in (me_ref[0], me_ref[0] ^ 1)]
            out = (keep_ref, send_ref)[i // 2]
            first = (i % 2 * count + c) * block
            for n in range(0, width, tile):
                value = sum(
                    jnp.dot(p, part[i * quarter : (i + 1) * quarter, n : n + tile], preferred_element_type=F32)
                    for p, part in zip(here, (mine_ref, back_ref))
                )
                if c == shared_at:
                    value += refs[-1][i * block : (i + 1) * block, n : n + tile]
                out[first : first + block, n : n + tile] = value.astype(out.dtype)


def middle_kernel(keep_ref, got_ref, rest_ref, send_ref):
    half = rest_ref.shape[0]
    rest_ref[...] = keep_ref[:half, :] + got_ref[:half, :].astype(F32)
    send_ref[...] = (keep_ref[half:, :] + got_ref[half:, :].astype(F32)).astype(BF16)


def sum_kernel(pieces, *refs):
    *parts, out = refs
    rows = out.shape[0] // len(pieces) if out.ndim == 2 else out.shape[0] * out.shape[1]
    for i, piece in enumerate(pieces):
        total = sum(parts[p][at : at + rows, :].astype(F32) for p, at in piece).astype(BF16)
        if out.ndim == 2:
            out[i * rows : (i + 1) * rows, :] = total
        else:
            out[...] = total.reshape(out.shape)


def shards(tokens, expert_ids, combine_weights, w_gate, w_up, w_down, shared_weights):
    step_count, row_count, width = tokens.shape
    top_count = expert_ids.shape[2]
    devices = lax.axis_size(AXIS)
    experts = w_gate.shape[0] * devices
    capacity = max(2, row_count * top_count * 2 // experts)
    planes = devices // GROUP
    units = w_gate.shape[2]
    index = lax.axis_index(AXIS)[None].astype(jnp.int32)
    block = step_count * row_count
    rows = GROUP // 2 * block
    slots = rows // row_count * capacity
    full = width + (3 * experts + 127) // 128 * 128
    sizes = (width, row_count, capacity, block)
    line = Line()

    turned_shape = (step_count, top_count, row_count)
    own, = line(
        functools.partial(own_kernel, (width, row_count, experts)),
        "own",
        [((block, full), BF16)],
        [index],
        [],
        stored=[tokens, expert_ids.transpose(0, 2, 1), combine_weights.transpose(0, 2, 1)],
        scratch=[
            pltpu.VMEM(tokens.shape, BF16),
            pltpu.VMEM(turned_shape, jnp.int32),
            pltpu.VMEM(turned_shape, F32),
            pltpu.SemaphoreType.DMA((3,)),
        ],
    )
    shared_other = other_core(shared_weights)
    gather_groups, reduce_groups, order = (GATHER_GROUPS, REDUCE_GROUPS, ORDER) if planes == 4 else any_groups(planes)
    home = {k: (g, i, len(group)) for g, group in enumerate(gather_groups) for i, k in enumerate(group)}
    paired = any(1 in group and 3 in group for group in gather_groups)
    far = {0: own}
    for k in range(2, planes, 2):
        far[k] = across(own, k)
    if not paired:
        far[1] = across(own, 1)
    held = {}
    hop, wide, leaving, chosen, mine, back, got, rest, last, arrived, packed, kept = ({} for _ in range(12))

    def load(name, weights):
        held[name], = line(
            load_kernel,
            "load",
            [(weights.shape, BF16)],
            [],
            [],
            stored=[weights],
            scratch=[pltpu.SemaphoreType.DMA((4,))],
        )

    def enter(g):
        group = gather_groups[g]
        if paired and 1 in group:
            near_far, = line(pack_kernel, "pack", [((2 * block, full), BF16)], [], [own, far[2]])
            packed[g] = across(near_far, 1)
            packed[g], = line(gate_kernel, "enter", [(packed[g].shape, BF16)], [], [packed[g]], alias={0: 0})
        elif len(group) > 1:
            packed[g], = line(
                pack_kernel, "pack", [((len(group) * block, full), BF16)], [], [far[k] for k in group]
            )
        elif group[0] > 0:
            k = group[0]
            packed[g], = line(gate_kernel, "enter", [((block, full), BF16)], [], [far[k]], alias={0: 0})
            far[k] = packed[g]
        else:
            packed[g] = own
        for k in group:
            if not paired and k >= 2 and k & 1 == 0:
                far[k + 1] = across(far[k], 1)
        hop[g] = first_hop(packed[g])

    def pack(g):
        count = 2 * len(gather_groups[g])
        packed[g], = line(pack_kernel, "pack", [((count * block, full), BF16)], [], [packed[g], hop[g]])
        wide[g] = second_hop(packed[g])

    def blocks(k):
        g, i, n = home[k]
        places = (i * block, (n + i) * block)
        return [packed[g], wide[g]], places * 2

    def dispatch(k):
        arrays, places = blocks(k)
        chosen[k], out = line(
            functools.partial(dispatch_kernel, (sizes, places)),
            "dispatch",
            [((slots, full), BF16)] * 2,
            [index],
            arrays,
        )
        leaving[k] = other_core(out)

    def expert(k):
        loads_down = "down" not in held
        arrays = [chosen[k], leaving[k], held["gate"], held["up"]]
        mine[k], out, *brought = line(
            functools.partial(expert_kernel, experts),
            "expert_load" if loads_down else "expert",
            [((slots, width), BF16)] * 2 + [(w_down.shape, BF16)] * loads_down,
            [index],
            arrays if loads_down else arrays + [held["down"]],
            stored=[w_down] if loads_down else [],
            scratch=[pltpu.VMEM((2 * slots, full), BF16), pltpu.VMEM((2 * slots, units), BF16)]
            + [pltpu.SemaphoreType.DMA((4,))] * loads_down,
        )
        if loads_down:
            held["down"], = brought
        back[k] = other_core(out)

    def shared():
        arrays, places = blocks(0)
        kept["shared"], held["up"] = line(
            functools.partial(shared_kernel, (sizes, places)),
            "shared",
            [((rows, width), F32), (w_up.shape, BF16)],
            [],
            [*arrays, shared_weights, shared_other],
            stored=[w_up],
            scratch=[pltpu.VMEM((rows, width), BF16), pltpu.SemaphoreType.DMA((4,))],
        )

    def combine(r):
        group = reduce_groups[r]
        arrays, all_places = [], []
        for k in group:
            pair, places = blocks(k)
            arrays += [*pair, mine[k], back[k]]
            all_places.append(places)
        shared_at = group.index(0) if 0 in group else -1
        if 0 in group:
            arrays.append(kept["shared"])
        half = 2 * block * len(group)
        kept[r], send = line(
            functools.partial(combine_kernel, (sizes, all_places, shared_at)),
            f"combine{len(group)}",
            [((half, width), F32), ((half, width), BF16)],
            [index],
            arrays,
        )
        got[r] = second_hop(send)

    def middle(r):
        half = block * len(reduce_groups[r])
        rest[r], send = line(
            middle_kernel, "middle", [((half, width), F32), ((half, width), BF16)], [], [kept[r], got[r]]
        )
        last[r] = first_hop(send)

    def leave(r):
        group = reduce_groups[r]
        for k in group:
            if k == 0 or (k == 3 and 1 in group):
                continue
            both = [k, 3] if k == 1 and 3 in group else [k]
            arrays, pieces = [rest[r], last[r]], []
            for j in both:
                at = group.index(j) * block
                pieces.append([(0, at), (1, at)])
            if k >= 2 and k & 1 == 0:
                array, at = arrived.pop(k + 1)
                arrays.append(array)
                pieces[0].append((2, at))
            out, = line(
                functools.partial(sum_kernel, pieces), "leave", [((len(both) * block, width), BF16)], [], arrays
            )
            out = across(out, 1 if k & 1 else k)
            for i, j in enumerate(both):
                arrived[j] = (out, i * block)

    def final():
        r = [r for r, group in enumerate(reduce_groups) if 0 in group][0]
        at = reduce_groups[r].index(0) * block
        arrays, pieces = [rest[r], last[r]], [(0, at), (1, at)]
        for array, at in arrived.values():
            pieces.append((len(arrays), at))
            arrays.append(array)
        out, = line(
            functools.partial(sum_kernel, [pieces]),
            "final",
            [((step_count, row_count, width), BF16)],
            [],
            arrays,
            inside=False,
        )
        return out

    steps = {
        "E": enter,
        "K": pack,
        "L": lambda i: load("gate", w_gate),
        "D": dispatch,
        "X": expert,
        "S": lambda i: shared(),
        "C": combine,
        "M": middle,
        "V": leave,
    }
    stores = {"h": hop, "w": wide, "c": leaving, "b": back, "g": got, "l": last}
    for step in order:
        step, *also = step.split(":")
        line.also = [stores[name[0]][int(name[1:])] for name in also]
        steps[step[0]](int(step[1:]))
    return final()


def solution(mesh):
    placed = (
        P(None, AXIS, None),
        P(None, AXIS, None),
        P(None, AXIS, None),
        P(AXIS, None, None),
        P(AXIS, None, None),
        P(AXIS, None, None),
        P(None, None, AXIS),
    )
    return jax.shard_map(
        shards, mesh=mesh, in_specs=placed, out_specs=P(None, AXIS, None), check_vma=False
    )
```

time: 112 us -> 99.4 us (0.89)
  starting transfers between devices: 32.9 us -> 27.4 us
  waiting for transfers between devices: 43.7 us -> 40.7 us
  Pallas kernels: 33.4 us -> 30.8 us
  other arithmetic: 1.4 us -> 0 us
    ppermute x31, starting transfers between devices: 32.9 us -> 27.4 us  [swap(): return lax.ppermute(block, AXIS, route)]
    ppermute x31, waiting for transfers between devices: 43.7 us -> 40.7 us  [swap(): return lax.ppermute(block, AXIS, route)]
    pallas_call x32 -> x30, Pallas kernels: 33.4 us -> 30.8 us  [__call__(): pl.pallas_call(body, in_specs=[SCALAR] * len(scalars) + [WHOLE] * len(arr...]
  transfers between devices with their start and end apart: 31 -> 31, of which waited for: 13 -> 15; matrix products, arithmetic and copies ran while one was open for 0% -> 0% of each run, Pallas kernels for 28% -> 30%
where the time goes in v3:
time: 99.4 us; the launch traced here: 99.2 us
  waiting for transfers between devices  40.7 us (41%)
  Pallas kernels  30.8 us (31%)
  starting transfers between devices  27.4 us (28%)
    ppermute x31, waiting for transfers between devices, swap(): return lax.ppermute(block, AXIS, route)  40.7 us
    pallas_call x30, Pallas kernels, __call__(): pl.pallas_call(body, in_specs=[SCALAR] * len(scalars) + [WHOLE] * len(arr...  30.8 us
    ppermute x31, starting transfers between devices, swap(): return lax.ppermute(block, AXIS, route)  27.4 us
  transfers between devices with their start and end apart: 31, of which 15 were waited for; matrix products, arithmetic and copies ran while one was open for 0% of the time, Pallas kernels for 30%

profile of v3, /device:TPU:0, one launch (start us, length us, event | category | flops | bytes accessed | tf_op | source)
XLA Modules:
  0.0 99.2 jit_solution(13341135078290597142)
XLA Ops:
  0.5 1.1 %own.1.refs_0_.refs_2_ = bf16[32,3712]{1,0:T(8,128)(2,1)S(1)} custom-call(s32[1]{0:T(128)} %bitcast.refs_0_, bf16[2,16,3584]{2,1,0:T(8,128)(2,1)} %refs_1_.1, s32[2,8,16]{2,1,0:T(8,128)} %bitcast.3, f32[2,8,16]{2,1,0:T(8,128)} %bitcast.4), custom_call_target="tpu_custom_call" | custom-call | flops 1 | bytes 1 | tf_op jit(solution)/shard_map/own/pallas_call | solution.py:80
  1.5 2.6 %collective-permute-start = (bf16[32,3712]{1,0:T(8,128)(2,1)S(1)}, bf16[32,3712]{1,0:T(8,128)(2,1)S(1)}, u32[]{:S(2)}, u32[]{:S(2)}) collective-permute-start(bf16[32,3712]{1,0:T(8,128)(2,1)S(1)} %own.1.refs_0_.refs_2_), channel_id=1, source_target_pairs={{0,2},{1,5},{2,0},{3,7},{4,6},{5,1},{6,4},{7,3},{8,10},{9,13},{10,... | collective-permute-start | bytes 712712 | tf_op jit(solution)/shard_map/ppermute | solution.py:21
  4.1 1.6 %collective-permute-start.3 = (bf16[32,3712]{1,0:T(8,128)(2,1)S(1)}, bf16[32,3712]{1,0:T(8,128)(2,1)S(1)}, u32[]{:S(2)}, u32[]{:S(2)}) collective-permute-start(bf16[32,3712]{1,0:T(8,128)(2,1)S(1)} %own.1.refs_0_.refs_2_), channel_id=1, source_target_pairs={{0,8},{1,9},{2,10},{3,11},{4,12},{5,13},{6,14},{7,15},{8,0},{9,1},... | collective-permute-start | bytes 712712 | tf_op jit(solution)/shard_map/ppermute | solution.py:21
  5.6 2.6 %collective-permute-start.2 = (bf16[32,3712]{1,0:T(8,128)(2,1)S(1)}, bf16[32,3712]{1,0:T(8,128)(2,1)S(1)}, u32[]{:S(2)}, u32[]{:S(2)}) collective-permute-start(bf16[32,3712]{1,0:T(8,128)(2,1)S(1)} %own.1.refs_0_.refs_2_), channel_id=1, source_target_pairs={{0,16},{1,17},{2,18},{3,19},{4,20},{5,21},{6,22},{7,23},{8,24},{9,... | collective-permute-start | bytes 712712 | tf_op jit(solution)/shard_map/ppermute | solution.py:21
  8.3 2.0 %collective-permute-start.1 = (bf16[64,3712]{1,0:T(8,128)(2,1)S(1)}, bf16[64,3712]{1,0:T(8,128)(2,1)S(1)}, u32[]{:S(2)}, u32[]{:S(2)}) collective-permute-start(bf16[64,3712]{1,0:T(8,128)(2,1)S(1)} %pack.4.refs_1_.refs_0_), channel_id=1, source_target_pairs={{0,4},{1,3},{2,6},{3,1},{4,0},{5,7},{6,2},{7,5},{8,12},{9,11},{10,... | collective-permute-start | bytes 1425416 | tf_op jit(solution)/shard_map/ppermute | solution.py:21
  10.3 3.2 %load.1.refs_1_.refs_3_ = bf16[1,3584,1024]{2,1,0:T(8,128)(2,1)S(1)} custom-call(bf16[1,3584,1024]{2,1,0:T(8,128)(2,1)} %refs_0_.1, bf16[64,3712]{1,0:T(8,128)(2,1)S(1)} %pack.4.refs_1_.refs_0_), custom_call_target="tpu_custom_call" | custom-call | flops 1 | bytes 1 | tf_op jit(solution)/shard_map/load/pallas_call | solution.py:80
  13.5 3.5 %collective-permute-done.3.refs_0_ = bf16[32,3712]{1,0:T(8,128)(2,1)S(1)} collective-permute-done((bf16[32,3712]{1,0:T(8,128)(2,1)S(1)}, bf16[32,3712]{1,0:T(8,128)(2,1)S(1)}, u32[]{:S(2)}, u32[]{:S(2)}) %collective-permute-start.3) | collective-permute-done | bytes 237600 | tf_op jit(solution)/shard_map/ppermute | solution.py:21
  17.0 2.4 %collective-permute-done.2.refs_0_ = bf16[32,3712]{1,0:T(8,128)(2,1)S(1)} collective-permute-done((bf16[32,3712]{1,0:T(8,128)(2,1)S(1)}, bf16[32,3712]{1,0:T(8,128)(2,1)S(1)}, u32[]{:S(2)}, u32[]{:S(2)}) %collective-permute-start.2) | collective-permute-done | bytes 237600 | tf_op jit(solution)/shard_map/ppermute | solution.py:21
  19.3 1.5 %collective-permute-start.5 = (bf16[32,3712]{1,0:T(8,128)(2,1)S(1)}, bf16[32,3712]{1,0:T(8,128)(2,1)S(1)}, u32[]{:S(2)}, u32[]{:S(2)}) collective-permute-start(bf16[32,3712]{1,0:T(8,128)(2,1)S(1)} %enter.4.refs_2_.refs_0_), channel_id=1, source_target_pairs={{0,2},{1,5},{2,0},{3,7},{4,6},{5,1},{6,4},{7,3},{8,10},{9,13},{10,... | collective-permute-start | bytes 712712 | tf_op jit(solution)/shard_map/ppermute | solution.py:21
  20.8 2.3 %collective-permute-done.7.refs_1_ = bf16[32,3712]{1,0:T(8,128)(2,1)S(1)} collective-permute-done((bf16[32,3712]{1,0:T(8,128)(2,1)S(1)}, bf16[32,3712]{1,0:T(8,128)(2,1)S(1)}, u32[]{:S(2)}, u32[]{:S(2)}) %collective-permute-start.7) | collective-permute-done | bytes 237600 | tf_op jit(solution)/shard_map/ppermute | solution.py:21
  23.6 3.4 %shared.1 = (f32[128,3584]{1,0:T(8,128)S(1)}, bf16[1,3584,1024]{2,1,0:T(8,128)(2,1)S(1)}) custom-call(bf16[64,3712]{1,0:T(8,128)(2,1)S(1)} %pack.4.refs_1_.refs_0_, bf16[64,3712]{1,0:T(8,128)(2,1)S(1)} %collective-permute-done.1.refs_1_.refs_2_.refs_3_.refs_4_, bf16[3,3584,128]{2,1,0:T(8,128)(2,1)S(1)} %copy-done, ...), custom_call_target="tpu_custom_call" | custom-call | flops 1 | bytes 1 | tf_op jit(solution)/shard_map/shared/pallas_call | solution.py:80
  27.1 1.7 %collective-permute-start.10 = (bf16[32,3712]{1,0:T(8,128)(2,1)S(1)}, bf16[32,3712]{1,0:T(8,128)(2,1)S(1)}, u32[]{:S(2)}, u32[]{:S(2)}) collective-permute-start(bf16[32,3712]{1,0:T(8,128)(2,1)S(1)} %enter.5.refs_3_.refs_0_), channel_id=1, source_target_pairs={{0,2},{1,5},{2,0},{3,7},{4,6},{5,1},{6,4},{7,3},{8,10},{9,13},{10,... | collective-permute-start | bytes 712712 | tf_op jit(solution)/shard_map/ppermute | solution.py:21
  28.8 1.6 %collective-permute-start.12 = (bf16[64,3712]{1,0:T(8,128)(2,1)S(1)}, bf16[64,3712]{1,0:T(8,128)(2,1)S(1)}, u32[]{:S(2)}, u32[]{:S(2)}) collective-permute-start(bf16[64,3712]{1,0:T(8,128)(2,1)S(1)} %pack.6.refs_1_), channel_id=1, source_target_pairs={{0,4},{1,3},{2,6},{3,1},{4,0},{5,7},{6,2},{7,5},{8,12},{9,11},{10,... | collective-permute-start | bytes 1425416 | tf_op jit(solution)/shard_map/ppermute | solution.py:21
  30.3 4.1 %collective-permute-done.8.refs_4_.refs_2_ = bf16[64,3712]{1,0:T(8,128)(2,1)S(1)} collective-permute-done((bf16[64,3712]{1,0:T(8,128)(2,1)S(1)}, bf16[64,3712]{1,0:T(8,128)(2,1)S(1)}, u32[]{:S(2)}, u32[]{:S(2)}) %collective-permute-start.8) | collective-permute-done | bytes 475168 | tf_op jit(solution)/shard_map/ppermute | solution.py:21
  36.5 1.8 %collective-permute-start.14 = (bf16[64,3712]{1,0:T(8,128)(2,1)S(1)}, bf16[64,3712]{1,0:T(8,128)(2,1)S(1)}, u32[]{:S(2)}, u32[]{:S(2)}) collective-permute-start(bf16[64,3712]{1,0:T(8,128)(2,1)S(1)} %pack.7.refs_3_.refs_1_), channel_id=1, source_target_pairs={{0,4},{1,3},{2,6},{3,1},{4,0},{5,7},{6,2},{7,5},{8,12},{9,11},{10,... | collective-permute-start | bytes 1425416 | tf_op jit(solution)/shard_map/ppermute | solution.py:21
  38.4 1.1 %collective-permute-done.12.refs_2_.refs_6_.refs_3_ = bf16[64,3712]{1,0:T(8,128)(2,1)S(1)} collective-permute-done((bf16[64,3712]{1,0:T(8,128)(2,1)S(1)}, bf16[64,3712]{1,0:T(8,128)(2,1)S(1)}, u32[]{:S(2)}, u32[]{:S(2)}) %collective-permute-start.12) | collective-permute-done | bytes 475168 | tf_op jit(solution)/shard_map/ppermute | solution.py:21
  40.2 6.0 %expert_load.1 = (bf16[64,3584]{1,0:T(8,128)(2,1)S(1)}, bf16[64,3584]{1,0:T(8,128)(2,1)S(1)}, bf16[1,1024,3584]{2,1,0:T(8,128)(2,1)S(1)}) custom-call(s32[1]{0:T(128)} %bitcast.refs_0_, bf16[64,3712]{1,0:T(8,128)(2,1)S(1)} %get-tuple-element.44.refs_3_.refs_1_, bf16[64,3712]{1,0:T(8,128)(2,1)S(1)} %collective-permute-done.11.refs_2_, ...), custom_call_target="tpu_custom_call" | custom-call | flops 1 | bytes 1 | tf_op jit(solution)/shard_map/expert_load/pallas_call | solution.py:80
  47.5 1.3 %collective-permute-done.15.refs_2_ = bf16[64,3712]{1,0:T(8,128)(2,1)S(1)} collective-permute-done((bf16[64,3712]{1,0:T(8,128)(2,1)S(1)}, bf16[64,3712]{1,0:T(8,128)(2,1)S(1)}, u32[]{:S(2)}, u32[]{:S(2)}) %collective-permute-start.15) | collective-permute-done | bytes 475168 | tf_op jit(solution)/shard_map/ppermute | solution.py:21
  48.8 3.3 %expert.3 = (bf16[64,3584]{1,0:T(8,128)(2,1)S(1)}, bf16[64,3584]{1,0:T(8,128)(2,1)S(1)}) custom-call(s32[1]{0:T(128)} %bitcast.refs_0_, bf16[64,3712]{1,0:T(8,128)(2,1)S(1)} %get-tuple-element.50.refs_1_.refs_6_, bf16[64,3712]{1,0:T(8,128)(2,1)S(1)} %collective-permute-done.15.refs_2_, bf16[1,3584,1024]{2,1,0:T(8,128)(2,1)S(1)} %load.1.refs_1_.refs_3_, ...), custom_call_target="tpu_custom_call" | custom-call | flops 1 | bytes 1 | tf_op jit(solution)/shard_map/expert/pallas_call | solution.py:80
  52.7 3.5 %expert.4 = (bf16[64,3584]{1,0:T(8,128)(2,1)S(1)}, bf16[64,3584]{1,0:T(8,128)(2,1)S(1)}) custom-call(s32[1]{0:T(128)} %bitcast.refs_0_, bf16[64,3712]{1,0:T(8,128)(2,1)S(1)} %get-tuple-element.46.refs_6_.refs_1_, bf16[64,3712]{1,0:T(8,128)(2,1)S(1)} %collective-permute-done.13.refs_2_, bf16[1,3584,1024]{2,1,0:T(8,128)(2,1)S(1)} %load.1.refs_1_.refs_3_, ...), custom_call_target="tpu_custom_call" | custom-call | flops 1 | bytes 1 | tf_op jit(solution)/shard_map/expert/pallas_call | solution.py:80
  57.1 0.9 collective-permute-start.20
  58.8 1.6 %collective-permute-start.19 = (bf16[64,3584]{1,0:T(8,128)(2,1)S(1)}, bf16[64,3584]{1,0:T(8,128)(2,1)S(1)}, u32[]{:S(2)}, u32[]{:S(2)}) collective-permute-start(bf16[64,3584]{1,0:T(8,128)(2,1)S(1)} %get-tuple-element.60), channel_id=1, source_target_pairs={{0,4},{1,3},{2,6},{3,1},{4,0},{5,7},{6,2},{7,5},{8,12},{9,11},{10,... | collective-permute-start | bytes 1376264 | tf_op jit(solution)/shard_map/ppermute | solution.py:21
  60.4 3.3 %expert.5 = (bf16[64,3584]{1,0:T(8,128)(2,1)S(1)}, bf16[64,3584]{1,0:T(8,128)(2,1)S(1)}) custom-call(s32[1]{0:T(128)} %bitcast.refs_0_, bf16[64,3712]{1,0:T(8,128)(2,1)S(1)} %get-tuple-element.41.refs_2_.refs_1_, bf16[64,3712]{1,0:T(8,128)(2,1)S(1)} %collective-permute-done.9.refs_2_, bf16[1,3584,1024]{2,1,0:T(8,128)(2,1)S(1)} %load.1.refs_1_.refs_3_, ...), custom_call_target="tpu_custom_call" | custom-call | flops 1 | bytes 1 | tf_op jit(solution)/shard_map/expert/pallas_call | solution.py:80
  63.9 1.7 %collective-permute-done.20.refs_1_.refs_3_ = bf16[64,3584]{1,0:T(8,128)(2,1)S(1)} collective-permute-done((bf16[64,3584]{1,0:T(8,128)(2,1)S(1)}, bf16[64,3584]{1,0:T(8,128)(2,1)S(1)}, u32[]{:S(2)}, u32[]{:S(2)}) %collective-permute-start.20) | collective-permute-done | bytes 458784 | tf_op jit(solution)/shard_map/ppermute | solution.py:21
  67.1 1.9 %collective-permute-start.26 = (bf16[64,3584]{1,0:T(8,128)(2,1)S(1)}, bf16[64,3584]{1,0:T(8,128)(2,1)S(1)}, u32[]{:S(2)}, u32[]{:S(2)}) collective-permute-start(bf16[64,3584]{1,0:T(8,128)(2,1)S(1)} %get-tuple-element.70), channel_id=1, source_target_pairs={{0,4},{1,3},{2,6},{3,1},{4,0},{5,7},{6,2},{7,5},{8,12},{9,11},{10,... | collective-permute-start | bytes 1376264 | tf_op jit(solution)/shard_map/ppermute | solution.py:21
  68.9 5.4 %collective-permute-done.21.refs_1_ = bf16[32,3584]{1,0:T(8,128)(2,1)S(1)} collective-permute-done((bf16[32,3584]{1,0:T(8,128)(2,1)S(1)}, bf16[32,3584]{1,0:T(8,128)(2,1)S(1)}, u32[]{:S(2)}, u32[]{:S(2)}) %collective-permute-start.21) | collective-permute-done | bytes 229408 | tf_op jit(solution)/shard_map/ppermute | solution.py:21
  76.1 1.5 %collective-permute-start.24 = (bf16[32,3584]{1,0:T(8,128)(2,1)S(1)}, bf16[32,3584]{1,0:T(8,128)(2,1)S(1)}, u32[]{:S(2)}, u32[]{:S(2)}) collective-permute-start(bf16[32,3584]{1,0:T(8,128)(2,1)S(1)} %get-tuple-element.69), channel_id=1, source_target_pairs={{0,2},{1,5},{2,0},{3,7},{4,6},{5,1},{6,4},{7,3},{8,10},{9,13},{10,... | collective-permute-start | bytes 688136 | tf_op jit(solution)/shard_map/ppermute | solution.py:21
  78.0 1.0 %collective-permute-done.26.refs_1_ = bf16[64,3584]{1,0:T(8,128)(2,1)S(1)} collective-permute-done((bf16[64,3584]{1,0:T(8,128)(2,1)S(1)}, bf16[64,3584]{1,0:T(8,128)(2,1)S(1)}, u32[]{:S(2)}, u32[]{:S(2)}) %collective-permute-start.26) | collective-permute-done | bytes 458784 | tf_op jit(solution)/shard_map/ppermute | solution.py:21
  79.1 5.5 %collective-permute-done.24.refs_1_ = bf16[32,3584]{1,0:T(8,128)(2,1)S(1)} collective-permute-done((bf16[32,3584]{1,0:T(8,128)(2,1)S(1)}, bf16[32,3584]{1,0:T(8,128)(2,1)S(1)}, u32[]{:S(2)}, u32[]{:S(2)}) %collective-permute-start.24) | collective-permute-done | bytes 229408 | tf_op jit(solution)/shard_map/ppermute | solution.py:21
  85.5 2.3 %collective-permute-done.23.refs_1_ = bf16[64,3584]{1,0:T(8,128)(2,1)S(1)} collective-permute-done((bf16[64,3584]{1,0:T(8,128)(2,1)S(1)}, bf16[64,3584]{1,0:T(8,128)(2,1)S(1)}, u32[]{:S(2)}, u32[]{:S(2)}) %collective-permute-start.23) | collective-permute-done | bytes 458784 | tf_op jit(solution)/shard_map/ppermute | solution.py:21
  89.0 6.4 %collective-permute-done.28.refs_2_ = bf16[32,3584]{1,0:T(8,128)(2,1)S(1)} collective-permute-done((bf16[32,3584]{1,0:T(8,128)(2,1)S(1)}, bf16[32,3584]{1,0:T(8,128)(2,1)S(1)}, u32[]{:S(2)}, u32[]{:S(2)}) %collective-permute-start.28) | collective-permute-done | bytes 229408 | tf_op jit(solution)/shard_map/ppermute | solution.py:21
  95.5 2.9 %collective-permute-done.30.refs_3_ = bf16[32,3584]{1,0:T(8,128)(2,1)S(1)} collective-permute-done((bf16[32,3584]{1,0:T(8,128)(2,1)S(1)}, bf16[32,3584]{1,0:T(8,128)(2,1)S(1)}, u32[]{:S(2)}, u32[]{:S(2)}) %collective-permute-start.30) | collective-permute-done | bytes 229408 | tf_op jit(solution)/shard_map/ppermute | solution.py:21
  (62 shorter events, 14.0 us)
Async XLA Ops:
  0.0 23.6 %collective-permute-start.6 = (bf16[3,3584,128]{2,1,0:T(8,128)(2,1)}, bf16[3,3584,128]{2,1,0:T(8,128)(2,1)S(1)}, u32[]{:S(2)}, u32[]{:S(2)}) collective-permute-start(bf16[3,3584,128]{2,1,0:T(8,128)(2,1)} %refs_2_.1), channel_id=1, source_target_pairs={{0,1},{1,0},{2,3},{3,2},{4,5},{5,4},{6,7},{7,6},{8,9},{9,8},{10,11... | collective-permute-start | bytes 8257544 | tf_op jit(solution)/shard_map/ppermute | solution.py:21
  1.5 6.7 %collective-permute-start = (bf16[32,3712]{1,0:T(8,128)(2,1)S(1)}, bf16[32,3712]{1,0:T(8,128)(2,1)S(1)}, u32[]{:S(2)}, u32[]{:S(2)}) collective-permute-start(bf16[32,3712]{1,0:T(8,128)(2,1)S(1)} %own.1.refs_0_.refs_2_), channel_id=1, source_target_pairs={{0,2},{1,5},{2,0},{3,7},{4,6},{5,1},{6,4},{7,3},{8,10},{9,13},{10,... | collective-permute-start | bytes 712712 | tf_op jit(solution)/shard_map/ppermute | solution.py:21
  4.1 12.9 %collective-permute-start.3 = (bf16[32,3712]{1,0:T(8,128)(2,1)S(1)}, bf16[32,3712]{1,0:T(8,128)(2,1)S(1)}, u32[]{:S(2)}, u32[]{:S(2)}) collective-permute-start(bf16[32,3712]{1,0:T(8,128)(2,1)S(1)} %own.1.refs_0_.refs_2_), channel_id=1, source_target_pairs={{0,8},{1,9},{2,10},{3,11},{4,12},{5,13},{6,14},{7,15},{8,0},{9,1},... | collective-permute-start | bytes 712712 | tf_op jit(solution)/shard_map/ppermute | solution.py:21
  5.6 13.7 %collective-permute-start.2 = (bf16[32,3712]{1,0:T(8,128)(2,1)S(1)}, bf16[32,3712]{1,0:T(8,128)(2,1)S(1)}, u32[]{:S(2)}, u32[]{:S(2)}) collective-permute-start(bf16[32,3712]{1,0:T(8,128)(2,1)S(1)} %own.1.refs_0_.refs_2_), channel_id=1, source_target_pairs={{0,16},{1,17},{2,18},{3,19},{4,20},{5,21},{6,22},{7,23},{8,24},{9,... | collective-permute-start | bytes 712712 | tf_op jit(solution)/shard_map/ppermute | solution.py:21
  8.3 15.3 %collective-permute-start.1 = (bf16[64,3712]{1,0:T(8,128)(2,1)S(1)}, bf16[64,3712]{1,0:T(8,128)(2,1)S(1)}, u32[]{:S(2)}, u32[]{:S(2)}) collective-permute-start(bf16[64,3712]{1,0:T(8,128)(2,1)S(1)} %pack.4.refs_1_.refs_0_), channel_id=1, source_target_pairs={{0,4},{1,3},{2,6},{3,1},{4,0},{5,7},{6,2},{7,5},{8,12},{9,11},{10,... | collective-permute-start | bytes 1425416 | tf_op jit(solution)/shard_map/ppermute | solution.py:21
  13.5 10.1 %copy-start = (bf16[3,3584,128]{2,1,0:T(8,128)(2,1)S(1)}, bf16[3,3584,128]{2,1,0:T(8,128)(2,1)}, u32[]{:S(2)}) copy-start(bf16[3,3584,128]{2,1,0:T(8,128)(2,1)} %refs_2_.1) | copy-start | bytes 8257540
  17.0 6.1 %collective-permute-start.7 = (bf16[32,3712]{1,0:T(8,128)(2,1)S(1)}, bf16[32,3712]{1,0:T(8,128)(2,1)S(1)}, u32[]{:S(2)}, u32[]{:S(2)}) collective-permute-start(bf16[32,3712]{1,0:T(8,128)(2,1)S(1)} %enter.3.refs_1_.refs_0_), channel_id=1, source_target_pairs={{0,2},{1,5},{2,0},{3,7},{4,6},{5,1},{6,4},{7,3},{8,10},{9,13},{10,... | collective-permute-start | bytes 712712 | tf_op jit(solution)/shard_map/ppermute | solution.py:21
  19.3 7.7 %collective-permute-start.5 = (bf16[32,3712]{1,0:T(8,128)(2,1)S(1)}, bf16[32,3712]{1,0:T(8,128)(2,1)S(1)}, u32[]{:S(2)}, u32[]{:S(2)}) collective-permute-start(bf16[32,3712]{1,0:T(8,128)(2,1)S(1)} %enter.4.refs_2_.refs_0_), channel_id=1, source_target_pairs={{0,2},{1,5},{2,0},{3,7},{4,6},{5,1},{6,4},{7,3},{8,10},{9,13},{10,... | collective-permute-start | bytes 712712 | tf_op jit(solution)/shard_map/ppermute | solution.py:21
  20.8 6.2 %collective-permute-start.4 = (bf16[32,3712]{1,0:T(8,128)(2,1)S(1)}, bf16[32,3712]{1,0:T(8,128)(2,1)S(1)}, u32[]{:S(2)}, u32[]{:S(2)}) collective-permute-start(bf16[32,3712]{1,0:T(8,128)(2,1)S(1)} %enter.4.refs_2_.refs_0_), channel_id=1, source_target_pairs={{0,8},{1,9},{2,10},{3,11},{4,12},{5,13},{6,14},{7,15},{8,0},{9,1},... | collective-permute-start | bytes 712712 | tf_op jit(solution)/shard_map/ppermute | solution.py:21
  23.1 11.3 %collective-permute-start.8 = (bf16[64,3712]{1,0:T(8,128)(2,1)S(1)}, bf16[64,3712]{1,0:T(8,128)(2,1)S(1)}, u32[]{:S(2)}, u32[]{:S(2)}) collective-permute-start(bf16[64,3712]{1,0:T(8,128)(2,1)S(1)} %pack.5.refs_5_.refs_1_), channel_id=1, source_target_pairs={{0,4},{1,3},{2,6},{3,1},{4,0},{5,7},{6,2},{7,5},{8,12},{9,11},{10,... | collective-permute-start | bytes 1425416 | tf_op jit(solution)/shard_map/ppermute | solution.py:21
  27.1 8.7 %collective-permute-start.10 = (bf16[32,3712]{1,0:T(8,128)(2,1)S(1)}, bf16[32,3712]{1,0:T(8,128)(2,1)S(1)}, u32[]{:S(2)}, u32[]{:S(2)}) collective-permute-start(bf16[32,3712]{1,0:T(8,128)(2,1)S(1)} %enter.5.refs_3_.refs_0_), channel_id=1, source_target_pairs={{0,2},{1,5},{2,0},{3,7},{4,6},{5,1},{6,4},{7,3},{8,10},{9,13},{10,... | collective-permute-start | bytes 712712 | tf_op jit(solution)/shard_map/ppermute | solution.py:21
  28.8 10.7 %collective-permute-start.12 = (bf16[64,3712]{1,0:T(8,128)(2,1)S(1)}, bf16[64,3712]{1,0:T(8,128)(2,1)S(1)}, u32[]{:S(2)}, u32[]{:S(2)}) collective-permute-start(bf16[64,3712]{1,0:T(8,128)(2,1)S(1)} %pack.6.refs_1_), channel_id=1, source_target_pairs={{0,4},{1,3},{2,6},{3,1},{4,0},{5,7},{6,2},{7,5},{8,12},{9,11},{10,... | collective-permute-start | bytes 1425416 | tf_op jit(solution)/shard_map/ppermute | solution.py:21
  36.5 3.7 %collective-permute-start.11 = (bf16[64,3712]{1,0:T(8,128)(2,1)S(1)}, bf16[64,3712]{1,0:T(8,128)(2,1)S(1)}, u32[]{:S(2)}, u32[]{:S(2)}) collective-permute-start(bf16[64,3712]{1,0:T(8,128)(2,1)S(1)} %get-tuple-element.45), channel_id=1, source_target_pairs={{0,1},{1,0},{2,3},{3,2},{4,5},{5,4},{6,7},{7,6},{8,9},{9,8},{10,11... | collective-permute-start | bytes 1425416 | tf_op jit(solution)/shard_map/ppermute | solution.py:21
  36.5 9.6 %collective-permute-start.14 = (bf16[64,3712]{1,0:T(8,128)(2,1)S(1)}, bf16[64,3712]{1,0:T(8,128)(2,1)S(1)}, u32[]{:S(2)}, u32[]{:S(2)}) collective-permute-start(bf16[64,3712]{1,0:T(8,128)(2,1)S(1)} %pack.7.refs_3_.refs_1_), channel_id=1, source_target_pairs={{0,4},{1,3},{2,6},{3,1},{4,0},{5,7},{6,2},{7,5},{8,12},{9,11},{10,... | collective-permute-start | bytes 1425416 | tf_op jit(solution)/shard_map/ppermute | solution.py:21
  46.9 1.9 %collective-permute-start.15 = (bf16[64,3712]{1,0:T(8,128)(2,1)S(1)}, bf16[64,3712]{1,0:T(8,128)(2,1)S(1)}, u32[]{:S(2)}, u32[]{:S(2)}) collective-permute-start(bf16[64,3712]{1,0:T(8,128)(2,1)S(1)} %get-tuple-element.51), channel_id=1, source_target_pairs={{0,1},{1,0},{2,3},{3,2},{4,5},{5,4},{6,7},{7,6},{8,9},{9,8},{10,11... | collective-permute-start | bytes 1425416 | tf_op jit(solution)/shard_map/ppermute | solution.py:21
  47.0 5.7 %collective-permute-start.13 = (bf16[64,3712]{1,0:T(8,128)(2,1)S(1)}, bf16[64,3712]{1,0:T(8,128)(2,1)S(1)}, u32[]{:S(2)}, u32[]{:S(2)}) collective-permute-start(bf16[64,3712]{1,0:T(8,128)(2,1)S(1)} %get-tuple-element.48), channel_id=1, source_target_pairs={{0,1},{1,0},{2,3},{3,2},{4,5},{5,4},{6,7},{7,6},{8,9},{9,8},{10,11... | collective-permute-start | bytes 1425416 | tf_op jit(solution)/shard_map/ppermute | solution.py:21
  52.1 4.3 %collective-permute-start.17 = (bf16[64,3584]{1,0:T(8,128)(2,1)S(1)}, bf16[64,3584]{1,0:T(8,128)(2,1)S(1)}, u32[]{:S(2)}, u32[]{:S(2)}) collective-permute-start(bf16[64,3584]{1,0:T(8,128)(2,1)S(1)} %get-tuple-element.55), channel_id=1, source_target_pairs={{0,1},{1,0},{2,3},{3,2},{4,5},{5,4},{6,7},{7,6},{8,9},{9,8},{10,11... | collective-permute-start | bytes 1376264 | tf_op jit(solution)/shard_map/ppermute | solution.py:21
  52.3 8.1 %collective-permute-start.9 = (bf16[64,3712]{1,0:T(8,128)(2,1)S(1)}, bf16[64,3712]{1,0:T(8,128)(2,1)S(1)}, u32[]{:S(2)}, u32[]{:S(2)}) collective-permute-start(bf16[64,3712]{1,0:T(8,128)(2,1)S(1)} %get-tuple-element.42), channel_id=1, source_target_pairs={{0,1},{1,0},{2,3},{3,2},{4,5},{5,4},{6,7},{7,6},{8,9},{9,8},{10,11... | collective-permute-start | bytes 1425416 | tf_op jit(solution)/shard_map/ppermute | solution.py:21
  56.2 1.9 %collective-permute-start.16 = (bf16[64,3584]{1,0:T(8,128)(2,1)S(1)}, bf16[64,3584]{1,0:T(8,128)(2,1)S(1)}, u32[]{:S(2)}, u32[]{:S(2)}) collective-permute-start(bf16[64,3584]{1,0:T(8,128)(2,1)S(1)} %get-tuple-element.54), channel_id=1, source_target_pairs={{0,1},{1,0},{2,3},{3,2},{4,5},{5,4},{6,7},{7,6},{8,9},{9,8},{10,11... | collective-permute-start | bytes 1376264 | tf_op jit(solution)/shard_map/ppermute | solution.py:21
  57.1 8.5 %collective-permute-start.20 = (bf16[64,3584]{1,0:T(8,128)(2,1)S(1)}, bf16[64,3584]{1,0:T(8,128)(2,1)S(1)}, u32[]{:S(2)}, u32[]{:S(2)}) collective-permute-start(bf16[64,3584]{1,0:T(8,128)(2,1)S(1)} %get-tuple-element.61), channel_id=1, source_target_pairs={{0,4},{1,3},{2,6},{3,1},{4,0},{5,7},{6,2},{7,5},{8,12},{9,11},{10,... | collective-permute-start | bytes 1376264 | tf_op jit(solution)/shard_map/ppermute | solution.py:21
  58.0 8.3 %collective-permute-start.22 = (bf16[64,3584]{1,0:T(8,128)(2,1)S(1)}, bf16[64,3584]{1,0:T(8,128)(2,1)S(1)}, u32[]{:S(2)}, u32[]{:S(2)}) collective-permute-start(bf16[64,3584]{1,0:T(8,128)(2,1)S(1)} %get-tuple-element.64), channel_id=1, source_target_pairs={{0,1},{1,0},{2,3},{3,2},{4,5},{5,4},{6,7},{7,6},{8,9},{9,8},{10,11... | collective-permute-start | bytes 1376264 | tf_op jit(solution)/shard_map/ppermute | solution.py:21
  58.8 15.6 %collective-permute-start.19 = (bf16[64,3584]{1,0:T(8,128)(2,1)S(1)}, bf16[64,3584]{1,0:T(8,128)(2,1)S(1)}, u32[]{:S(2)}, u32[]{:S(2)}) collective-permute-start(bf16[64,3584]{1,0:T(8,128)(2,1)S(1)} %get-tuple-element.60), channel_id=1, source_target_pairs={{0,4},{1,3},{2,6},{3,1},{4,0},{5,7},{6,2},{7,5},{8,12},{9,11},{10,... | collective-permute-start | bytes 1376264 | tf_op jit(solution)/shard_map/ppermute | solution.py:21
  63.7 10.8 %collective-permute-start.18 = (bf16[64,3584]{1,0:T(8,128)(2,1)S(1)}, bf16[64,3584]{1,0:T(8,128)(2,1)S(1)}, u32[]{:S(2)}, u32[]{:S(2)}) collective-permute-start(bf16[64,3584]{1,0:T(8,128)(2,1)S(1)} %get-tuple-element.59), channel_id=1, source_target_pairs={{0,1},{1,0},{2,3},{3,2},{4,5},{5,4},{6,7},{7,6},{8,9},{9,8},{10,11... | collective-permute-start | bytes 1376264 | tf_op jit(solution)/shard_map/ppermute | solution.py:21
  65.8 8.6 %collective-permute-start.21 = (bf16[32,3584]{1,0:T(8,128)(2,1)S(1)}, bf16[32,3584]{1,0:T(8,128)(2,1)S(1)}, u32[]{:S(2)}, u32[]{:S(2)}) collective-permute-start(bf16[32,3584]{1,0:T(8,128)(2,1)S(1)} %get-tuple-element.63), channel_id=1, source_target_pairs={{0,2},{1,5},{2,0},{3,7},{4,6},{5,1},{6,4},{7,3},{8,10},{9,13},{10,... | collective-permute-start | bytes 688136 | tf_op jit(solution)/shard_map/ppermute | solution.py:21
  67.1 11.9 %collective-permute-start.26 = (bf16[64,3584]{1,0:T(8,128)(2,1)S(1)}, bf16[64,3584]{1,0:T(8,128)(2,1)S(1)}, u32[]{:S(2)}, u32[]{:S(2)}) collective-permute-start(bf16[64,3584]{1,0:T(8,128)(2,1)S(1)} %get-tuple-element.70), channel_id=1, source_target_pairs={{0,4},{1,3},{2,6},{3,1},{4,0},{5,7},{6,2},{7,5},{8,12},{9,11},{10,... | collective-permute-start | bytes 1376264 | tf_op jit(solution)/shard_map/ppermute | solution.py:21
  75.2 12.6 %collective-permute-start.23 = (bf16[64,3584]{1,0:T(8,128)(2,1)S(1)}, bf16[64,3584]{1,0:T(8,128)(2,1)S(1)}, u32[]{:S(2)}, u32[]{:S(2)}) collective-permute-start(bf16[64,3584]{1,0:T(8,128)(2,1)S(1)} %get-tuple-element.68), channel_id=1, source_target_pairs={{0,4},{1,3},{2,6},{3,1},{4,0},{5,7},{6,2},{7,5},{8,12},{9,11},{10,... | collective-permute-start | bytes 1376264 | tf_op jit(solution)/shard_map/ppermute | solution.py:21
  76.1 8.5 %collective-permute-start.24 = (bf16[32,3584]{1,0:T(8,128)(2,1)S(1)}, bf16[32,3584]{1,0:T(8,128)(2,1)S(1)}, u32[]{:S(2)}, u32[]{:S(2)}) collective-permute-start(bf16[32,3584]{1,0:T(8,128)(2,1)S(1)} %get-tuple-element.69), channel_id=1, source_target_pairs={{0,2},{1,5},{2,0},{3,7},{4,6},{5,1},{6,4},{7,3},{8,10},{9,13},{10,... | collective-permute-start | bytes 688136 | tf_op jit(solution)/shard_map/ppermute | solution.py:21
  77.7 7.0 %collective-permute-start.25 = (bf16[32,3584]{1,0:T(8,128)(2,1)S(1)}, bf16[32,3584]{1,0:T(8,128)(2,1)S(1)}, u32[]{:S(2)}, u32[]{:S(2)}) collective-permute-start(bf16[32,3584]{1,0:T(8,128)(2,1)S(1)} %leave.3.refs_2_), channel_id=1, source_target_pairs={{0,8},{1,9},{2,10},{3,11},{4,12},{5,13},{6,14},{7,15},{8,0},{9,1},... | collective-permute-start | bytes 688136 | tf_op jit(solution)/shard_map/ppermute | solution.py:21
  79.1 9.4 %collective-permute-start.29 = (bf16[32,3584]{1,0:T(8,128)(2,1)S(1)}, bf16[32,3584]{1,0:T(8,128)(2,1)S(1)}, u32[]{:S(2)}, u32[]{:S(2)}) collective-permute-start(bf16[32,3584]{1,0:T(8,128)(2,1)S(1)} %get-tuple-element.74), channel_id=1, source_target_pairs={{0,2},{1,5},{2,0},{3,7},{4,6},{5,1},{6,4},{7,3},{8,10},{9,13},{10,... | collective-permute-start | bytes 688136 | tf_op jit(solution)/shard_map/ppermute | solution.py:21
  84.8 10.7 %collective-permute-start.28 = (bf16[32,3584]{1,0:T(8,128)(2,1)S(1)}, bf16[32,3584]{1,0:T(8,128)(2,1)S(1)}, u32[]{:S(2)}, u32[]{:S(2)}) collective-permute-start(bf16[32,3584]{1,0:T(8,128)(2,1)S(1)} %leave.4.refs_2_), channel_id=1, source_target_pairs={{0,16},{1,17},{2,18},{3,19},{4,20},{5,21},{6,22},{7,23},{8,24},{9,... | collective-permute-start | bytes 688136 | tf_op jit(solution)/shard_map/ppermute | solution.py:21
  87.9 7.5 %collective-permute-start.27 = (bf16[32,3584]{1,0:T(8,128)(2,1)S(1)}, bf16[32,3584]{1,0:T(8,128)(2,1)S(1)}, u32[]{:S(2)}, u32[]{:S(2)}) collective-permute-start(bf16[32,3584]{1,0:T(8,128)(2,1)S(1)} %get-tuple-element.73), channel_id=1, source_target_pairs={{0,2},{1,5},{2,0},{3,7},{4,6},{5,1},{6,4},{7,3},{8,10},{9,13},{10,... | collective-permute-start | bytes 688136 | tf_op jit(solution)/shard_map/ppermute | solution.py:21
  88.6 9.8 %collective-permute-start.30 = (bf16[32,3584]{1,0:T(8,128)(2,1)S(1)}, bf16[32,3584]{1,0:T(8,128)(2,1)S(1)}, u32[]{:S(2)}, u32[]{:S(2)}) collective-permute-start(bf16[32,3584]{1,0:T(8,128)(2,1)S(1)} %leave.5.refs_4_), channel_id=1, source_target_pairs={{0,8},{1,9},{2,10},{3,11},{4,12},{5,13},{6,14},{7,15},{8,0},{9,1},... | collective-permute-start | bytes 688136 | tf_op jit(solution)/shard_map/ppermute | solution.py:21

commit v4 on v3

--- a/solution.py
+++ b/solution.py
@@ -46,18 +46,18 @@
 
 
 ORDER = (
-    "E0", "K0", "L0", "E1", "E2", "K1", "S0", "K2", "E3", "D0:w1", "K3:w0", "D1:w0", "D2", "X1",
-    "D3", "X3", "X2", "C0", "C1", "X0", "M0", "C2:w2", "V0:w2:h2", "M1:w0", "C3:h0", "M2", "V1",
-    "M3:g0", "V2:w3", "V3:w3",
+    "E0", "K0", "L0", "E1", "E2", "K1", "K2", "S0", "E3", "D0:h1", "L1:w0", "D1", "K3", "D2", "X1",
+    "X2", "D3", "C0:w2", "X3", "C1", "X0", "M0", "C2", "M1", "V0", "C3:h1", "M2", "V2", "M3",
 )
 GATHER_GROUPS = ((0,), (1,), (2,), (3,))
-REDUCE_GROUPS = ((3,), (2,), (1,), (0,))
+DIRECT = True
+REDUCE_GROUPS = ((2,), (1,), (3,), (0,))
 
 
 def any_groups(planes):
     gather = tuple((k,) for k in range(planes))
     reduce = tuple((k,) for k in reversed(range(planes)))
-    steps = ["E0", "K0", "L0"]
+    steps = ["E0", "K0", "L0", "L1"]
     for k in range(1, planes):
         steps += [f"E{k}", f"K{k}"]
     steps += ["S0"]
@@ -188,16 +188,7 @@
             ).astype(BF16)
 
 
-def expert_kernel(experts, me_ref, own_ref, got_ref, gate_ref, up_ref, down_ref, *refs):
-    if len(refs) > 4:
-        mine_ref, sent_ref, held_ref, rows_ref, hidden, sems = refs
-        copies = loading(down_ref, held_ref, sems)
-        down_ref = held_ref
-    else:
-        mine_ref, sent_ref, rows_ref, hidden = refs
-        copies = []
-    for copy in copies:
-        copy.start()
+def expert_kernel(experts, me_ref, own_ref, got_ref, gate_ref, up_ref, down_ref, mine_ref, sent_ref, rows_ref, hidden):
     _, width, units = gate_ref.shape
     slots = own_ref.shape[0]
     rows_ref[:slots, :] = own_ref[...]
@@ -210,8 +201,6 @@
         gate_val = jnp.dot(rows, gate_ref[0, :, j : j + tile], preferred_element_type=F32)
         up_val = jnp.dot(rows, up_ref[0, :, j : j + tile], preferred_element_type=F32)
         hidden[:, j : j + tile] = (gate_val / (1.0 + jnp.exp(-gate_val)) * up_val).astype(BF16)
-    for copy in copies:
-        copy.wait()
     tile = 512
     for n in range(0, width, tile):
         value = jnp.dot(hidden[...], down_ref[0, :, n : n + tile], preferred_element_type=F32)
@@ -269,10 +258,12 @@
                 out[first : first + block, n : n + tile] = value.astype(out.dtype)
 
 
-def middle_kernel(keep_ref, got_ref, rest_ref, send_ref):
+def middle_kernel(keep_ref, got_ref, *refs):
+    *more, rest_ref, send_ref = refs
     half = rest_ref.shape[0]
-    rest_ref[...] = keep_ref[:half, :] + got_ref[:half, :].astype(F32)
-    send_ref[...] = (keep_ref[half:, :] + got_ref[half:, :].astype(F32)).astype(BF16)
+    parts = [got_ref, *more]
+    rest_ref[...] = keep_ref[:half, :] + sum(part[:half, :].astype(F32) for part in parts)
+    send_ref[...] = (keep_ref[half:, :] + sum(part[half:, :].astype(F32) for part in parts)).astype(BF16)
 
 
 def sum_kernel(pieces, *refs):
@@ -327,7 +318,7 @@
     if not paired:
         far[1] = across(own, 1)
     held = {}
-    hop, wide, leaving, chosen, mine, back, got, rest, last, arrived, packed, kept = ({} for _ in range(12))
+    hop, wide, leaving, chosen, mine, back, got, rest, last, arrived, packed, kept, coming, crossed = ({} for _ in range(14))
 
     def load(name, weights):
         held[name], = line(
@@ -383,20 +374,14 @@
         leaving[k] = other_core(out)
 
     def expert(k):
-        loads_down = "down" not in held
-        arrays = [chosen[k], leaving[k], held["gate"], held["up"]]
-        mine[k], out, *brought = line(
+        mine[k], out = line(
             functools.partial(expert_kernel, experts),
-            "expert_load" if loads_down else "expert",
-            [((slots, width), BF16)] * 2 + [(w_down.shape, BF16)] * loads_down,
+            "expert",
+            [((slots, width), BF16)] * 2,
             [index],
-            arrays if loads_down else arrays + [held["down"]],
-            stored=[w_down] if loads_down else [],
-            scratch=[pltpu.VMEM((2 * slots, full), BF16), pltpu.VMEM((2 * slots, units), BF16)]
-            + [pltpu.SemaphoreType.DMA((4,))] * loads_down,
-        )
-        if loads_down:
-            held["down"], = brought
+            [chosen[k], leaving[k], held["gate"], held["up"], held["down"]],
+            scratch=[pltpu.VMEM((2 * slots, full), BF16), pltpu.VMEM((2 * slots, units), BF16)],
+        )
         back[k] = other_core(out)
 
     def shared():
@@ -432,32 +417,48 @@
         got[r] = second_hop(send)
 
     def middle(r):
-        half = block * len(reduce_groups[r])
+        group = reduce_groups[r]
+        if group == (1,):
+            out, = line(
+                functools.partial(sum_kernel, [[(0, 0), (1, 0)]]),
+                "sum",
+                [((2 * block, width), BF16)],
+                [],
+                [kept[r], got[r]],
+            )
+            crossed[1] = across(out, 1)
+            return
+        half = block * len(group)
         rest[r], send = line(
-            middle_kernel, "middle", [((half, width), F32), ((half, width), BF16)], [], [kept[r], got[r]]
+            middle_kernel,
+            "middle",
+            [((half, width), F32), ((half, width), BF16)],
+            [],
+            [kept[r], got[r]] + ([crossed[1]] if 0 in group else []),
         )
         last[r] = first_hop(send)
 
     def leave(r):
         group = reduce_groups[r]
         for k in group:
-            if k == 0 or (k == 3 and 1 in group):
+            if k < 2:
                 continue
-            both = [k, 3] if k == 1 and 3 in group else [k]
+            both = [k]
             arrays, pieces = [rest[r], last[r]], []
             for j in both:
                 at = group.index(j) * block
                 pieces.append([(0, at), (1, at)])
-            if k >= 2 and k & 1 == 0:
+            if k >= 2 and k & 1 == 0 and not DIRECT:
                 array, at = arrived.pop(k + 1)
                 arrays.append(array)
                 pieces[0].append((2, at))
             out, = line(
                 functools.partial(sum_kernel, pieces), "leave", [((len(both) * block, width), BF16)], [], arrays
             )
-            out = across(out, 1 if k & 1 else k)
+            out = across(out, 1 if k & 1 and not DIRECT else k)
             for i, j in enumerate(both):
                 arrived[j] = (out, i * block)
+                coming[j] = out
 
     def final():
         r = [r for r, group in enumerate(reduce_groups) if 0 in group][0]
@@ -479,7 +480,7 @@
     steps = {
         "E": enter,
         "K": pack,
-        "L": lambda i: load("gate", w_gate),
+        "L": lambda i: load("down", w_down) if i else load("gate", w_gate),
         "D": dispatch,
         "X": expert,
         "S": lambda i: shared(),
@@ -487,7 +488,7 @@
         "M": middle,
         "V": leave,
     }
-    stores = {"h": hop, "w": wide, "c": leaving, "b": back, "g": got, "l": last}
+    stores = {"h": hop, "w": wide, "c": leaving, "b": back, "g": got, "l": last, "a": coming, "z": crossed}
     for step in order:
         step, *also = step.split(":")
         line.also = [stores[name[0]][int(name[1:])] for name in also]

time: 99.4 us -> 96.4 us (0.970); the launches traced: 99.2 us -> 94.8 us
  waiting for transfers between devices: 40.7 us -> 37.2 us
  starting transfers between devices: 27.4 us -> 26 us
    ppermute x31 -> x30, waiting for transfers between devices: 40.7 us -> 37.2 us  [swap(): return lax.ppermute(block, AXIS, route)]
    ppermute x31 -> x30, starting transfers between devices: 27.4 us -> 26 us  [swap(): return lax.ppermute(block, AXIS, route)]
  transfers between devices with their start and end apart: 31 -> 30, of which waited for: 15 -> 13; matrix products, arithmetic and copies ran while one was open for 0% -> 0% of each run, Pallas kernels for 30% -> 32%
where the time goes in v4:
time: 96.4 us; the launch traced here: 94.8 us
  waiting for transfers between devices  37.2 us (39%)
  Pallas kernels  31.3 us (32%)
  starting transfers between devices  26 us (27%)
    ppermute x30, waiting for transfers between devices, swap(): return lax.ppermute(block, AXIS, route)  37.2 us
    pallas_call x30, Pallas kernels, __call__(): pl.pallas_call(body, in_specs=[SCALAR] * len(scalars) + [WHOLE] * len(arr...  31.3 us
    ppermute x30, starting transfers between devices, swap(): return lax.ppermute(block, AXIS, route)  26 us
  transfers between devices with their start and end apart: 30, of which 13 were waited for; matrix products, arithmetic and copies ran while one was open for 0% of the time, Pallas kernels for 32%

profile of v4, /device:TPU:0, one launch (start us, length us, event | category | flops | bytes accessed | tf_op | source)
XLA Modules:
  0.0 94.8 jit_solution(14251617146829442624)
XLA Ops:
  0.5 1.1 %own.1.refs_0_.refs_2_ = bf16[32,3712]{1,0:T(8,128)(2,1)S(1)} custom-call(s32[1]{0:T(128)} %bitcast.refs_0_, bf16[2,16,3584]{2,1,0:T(8,128)(2,1)} %refs_1_.1, s32[2,8,16]{2,1,0:T(8,128)} %bitcast.3, f32[2,8,16]{2,1,0:T(8,128)} %bitcast.4), custom_call_target="tpu_custom_call" | custom-call | flops 1 | bytes 1 | tf_op jit(solution)/shard_map/own/pallas_call | solution.py:80
  1.5 2.6 %collective-permute-start = (bf16[32,3712]{1,0:T(8,128)(2,1)S(1)}, bf16[32,3712]{1,0:T(8,128)(2,1)S(1)}, u32[]{:S(2)}, u32[]{:S(2)}) collective-permute-start(bf16[32,3712]{1,0:T(8,128)(2,1)S(1)} %own.1.refs_0_.refs_2_), channel_id=1, source_target_pairs={{0,2},{1,5},{2,0},{3,7},{4,6},{5,1},{6,4},{7,3},{8,10},{9,13},{10,... | collective-permute-start | bytes 712712 | tf_op jit(solution)/shard_map/ppermute | solution.py:21
  4.1 1.6 %collective-permute-start.3 = (bf16[32,3712]{1,0:T(8,128)(2,1)S(1)}, bf16[32,3712]{1,0:T(8,128)(2,1)S(1)}, u32[]{:S(2)}, u32[]{:S(2)}) collective-permute-start(bf16[32,3712]{1,0:T(8,128)(2,1)S(1)} %own.1.refs_0_.refs_2_), channel_id=1, source_target_pairs={{0,8},{1,9},{2,10},{3,11},{4,12},{5,13},{6,14},{7,15},{8,0},{9,1},... | collective-permute-start | bytes 712712 | tf_op jit(solution)/shard_map/ppermute | solution.py:21
  5.6 2.6 %collective-permute-start.2 = (bf16[32,3712]{1,0:T(8,128)(2,1)S(1)}, bf16[32,3712]{1,0:T(8,128)(2,1)S(1)}, u32[]{:S(2)}, u32[]{:S(2)}) collective-permute-start(bf16[32,3712]{1,0:T(8,128)(2,1)S(1)} %own.1.refs_0_.refs_2_), channel_id=1, source_target_pairs={{0,16},{1,17},{2,18},{3,19},{4,20},{5,21},{6,22},{7,23},{8,24},{9,... | collective-permute-start | bytes 712712 | tf_op jit(solution)/shard_map/ppermute | solution.py:21
  8.3 2.0 %collective-permute-start.1 = (bf16[64,3712]{1,0:T(8,128)(2,1)S(1)}, bf16[64,3712]{1,0:T(8,128)(2,1)S(1)}, u32[]{:S(2)}, u32[]{:S(2)}) collective-permute-start(bf16[64,3712]{1,0:T(8,128)(2,1)S(1)} %pack.4.refs_1_.refs_0_), channel_id=1, source_target_pairs={{0,4},{1,3},{2,6},{3,1},{4,0},{5,7},{6,2},{7,5},{8,12},{9,11},{10,... | collective-permute-start | bytes 1425416 | tf_op jit(solution)/shard_map/ppermute | solution.py:21
  10.3 3.2 %load.2.refs_1_.refs_3_ = bf16[1,3584,1024]{2,1,0:T(8,128)(2,1)S(1)} custom-call(bf16[1,3584,1024]{2,1,0:T(8,128)(2,1)} %refs_0_.2, bf16[64,3712]{1,0:T(8,128)(2,1)S(1)} %pack.4.refs_1_.refs_0_), custom_call_target="tpu_custom_call" | custom-call | flops 1 | bytes 1 | tf_op jit(solution)/shard_map/load/pallas_call | solution.py:80
  13.5 3.5 %collective-permute-done.3.refs_0_ = bf16[32,3712]{1,0:T(8,128)(2,1)S(1)} collective-permute-done((bf16[32,3712]{1,0:T(8,128)(2,1)S(1)}, bf16[32,3712]{1,0:T(8,128)(2,1)S(1)}, u32[]{:S(2)}, u32[]{:S(2)}) %collective-permute-start.3) | collective-permute-done | bytes 237600 | tf_op jit(solution)/shard_map/ppermute | solution.py:21
  17.0 2.4 %collective-permute-done.2.refs_0_ = bf16[32,3712]{1,0:T(8,128)(2,1)S(1)} collective-permute-done((bf16[32,3712]{1,0:T(8,128)(2,1)S(1)}, bf16[32,3712]{1,0:T(8,128)(2,1)S(1)}, u32[]{:S(2)}, u32[]{:S(2)}) %collective-permute-start.2) | collective-permute-done | bytes 237600 | tf_op jit(solution)/shard_map/ppermute | solution.py:21
  19.3 1.5 %collective-permute-start.6 = (bf16[32,3712]{1,0:T(8,128)(2,1)S(1)}, bf16[32,3712]{1,0:T(8,128)(2,1)S(1)}, u32[]{:S(2)}, u32[]{:S(2)}) collective-permute-start(bf16[32,3712]{1,0:T(8,128)(2,1)S(1)} %enter.4.refs_2_.refs_0_), channel_id=1, source_target_pairs={{0,2},{1,5},{2,0},{3,7},{4,6},{5,1},{6,4},{7,3},{8,10},{9,13},{10,... | collective-permute-start | bytes 712712 | tf_op jit(solution)/shard_map/ppermute | solution.py:21
  20.8 2.3 %collective-permute-done.7.refs_1_.refs_4_.refs_7_ = bf16[32,3712]{1,0:T(8,128)(2,1)S(1)} collective-permute-done((bf16[32,3712]{1,0:T(8,128)(2,1)S(1)}, bf16[32,3712]{1,0:T(8,128)(2,1)S(1)}, u32[]{:S(2)}, u32[]{:S(2)}) %collective-permute-start.7) | collective-permute-done | bytes 237600 | tf_op jit(solution)/shard_map/ppermute | solution.py:21
  23.6 3.3 %collective-permute-done.6.refs_1_ = bf16[32,3712]{1,0:T(8,128)(2,1)S(1)} collective-permute-done((bf16[32,3712]{1,0:T(8,128)(2,1)S(1)}, bf16[32,3712]{1,0:T(8,128)(2,1)S(1)}, u32[]{:S(2)}, u32[]{:S(2)}) %collective-permute-start.6) | collective-permute-done | bytes 237600 | tf_op jit(solution)/shard_map/ppermute | solution.py:21
  27.4 3.4 %shared.1 = (f32[128,3584]{1,0:T(8,128)S(1)}, bf16[1,3584,1024]{2,1,0:T(8,128)(2,1)S(1)}) custom-call(bf16[64,3712]{1,0:T(8,128)(2,1)S(1)} %pack.4.refs_1_.refs_0_, bf16[64,3712]{1,0:T(8,128)(2,1)S(1)} %collective-permute-done.1.refs_1_.refs_2_, bf16[3,3584,128]{2,1,0:T(8,128)(2,1)S(1)} %copy-done, bf16[3,3584,128]{2,1,0:T(8,128)(2,1)S(1)} %collective-permute-done.5.refs_3_, ...), custom_call_target="tpu_custom_call" | custom-call | flops 1 | bytes 1 | tf_op jit(solution)/shard_map/shared/pallas_call | solution.py:80
  30.8 1.7 %collective-permute-start.12 = (bf16[32,3712]{1,0:T(8,128)(2,1)S(1)}, bf16[32,3712]{1,0:T(8,128)(2,1)S(1)}, u32[]{:S(2)}, u32[]{:S(2)}) collective-permute-start(bf16[32,3712]{1,0:T(8,128)(2,1)S(1)} %enter.5.refs_3_.refs_0_), channel_id=1, source_target_pairs={{0,2},{1,5},{2,0},{3,7},{4,6},{5,1},{6,4},{7,3},{8,10},{9,13},{10,... | collective-permute-start | bytes 712712 | tf_op jit(solution)/shard_map/ppermute | solution.py:21
  33.2 3.2 %load.3.refs_3_.refs_5_ = bf16[1,1024,3584]{2,1,0:T(8,128)(2,1)S(1)} custom-call(bf16[1,1024,3584]{2,1,0:T(8,128)(2,1)} %refs_0_.3, bf16[64,3712]{1,0:T(8,128)(2,1)S(1)} %get-tuple-element.38.refs_1_, bf16[64,3712]{1,0:T(8,128)(2,1)S(1)} %collective-permute-done.1.refs_1_.refs_2_), custom_call_target="tpu_custom_call" | custom-call | flops 1 | bytes 1 | tf_op jit(solution)/shard_map/load/pallas_call | solution.py:80
  37.2 1.2 %collective-permute-done.12.refs_1_ = bf16[32,3712]{1,0:T(8,128)(2,1)S(1)} collective-permute-done((bf16[32,3712]{1,0:T(8,128)(2,1)S(1)}, bf16[32,3712]{1,0:T(8,128)(2,1)S(1)}, u32[]{:S(2)}, u32[]{:S(2)}) %collective-permute-start.12) | collective-permute-done | bytes 237600 | tf_op jit(solution)/shard_map/ppermute | solution.py:21
  38.4 1.1 %collective-permute-done.11.refs_2_.refs_6_ = bf16[64,3712]{1,0:T(8,128)(2,1)S(1)} collective-permute-done((bf16[64,3712]{1,0:T(8,128)(2,1)S(1)}, bf16[64,3712]{1,0:T(8,128)(2,1)S(1)}, u32[]{:S(2)}, u32[]{:S(2)}) %collective-permute-start.11) | collective-permute-done | bytes 475168 | tf_op jit(solution)/shard_map/ppermute | solution.py:21
  40.7 3.3 %expert.4 = (bf16[64,3584]{1,0:T(8,128)(2,1)S(1)}, bf16[64,3584]{1,0:T(8,128)(2,1)S(1)}) custom-call(s32[1]{0:T(128)} %bitcast.refs_0_, bf16[64,3712]{1,0:T(8,128)(2,1)S(1)} %get-tuple-element.41.refs_2_.refs_1_, bf16[64,3712]{1,0:T(8,128)(2,1)S(1)} %collective-permute-done.10.refs_2_, bf16[1,3584,1024]{2,1,0:T(8,128)(2,1)S(1)} %load.2.refs_1_.refs_3_, ...), custom_call_target="tpu_custom_call" | custom-call | flops 1 | bytes 1 | tf_op jit(solution)/shard_map/expert/pallas_call | solution.py:80
  44.0 3.3 %expert.5 = (bf16[64,3584]{1,0:T(8,128)(2,1)S(1)}, bf16[64,3584]{1,0:T(8,128)(2,1)S(1)}) custom-call(s32[1]{0:T(128)} %bitcast.refs_0_, bf16[64,3712]{1,0:T(8,128)(2,1)S(1)} %get-tuple-element.43.refs_6_.refs_1_, bf16[64,3712]{1,0:T(8,128)(2,1)S(1)} %collective-permute-done.15.refs_2_, bf16[1,3584,1024]{2,1,0:T(8,128)(2,1)S(1)} %load.2.refs_1_.refs_3_, ...), custom_call_target="tpu_custom_call" | custom-call | flops 1 | bytes 1 | tf_op jit(solution)/shard_map/expert/pallas_call | solution.py:80
  47.3 1.6 %collective-permute-done.14.refs_2_ = bf16[64,3712]{1,0:T(8,128)(2,1)S(1)} collective-permute-done((bf16[64,3712]{1,0:T(8,128)(2,1)S(1)}, bf16[64,3712]{1,0:T(8,128)(2,1)S(1)}, u32[]{:S(2)}, u32[]{:S(2)}) %collective-permute-start.14) | collective-permute-done | bytes 475168 | tf_op jit(solution)/shard_map/ppermute | solution.py:21
  50.8 1.5 %collective-permute-done.17.refs_4_ = bf16[64,3584]{1,0:T(8,128)(2,1)S(1)} collective-permute-done((bf16[64,3584]{1,0:T(8,128)(2,1)S(1)}, bf16[64,3584]{1,0:T(8,128)(2,1)S(1)}, u32[]{:S(2)}, u32[]{:S(2)}) %collective-permute-start.17) | collective-permute-done | bytes 458784 | tf_op jit(solution)/shard_map/ppermute | solution.py:21
  53.4 3.5 %expert.6 = (bf16[64,3584]{1,0:T(8,128)(2,1)S(1)}, bf16[64,3584]{1,0:T(8,128)(2,1)S(1)}) custom-call(s32[1]{0:T(128)} %bitcast.refs_0_, bf16[64,3712]{1,0:T(8,128)(2,1)S(1)} %get-tuple-element.48.refs_5_.refs_1_, bf16[64,3712]{1,0:T(8,128)(2,1)S(1)} %collective-permute-done.16.refs_2_, bf16[1,3584,1024]{2,1,0:T(8,128)(2,1)S(1)} %load.2.refs_1_.refs_3_, ...), custom_call_target="tpu_custom_call" | custom-call | flops 1 | bytes 1 | tf_op jit(solution)/shard_map/expert/pallas_call | solution.py:80
  57.7 1.7 %collective-permute-start.21 = (bf16[64,3584]{1,0:T(8,128)(2,1)S(1)}, bf16[64,3584]{1,0:T(8,128)(2,1)S(1)}, u32[]{:S(2)}, u32[]{:S(2)}) collective-permute-start(bf16[64,3584]{1,0:T(8,128)(2,1)S(1)} %get-tuple-element.59), channel_id=1, source_target_pairs={{0,4},{1,3},{2,6},{3,1},{4,0},{5,7},{6,2},{7,5},{8,12},{9,11},{10,... | collective-permute-start | bytes 1376264 | tf_op jit(solution)/shard_map/ppermute | solution.py:21
  59.4 3.3 %expert.7 = (bf16[64,3584]{1,0:T(8,128)(2,1)S(1)}, bf16[64,3584]{1,0:T(8,128)(2,1)S(1)}) custom-call(s32[1]{0:T(128)} %bitcast.refs_0_, bf16[64,3712]{1,0:T(8,128)(2,1)S(1)} %get-tuple-element.38.refs_1_, bf16[64,3712]{1,0:T(8,128)(2,1)S(1)} %collective-permute-done.8.refs_2_, bf16[1,3584,1024]{2,1,0:T(8,128)(2,1)S(1)} %load.2.refs_1_.refs_3_, ...), custom_call_target="tpu_custom_call" | custom-call | flops 1 | bytes 1 | tf_op jit(solution)/shard_map/expert/pallas_call | solution.py:80
  64.2 1.7 %collective-permute-start.20 = (bf16[32,3584]{1,0:T(8,128)(2,1)S(1)}, bf16[32,3584]{1,0:T(8,128)(2,1)S(1)}, u32[]{:S(2)}, u32[]{:S(2)}) collective-permute-start(bf16[32,3584]{1,0:T(8,128)(2,1)S(1)} %get-tuple-element.58), channel_id=1, source_target_pairs={{0,2},{1,5},{2,0},{3,7},{4,6},{5,1},{6,4},{7,3},{8,10},{9,13},{10,... | collective-permute-start | bytes 688136 | tf_op jit(solution)/shard_map/ppermute | solution.py:21
  66.6 6.1 %collective-permute-done.20.refs_1_ = bf16[32,3584]{1,0:T(8,128)(2,1)S(1)} collective-permute-done((bf16[32,3584]{1,0:T(8,128)(2,1)S(1)}, bf16[32,3584]{1,0:T(8,128)(2,1)S(1)}, u32[]{:S(2)}, u32[]{:S(2)}) %collective-permute-start.20) | collective-permute-done | bytes 229408 | tf_op jit(solution)/shard_map/ppermute | solution.py:21
  73.5 1.8 %collective-permute-start.23 = (bf16[64,3584]{1,0:T(8,128)(2,1)S(1)}, bf16[64,3584]{1,0:T(8,128)(2,1)S(1)}, u32[]{:S(2)}, u32[]{:S(2)}) collective-permute-start(bf16[64,3584]{1,0:T(8,128)(2,1)S(1)} %get-tuple-element.63), channel_id=1, source_target_pairs={{0,4},{1,3},{2,6},{3,1},{4,0},{5,7},{6,2},{7,5},{8,12},{9,11},{10,... | collective-permute-start | bytes 1376264 | tf_op jit(solution)/shard_map/ppermute | solution.py:21
  75.8 0.8 collective-permute-start.28
  76.6 6.1 %collective-permute-done.26.refs_1_ = bf16[32,3584]{1,0:T(8,128)(2,1)S(1)} collective-permute-done((bf16[32,3584]{1,0:T(8,128)(2,1)S(1)}, bf16[32,3584]{1,0:T(8,128)(2,1)S(1)}, u32[]{:S(2)}, u32[]{:S(2)}) %collective-permute-start.26) | collective-permute-done | bytes 229408 | tf_op jit(solution)/shard_map/ppermute | solution.py:21
  82.8 1.6 %collective-permute-done.23.refs_1_ = bf16[64,3584]{1,0:T(8,128)(2,1)S(1)} collective-permute-done((bf16[64,3584]{1,0:T(8,128)(2,1)S(1)}, bf16[64,3584]{1,0:T(8,128)(2,1)S(1)}, u32[]{:S(2)}, u32[]{:S(2)}) %collective-permute-start.23) | collective-permute-done | bytes 458784 | tf_op jit(solution)/shard_map/ppermute | solution.py:21
  85.3 2.6 %collective-permute-start.29 = (bf16[32,3584]{1,0:T(8,128)(2,1)S(1)}, bf16[32,3584]{1,0:T(8,128)(2,1)S(1)}, u32[]{:S(2)}, u32[]{:S(2)}) collective-permute-start(bf16[32,3584]{1,0:T(8,128)(2,1)S(1)} %leave.3.refs_3_), channel_id=1, source_target_pairs={{0,24},{1,25},{2,26},{3,27},{4,28},{5,29},{6,30},{7,31},{8,16},{9,... | collective-permute-start | bytes 688136 | tf_op jit(solution)/shard_map/ppermute | solution.py:21
  87.9 6.1 %collective-permute-done.28.refs_2_ = bf16[32,3584]{1,0:T(8,128)(2,1)S(1)} collective-permute-done((bf16[32,3584]{1,0:T(8,128)(2,1)S(1)}, bf16[32,3584]{1,0:T(8,128)(2,1)S(1)}, u32[]{:S(2)}, u32[]{:S(2)}) %collective-permute-start.28) | collective-permute-done | bytes 229408 | tf_op jit(solution)/shard_map/ppermute | solution.py:21
  94.0 0.8 final.1
  (60 shorter events, 12.1 us)
Async XLA Ops:
  0.0 27.4 %collective-permute-start.5 = (bf16[3,3584,128]{2,1,0:T(8,128)(2,1)}, bf16[3,3584,128]{2,1,0:T(8,128)(2,1)S(1)}, u32[]{:S(2)}, u32[]{:S(2)}) collective-permute-start(bf16[3,3584,128]{2,1,0:T(8,128)(2,1)} %refs_2_.1), channel_id=1, source_target_pairs={{0,1},{1,0},{2,3},{3,2},{4,5},{5,4},{6,7},{7,6},{8,9},{9,8},{10,11... | collective-permute-start | bytes 8257544 | tf_op jit(solution)/shard_map/ppermute | solution.py:21
  1.5 6.7 %collective-permute-start = (bf16[32,3712]{1,0:T(8,128)(2,1)S(1)}, bf16[32,3712]{1,0:T(8,128)(2,1)S(1)}, u32[]{:S(2)}, u32[]{:S(2)}) collective-permute-start(bf16[32,3712]{1,0:T(8,128)(2,1)S(1)} %own.1.refs_0_.refs_2_), channel_id=1, source_target_pairs={{0,2},{1,5},{2,0},{3,7},{4,6},{5,1},{6,4},{7,3},{8,10},{9,13},{10,... | collective-permute-start | bytes 712712 | tf_op jit(solution)/shard_map/ppermute | solution.py:21
  4.1 12.9 %collective-permute-start.3 = (bf16[32,3712]{1,0:T(8,128)(2,1)S(1)}, bf16[32,3712]{1,0:T(8,128)(2,1)S(1)}, u32[]{:S(2)}, u32[]{:S(2)}) collective-permute-start(bf16[32,3712]{1,0:T(8,128)(2,1)S(1)} %own.1.refs_0_.refs_2_), channel_id=1, source_target_pairs={{0,8},{1,9},{2,10},{3,11},{4,12},{5,13},{6,14},{7,15},{8,0},{9,1},... | collective-permute-start | bytes 712712 | tf_op jit(solution)/shard_map/ppermute | solution.py:21
  5.6 13.7 %collective-permute-start.2 = (bf16[32,3712]{1,0:T(8,128)(2,1)S(1)}, bf16[32,3712]{1,0:T(8,128)(2,1)S(1)}, u32[]{:S(2)}, u32[]{:S(2)}) collective-permute-start(bf16[32,3712]{1,0:T(8,128)(2,1)S(1)} %own.1.refs_0_.refs_2_), channel_id=1, source_target_pairs={{0,16},{1,17},{2,18},{3,19},{4,20},{5,21},{6,22},{7,23},{8,24},{9,... | collective-permute-start | bytes 712712 | tf_op jit(solution)/shard_map/ppermute | solution.py:21
  8.3 19.1 %collective-permute-start.1 = (bf16[64,3712]{1,0:T(8,128)(2,1)S(1)}, bf16[64,3712]{1,0:T(8,128)(2,1)S(1)}, u32[]{:S(2)}, u32[]{:S(2)}) collective-permute-start(bf16[64,3712]{1,0:T(8,128)(2,1)S(1)} %pack.4.refs_1_.refs_0_), channel_id=1, source_target_pairs={{0,4},{1,3},{2,6},{3,1},{4,0},{5,7},{6,2},{7,5},{8,12},{9,11},{10,... | collective-permute-start | bytes 1425416 | tf_op jit(solution)/shard_map/ppermute | solution.py:21
  13.5 13.9 %copy-start = (bf16[3,3584,128]{2,1,0:T(8,128)(2,1)S(1)}, bf16[3,3584,128]{2,1,0:T(8,128)(2,1)}, u32[]{:S(2)}) copy-start(bf16[3,3584,128]{2,1,0:T(8,128)(2,1)} %refs_2_.1) | copy-start | bytes 8257540
  17.0 6.1 %collective-permute-start.7 = (bf16[32,3712]{1,0:T(8,128)(2,1)S(1)}, bf16[32,3712]{1,0:T(8,128)(2,1)S(1)}, u32[]{:S(2)}, u32[]{:S(2)}) collective-permute-start(bf16[32,3712]{1,0:T(8,128)(2,1)S(1)} %enter.3.refs_1_.refs_0_), channel_id=1, source_target_pairs={{0,2},{1,5},{2,0},{3,7},{4,6},{5,1},{6,4},{7,3},{8,10},{9,13},{10,... | collective-permute-start | bytes 712712 | tf_op jit(solution)/shard_map/ppermute | solution.py:21
  19.3 7.5 %collective-permute-start.6 = (bf16[32,3712]{1,0:T(8,128)(2,1)S(1)}, bf16[32,3712]{1,0:T(8,128)(2,1)S(1)}, u32[]{:S(2)}, u32[]{:S(2)}) collective-permute-start(bf16[32,3712]{1,0:T(8,128)(2,1)S(1)} %enter.4.refs_2_.refs_0_), channel_id=1, source_target_pairs={{0,2},{1,5},{2,0},{3,7},{4,6},{5,1},{6,4},{7,3},{8,10},{9,13},{10,... | collective-permute-start | bytes 712712 | tf_op jit(solution)/shard_map/ppermute | solution.py:21
  23.1 13.3 %collective-permute-start.9 = (bf16[64,3712]{1,0:T(8,128)(2,1)S(1)}, bf16[64,3712]{1,0:T(8,128)(2,1)S(1)}, u32[]{:S(2)}, u32[]{:S(2)}) collective-permute-start(bf16[64,3712]{1,0:T(8,128)(2,1)S(1)} %pack.5.refs_2_.refs_1_), channel_id=1, source_target_pairs={{0,4},{1,3},{2,6},{3,1},{4,0},{5,7},{6,2},{7,5},{8,12},{9,11},{10,... | collective-permute-start | bytes 1425416 | tf_op jit(solution)/shard_map/ppermute | solution.py:21
  23.6 7.3 %collective-permute-start.4 = (bf16[32,3712]{1,0:T(8,128)(2,1)S(1)}, bf16[32,3712]{1,0:T(8,128)(2,1)S(1)}, u32[]{:S(2)}, u32[]{:S(2)}) collective-permute-start(bf16[32,3712]{1,0:T(8,128)(2,1)S(1)} %enter.4.refs_2_.refs_0_), channel_id=1, source_target_pairs={{0,8},{1,9},{2,10},{3,11},{4,12},{5,13},{6,14},{7,15},{8,0},{9,1},... | collective-permute-start | bytes 712712 | tf_op jit(solution)/shard_map/ppermute | solution.py:21
  26.9 12.6 %collective-permute-start.11 = (bf16[64,3712]{1,0:T(8,128)(2,1)S(1)}, bf16[64,3712]{1,0:T(8,128)(2,1)S(1)}, u32[]{:S(2)}, u32[]{:S(2)}) collective-permute-start(bf16[64,3712]{1,0:T(8,128)(2,1)S(1)} %pack.6.refs_5_.refs_1_), channel_id=1, source_target_pairs={{0,4},{1,3},{2,6},{3,1},{4,0},{5,7},{6,2},{7,5},{8,12},{9,11},{10,... | collective-permute-start | bytes 1425416 | tf_op jit(solution)/shard_map/ppermute | solution.py:21
  30.8 7.5 %collective-permute-start.12 = (bf16[32,3712]{1,0:T(8,128)(2,1)S(1)}, bf16[32,3712]{1,0:T(8,128)(2,1)S(1)}, u32[]{:S(2)}, u32[]{:S(2)}) collective-permute-start(bf16[32,3712]{1,0:T(8,128)(2,1)S(1)} %enter.5.refs_3_.refs_0_), channel_id=1, source_target_pairs={{0,2},{1,5},{2,0},{3,7},{4,6},{5,1},{6,4},{7,3},{8,10},{9,13},{10,... | collective-permute-start | bytes 712712 | tf_op jit(solution)/shard_map/ppermute | solution.py:21
  37.1 3.6 %collective-permute-start.10 = (bf16[64,3712]{1,0:T(8,128)(2,1)S(1)}, bf16[64,3712]{1,0:T(8,128)(2,1)S(1)}, u32[]{:S(2)}, u32[]{:S(2)}) collective-permute-start(bf16[64,3712]{1,0:T(8,128)(2,1)S(1)} %get-tuple-element.42), channel_id=1, source_target_pairs={{0,1},{1,0},{2,3},{3,2},{4,5},{5,4},{6,7},{7,6},{8,9},{9,8},{10,11... | collective-permute-start | bytes 1425416 | tf_op jit(solution)/shard_map/ppermute | solution.py:21
  40.2 3.8 %collective-permute-start.15 = (bf16[64,3712]{1,0:T(8,128)(2,1)S(1)}, bf16[64,3712]{1,0:T(8,128)(2,1)S(1)}, u32[]{:S(2)}, u32[]{:S(2)}) collective-permute-start(bf16[64,3712]{1,0:T(8,128)(2,1)S(1)} %get-tuple-element.46), channel_id=1, source_target_pairs={{0,1},{1,0},{2,3},{3,2},{4,5},{5,4},{6,7},{7,6},{8,9},{9,8},{10,11... | collective-permute-start | bytes 1425416 | tf_op jit(solution)/shard_map/ppermute | solution.py:21
  40.3 8.7 %collective-permute-start.14 = (bf16[64,3712]{1,0:T(8,128)(2,1)S(1)}, bf16[64,3712]{1,0:T(8,128)(2,1)S(1)}, u32[]{:S(2)}, u32[]{:S(2)}) collective-permute-start(bf16[64,3712]{1,0:T(8,128)(2,1)S(1)} %pack.7.refs_3_.refs_1_), channel_id=1, source_target_pairs={{0,4},{1,3},{2,6},{3,1},{4,0},{5,7},{6,2},{7,5},{8,12},{9,11},{10,... | collective-permute-start | bytes 1425416 | tf_op jit(solution)/shard_map/ppermute | solution.py:21
  49.7 3.7 %collective-permute-start.16 = (bf16[64,3712]{1,0:T(8,128)(2,1)S(1)}, bf16[64,3712]{1,0:T(8,128)(2,1)S(1)}, u32[]{:S(2)}, u32[]{:S(2)}) collective-permute-start(bf16[64,3712]{1,0:T(8,128)(2,1)S(1)} %get-tuple-element.49), channel_id=1, source_target_pairs={{0,1},{1,0},{2,3},{3,2},{4,5},{5,4},{6,7},{7,6},{8,9},{9,8},{10,11... | collective-permute-start | bytes 1425416 | tf_op jit(solution)/shard_map/ppermute | solution.py:21
  49.8 2.5 %collective-permute-start.17 = (bf16[64,3584]{1,0:T(8,128)(2,1)S(1)}, bf16[64,3584]{1,0:T(8,128)(2,1)S(1)}, u32[]{:S(2)}, u32[]{:S(2)}) collective-permute-start(bf16[64,3584]{1,0:T(8,128)(2,1)S(1)} %get-tuple-element.50), channel_id=1, source_target_pairs={{0,1},{1,0},{2,3},{3,2},{4,5},{5,4},{6,7},{7,6},{8,9},{9,8},{10,11... | collective-permute-start | bytes 1376264 | tf_op jit(solution)/shard_map/ppermute | solution.py:21
  50.3 9.2 %collective-permute-start.8 = (bf16[64,3712]{1,0:T(8,128)(2,1)S(1)}, bf16[64,3712]{1,0:T(8,128)(2,1)S(1)}, u32[]{:S(2)}, u32[]{:S(2)}) collective-permute-start(bf16[64,3712]{1,0:T(8,128)(2,1)S(1)} %get-tuple-element.39), channel_id=1, source_target_pairs={{0,1},{1,0},{2,3},{3,2},{4,5},{5,4},{6,7},{7,6},{8,9},{9,8},{10,11... | collective-permute-start | bytes 1425416 | tf_op jit(solution)/shard_map/ppermute | solution.py:21
  50.3 6.6 %collective-permute-start.13 = (bf16[64,3584]{1,0:T(8,128)(2,1)S(1)}, bf16[64,3584]{1,0:T(8,128)(2,1)S(1)}, u32[]{:S(2)}, u32[]{:S(2)}) collective-permute-start(bf16[64,3584]{1,0:T(8,128)(2,1)S(1)} %get-tuple-element.45), channel_id=1, source_target_pairs={{0,1},{1,0},{2,3},{3,2},{4,5},{5,4},{6,7},{7,6},{8,9},{9,8},{10,11... | collective-permute-start | bytes 1376264 | tf_op jit(solution)/shard_map/ppermute | solution.py:21
  53.0 10.1 %collective-permute-start.19 = (bf16[64,3584]{1,0:T(8,128)(2,1)S(1)}, bf16[64,3584]{1,0:T(8,128)(2,1)S(1)}, u32[]{:S(2)}, u32[]{:S(2)}) collective-permute-start(bf16[64,3584]{1,0:T(8,128)(2,1)S(1)} %get-tuple-element.56), channel_id=1, source_target_pairs={{0,4},{1,3},{2,6},{3,1},{4,0},{5,7},{6,2},{7,5},{8,12},{9,11},{10,... | collective-permute-start | bytes 1376264 | tf_op jit(solution)/shard_map/ppermute | solution.py:21
  56.9 6.2 %collective-permute-start.22 = (bf16[64,3584]{1,0:T(8,128)(2,1)S(1)}, bf16[64,3584]{1,0:T(8,128)(2,1)S(1)}, u32[]{:S(2)}, u32[]{:S(2)}) collective-permute-start(bf16[64,3584]{1,0:T(8,128)(2,1)S(1)} %get-tuple-element.60), channel_id=1, source_target_pairs={{0,1},{1,0},{2,3},{3,2},{4,5},{5,4},{6,7},{7,6},{8,9},{9,8},{10,11... | collective-permute-start | bytes 1376264 | tf_op jit(solution)/shard_map/ppermute | solution.py:21
  57.7 8.7 %collective-permute-start.21 = (bf16[64,3584]{1,0:T(8,128)(2,1)S(1)}, bf16[64,3584]{1,0:T(8,128)(2,1)S(1)}, u32[]{:S(2)}, u32[]{:S(2)}) collective-permute-start(bf16[64,3584]{1,0:T(8,128)(2,1)S(1)} %get-tuple-element.59), channel_id=1, source_target_pairs={{0,4},{1,3},{2,6},{3,1},{4,0},{5,7},{6,2},{7,5},{8,12},{9,11},{10,... | collective-permute-start | bytes 1376264 | tf_op jit(solution)/shard_map/ppermute | solution.py:21
  62.8 10.0 %collective-permute-start.18 = (bf16[64,3584]{1,0:T(8,128)(2,1)S(1)}, bf16[64,3584]{1,0:T(8,128)(2,1)S(1)}, u32[]{:S(2)}, u32[]{:S(2)}) collective-permute-start(bf16[64,3584]{1,0:T(8,128)(2,1)S(1)} %get-tuple-element.55), channel_id=1, source_target_pairs={{0,1},{1,0},{2,3},{3,2},{4,5},{5,4},{6,7},{7,6},{8,9},{9,8},{10,11... | collective-permute-start | bytes 1376264 | tf_op jit(solution)/shard_map/ppermute | solution.py:21
  63.8 11.5 %collective-permute-start.25 = (bf16[64,3584]{1,0:T(8,128)(2,1)S(1)}, bf16[64,3584]{1,0:T(8,128)(2,1)S(1)}, u32[]{:S(2)}, u32[]{:S(2)}) collective-permute-start(bf16[64,3584]{1,0:T(8,128)(2,1)S(1)} %get-tuple-element.64), channel_id=1, source_target_pairs={{0,4},{1,3},{2,6},{3,1},{4,0},{5,7},{6,2},{7,5},{8,12},{9,11},{10,... | collective-permute-start | bytes 1376264 | tf_op jit(solution)/shard_map/ppermute | solution.py:21
  64.2 8.5 %collective-permute-start.20 = (bf16[32,3584]{1,0:T(8,128)(2,1)S(1)}, bf16[32,3584]{1,0:T(8,128)(2,1)S(1)}, u32[]{:S(2)}, u32[]{:S(2)}) collective-permute-start(bf16[32,3584]{1,0:T(8,128)(2,1)S(1)} %get-tuple-element.58), channel_id=1, source_target_pairs={{0,2},{1,5},{2,0},{3,7},{4,6},{5,1},{6,4},{7,3},{8,10},{9,13},{10,... | collective-permute-start | bytes 688136 | tf_op jit(solution)/shard_map/ppermute | solution.py:21
  66.5 16.3 %collective-permute-start.24 = (bf16[64,3584]{1,0:T(8,128)(2,1)S(1)}, bf16[64,3584]{1,0:T(8,128)(2,1)S(1)}, u32[]{:S(2)}, u32[]{:S(2)}) collective-permute-start(bf16[64,3584]{1,0:T(8,128)(2,1)S(1)} %sum.1.refs_2_), channel_id=1, source_target_pairs={{0,8},{1,9},{2,10},{3,11},{4,12},{5,13},{6,14},{7,15},{8,0},{9,1},... | collective-permute-start | bytes 1376264 | tf_op jit(solution)/shard_map/ppermute | solution.py:21
  73.5 10.9 %collective-permute-start.23 = (bf16[64,3584]{1,0:T(8,128)(2,1)S(1)}, bf16[64,3584]{1,0:T(8,128)(2,1)S(1)}, u32[]{:S(2)}, u32[]{:S(2)}) collective-permute-start(bf16[64,3584]{1,0:T(8,128)(2,1)S(1)} %get-tuple-element.63), channel_id=1, source_target_pairs={{0,4},{1,3},{2,6},{3,1},{4,0},{5,7},{6,2},{7,5},{8,12},{9,11},{10,... | collective-permute-start | bytes 1376264 | tf_op jit(solution)/shard_map/ppermute | solution.py:21
  75.4 7.3 %collective-permute-start.26 = (bf16[32,3584]{1,0:T(8,128)(2,1)S(1)}, bf16[32,3584]{1,0:T(8,128)(2,1)S(1)}, u32[]{:S(2)}, u32[]{:S(2)}) collective-permute-start(bf16[32,3584]{1,0:T(8,128)(2,1)S(1)} %get-tuple-element.66), channel_id=1, source_target_pairs={{0,2},{1,5},{2,0},{3,7},{4,6},{5,1},{6,4},{7,3},{8,10},{9,13},{10,... | collective-permute-start | bytes 688136 | tf_op jit(solution)/shard_map/ppermute | solution.py:21
  75.8 18.2 %collective-permute-start.28 = (bf16[32,3584]{1,0:T(8,128)(2,1)S(1)}, bf16[32,3584]{1,0:T(8,128)(2,1)S(1)}, u32[]{:S(2)}, u32[]{:S(2)}) collective-permute-start(bf16[32,3584]{1,0:T(8,128)(2,1)S(1)} %leave.2.refs_6_), channel_id=1, source_target_pairs={{0,16},{1,17},{2,18},{3,19},{4,20},{5,21},{6,22},{7,23},{8,24},{9,... | collective-permute-start | bytes 688136 | tf_op jit(solution)/shard_map/ppermute | solution.py:21
  84.6 9.4 %collective-permute-start.27 = (bf16[32,3584]{1,0:T(8,128)(2,1)S(1)}, bf16[32,3584]{1,0:T(8,128)(2,1)S(1)}, u32[]{:S(2)}, u32[]{:S(2)}) collective-permute-start(bf16[32,3584]{1,0:T(8,128)(2,1)S(1)} %get-tuple-element.68), channel_id=1, source_target_pairs={{0,2},{1,5},{2,0},{3,7},{4,6},{5,1},{6,4},{7,3},{8,10},{9,13},{10,... | collective-permute-start | bytes 688136 | tf_op jit(solution)/shard_map/ppermute | solution.py:21
  85.3 8.8 %collective-permute-start.29 = (bf16[32,3584]{1,0:T(8,128)(2,1)S(1)}, bf16[32,3584]{1,0:T(8,128)(2,1)S(1)}, u32[]{:S(2)}, u32[]{:S(2)}) collective-permute-start(bf16[32,3584]{1,0:T(8,128)(2,1)S(1)} %leave.3.refs_3_), channel_id=1, source_target_pairs={{0,24},{1,25},{2,26},{3,27},{4,28},{5,29},{6,30},{7,31},{8,16},{9,... | collective-permute-start | bytes 688136 | tf_op jit(solution)/shard_map/ppermute | solution.py:21

commit v5 on v4

--- a/solution.py
+++ b/solution.py
@@ -47,7 +47,7 @@
 
 ORDER = (
     "E0", "K0", "L0", "E1", "E2", "K1", "K2", "S0", "E3", "D0:h1", "L1:w0", "D1", "K3", "D2", "X1",
-    "X2", "D3", "C0:w2", "X3", "C1", "X0", "M0", "C2", "M1", "V0", "C3:h1", "M2", "V2", "M3",
+    "X2", "D3", "C0:w2", "C1", "X3", "X0", "M0", "C2", "M1", "V0", "C3:h1", "M2", "V2", "M3",
 )
 GATHER_GROUPS = ((0,), (1,), (2,), (3,))
 DIRECT = True
@@ -308,7 +308,8 @@
             pltpu.SemaphoreType.DMA((3,)),
         ],
     )
-    shared_other = other_core(shared_weights)
+    later, _ = lax.optimization_barrier((shared_weights, own))
+    shared_other = other_core(later)
     gather_groups, reduce_groups, order = (GATHER_GROUPS, REDUCE_GROUPS, ORDER) if planes == 4 else any_groups(planes)
     home = {k: (g, i, len(group)) for g, group in enumerate(gather_groups) for i, k in enumerate(group)}
     paired = any(1 in group and 3 in group for group in gather_groups)

time: 96.4 us -> 96.4 us (level)
  transfers between devices with their start and end apart: 30 -> 30, of which waited for: 13 -> 13; matrix products, arithmetic and copies ran while one was open for 0% -> 0% of each run, Pallas kernels for 32% -> 30%
where the time goes in v5:
time: 96.4 us; the launch traced here: 94.8 us
  waiting for transfers between devices  36.5 us (38%)
  Pallas kernels  31.3 us (32%)
  starting transfers between devices  26.7 us (28%)
    ppermute x30, waiting for transfers between devices, swap(): return lax.ppermute(block, AXIS, route)  36.5 us
    pallas_call x30, Pallas kernels, __call__(): pl.pallas_call(body, in_specs=[SCALAR] * len(scalars) + [WHOLE] * len(arr...  31.3 us
    ppermute x30, starting transfers between devices, swap(): return lax.ppermute(block, AXIS, route)  26.7 us
  transfers between devices with their start and end apart: 30, of which 13 were waited for; matrix products, arithmetic and copies ran while one was open for 0% of the time, Pallas kernels for 30%

profile of v5, /device:TPU:0, one launch (start us, length us, event | category | flops | bytes accessed | tf_op | source)
XLA Modules:
  0.0 94.8 jit_solution(13459951520322167154)
XLA Ops:
  0.0 1.1 %own.1.refs_0_.refs_2_ = bf16[32,3712]{1,0:T(8,128)(2,1)S(1)} custom-call(s32[1]{0:T(128)} %bitcast.refs_0_, bf16[2,16,3584]{2,1,0:T(8,128)(2,1)} %refs_1_.1, s32[2,8,16]{2,1,0:T(8,128)} %bitcast.3, f32[2,8,16]{2,1,0:T(8,128)} %bitcast.4), custom_call_target="tpu_custom_call" | custom-call | flops 1 | bytes 1 | tf_op jit(solution)/shard_map/own/pallas_call | solution.py:80
  1.6 2.6 %collective-permute-start = (bf16[32,3712]{1,0:T(8,128)(2,1)S(1)}, bf16[32,3712]{1,0:T(8,128)(2,1)S(1)}, u32[]{:S(2)}, u32[]{:S(2)}) collective-permute-start(bf16[32,3712]{1,0:T(8,128)(2,1)S(1)} %own.1.refs_0_.refs_2_), channel_id=1, source_target_pairs={{0,2},{1,5},{2,0},{3,7},{4,6},{5,1},{6,4},{7,3},{8,10},{9,13},{10,... | collective-permute-start | bytes 712712 | tf_op jit(solution)/shard_map/ppermute | solution.py:21
  4.1 1.6 %collective-permute-start.3 = (bf16[32,3712]{1,0:T(8,128)(2,1)S(1)}, bf16[32,3712]{1,0:T(8,128)(2,1)S(1)}, u32[]{:S(2)}, u32[]{:S(2)}) collective-permute-start(bf16[32,3712]{1,0:T(8,128)(2,1)S(1)} %own.1.refs_0_.refs_2_), channel_id=1, source_target_pairs={{0,8},{1,9},{2,10},{3,11},{4,12},{5,13},{6,14},{7,15},{8,0},{9,1},... | collective-permute-start | bytes 712712 | tf_op jit(solution)/shard_map/ppermute | solution.py:21
  5.7 2.6 %collective-permute-start.2 = (bf16[32,3712]{1,0:T(8,128)(2,1)S(1)}, bf16[32,3712]{1,0:T(8,128)(2,1)S(1)}, u32[]{:S(2)}, u32[]{:S(2)}) collective-permute-start(bf16[32,3712]{1,0:T(8,128)(2,1)S(1)} %own.1.refs_0_.refs_2_), channel_id=1, source_target_pairs={{0,16},{1,17},{2,18},{3,19},{4,20},{5,21},{6,22},{7,23},{8,24},{9,... | collective-permute-start | bytes 712712 | tf_op jit(solution)/shard_map/ppermute | solution.py:21
  8.4 2.0 %collective-permute-start.1 = (bf16[64,3712]{1,0:T(8,128)(2,1)S(1)}, bf16[64,3712]{1,0:T(8,128)(2,1)S(1)}, u32[]{:S(2)}, u32[]{:S(2)}) collective-permute-start(bf16[64,3712]{1,0:T(8,128)(2,1)S(1)} %pack.4.refs_1_.refs_0_), channel_id=1, source_target_pairs={{0,4},{1,3},{2,6},{3,1},{4,0},{5,7},{6,2},{7,5},{8,12},{9,11},{10,... | collective-permute-start | bytes 1425416 | tf_op jit(solution)/shard_map/ppermute | solution.py:21
  10.4 3.2 %load.2.refs_1_.refs_3_ = bf16[1,3584,1024]{2,1,0:T(8,128)(2,1)S(1)} custom-call(bf16[1,3584,1024]{2,1,0:T(8,128)(2,1)} %refs_0_.2, bf16[64,3712]{1,0:T(8,128)(2,1)S(1)} %pack.4.refs_1_.refs_0_), custom_call_target="tpu_custom_call" | custom-call | flops 1 | bytes 1 | tf_op jit(solution)/shard_map/load/pallas_call | solution.py:80
  13.6 3.4 %collective-permute-done.3.refs_0_ = bf16[32,3712]{1,0:T(8,128)(2,1)S(1)} collective-permute-done((bf16[32,3712]{1,0:T(8,128)(2,1)S(1)}, bf16[32,3712]{1,0:T(8,128)(2,1)S(1)}, u32[]{:S(2)}, u32[]{:S(2)}) %collective-permute-start.3) | collective-permute-done | bytes 237600 | tf_op jit(solution)/shard_map/ppermute | solution.py:21
  17.1 2.2 %collective-permute-done.2.refs_0_ = bf16[32,3712]{1,0:T(8,128)(2,1)S(1)} collective-permute-done((bf16[32,3712]{1,0:T(8,128)(2,1)S(1)}, bf16[32,3712]{1,0:T(8,128)(2,1)S(1)}, u32[]{:S(2)}, u32[]{:S(2)}) %collective-permute-start.2) | collective-permute-done | bytes 237600 | tf_op jit(solution)/shard_map/ppermute | solution.py:21
  19.3 1.5 %collective-permute-start.6 = (bf16[32,3712]{1,0:T(8,128)(2,1)S(1)}, bf16[32,3712]{1,0:T(8,128)(2,1)S(1)}, u32[]{:S(2)}, u32[]{:S(2)}) collective-permute-start(bf16[32,3712]{1,0:T(8,128)(2,1)S(1)} %enter.4.refs_2_.refs_0_), channel_id=1, source_target_pairs={{0,2},{1,5},{2,0},{3,7},{4,6},{5,1},{6,4},{7,3},{8,10},{9,13},{10,... | collective-permute-start | bytes 712712 | tf_op jit(solution)/shard_map/ppermute | solution.py:21
  20.8 2.3 %collective-permute-done.7.refs_1_.refs_4_.refs_7_ = bf16[32,3712]{1,0:T(8,128)(2,1)S(1)} collective-permute-done((bf16[32,3712]{1,0:T(8,128)(2,1)S(1)}, bf16[32,3712]{1,0:T(8,128)(2,1)S(1)}, u32[]{:S(2)}, u32[]{:S(2)}) %collective-permute-start.7) | collective-permute-done | bytes 237600 | tf_op jit(solution)/shard_map/ppermute | solution.py:21
  23.5 3.4 %collective-permute-done.6.refs_1_ = bf16[32,3712]{1,0:T(8,128)(2,1)S(1)} collective-permute-done((bf16[32,3712]{1,0:T(8,128)(2,1)S(1)}, bf16[32,3712]{1,0:T(8,128)(2,1)S(1)}, u32[]{:S(2)}, u32[]{:S(2)}) %collective-permute-start.6) | collective-permute-done | bytes 237600 | tf_op jit(solution)/shard_map/ppermute | solution.py:21
  27.4 3.4 %shared.1 = (f32[128,3584]{1,0:T(8,128)S(1)}, bf16[1,3584,1024]{2,1,0:T(8,128)(2,1)S(1)}) custom-call(bf16[64,3712]{1,0:T(8,128)(2,1)S(1)} %pack.4.refs_1_.refs_0_, bf16[64,3712]{1,0:T(8,128)(2,1)S(1)} %collective-permute-done.1.refs_1_.refs_2_, bf16[3,3584,128]{2,1,0:T(8,128)(2,1)S(1)} %copy-done, bf16[3,3584,128]{2,1,0:T(8,128)(2,1)S(1)} %collective-permute-done.5.refs_3_, ...), custom_call_target="tpu_custom_call" | custom-call | flops 1 | bytes 1 | tf_op jit(solution)/shard_map/shared/pallas_call | solution.py:80
  30.9 1.7 %collective-permute-start.9 = (bf16[32,3712]{1,0:T(8,128)(2,1)S(1)}, bf16[32,3712]{1,0:T(8,128)(2,1)S(1)}, u32[]{:S(2)}, u32[]{:S(2)}) collective-permute-start(bf16[32,3712]{1,0:T(8,128)(2,1)S(1)} %enter.5.refs_3_.refs_0_), channel_id=1, source_target_pairs={{0,2},{1,5},{2,0},{3,7},{4,6},{5,1},{6,4},{7,3},{8,10},{9,13},{10,... | collective-permute-start | bytes 712712 | tf_op jit(solution)/shard_map/ppermute | solution.py:21
  33.3 3.2 %load.3.refs_3_.refs_5_ = bf16[1,1024,3584]{2,1,0:T(8,128)(2,1)S(1)} custom-call(bf16[1,1024,3584]{2,1,0:T(8,128)(2,1)} %refs_0_.3, bf16[64,3712]{1,0:T(8,128)(2,1)S(1)} %get-tuple-element.40.refs_1_, bf16[64,3712]{1,0:T(8,128)(2,1)S(1)} %collective-permute-done.1.refs_1_.refs_2_), custom_call_target="tpu_custom_call" | custom-call | flops 1 | bytes 1 | tf_op jit(solution)/shard_map/load/pallas_call | solution.py:80
  37.3 1.1 %collective-permute-done.9.refs_1_ = bf16[32,3712]{1,0:T(8,128)(2,1)S(1)} collective-permute-done((bf16[32,3712]{1,0:T(8,128)(2,1)S(1)}, bf16[32,3712]{1,0:T(8,128)(2,1)S(1)}, u32[]{:S(2)}, u32[]{:S(2)}) %collective-permute-start.9) | collective-permute-done | bytes 237600 | tf_op jit(solution)/shard_map/ppermute | solution.py:21
  38.4 1.1 %collective-permute-done.12.refs_2_.refs_6_ = bf16[64,3712]{1,0:T(8,128)(2,1)S(1)} collective-permute-done((bf16[64,3712]{1,0:T(8,128)(2,1)S(1)}, bf16[64,3712]{1,0:T(8,128)(2,1)S(1)}, u32[]{:S(2)}, u32[]{:S(2)}) %collective-permute-start.12) | collective-permute-done | bytes 475168 | tf_op jit(solution)/shard_map/ppermute | solution.py:21
  40.7 3.3 %expert.4 = (bf16[64,3584]{1,0:T(8,128)(2,1)S(1)}, bf16[64,3584]{1,0:T(8,128)(2,1)S(1)}) custom-call(s32[1]{0:T(128)} %bitcast.refs_0_, bf16[64,3712]{1,0:T(8,128)(2,1)S(1)} %get-tuple-element.43.refs_2_.refs_1_, bf16[64,3712]{1,0:T(8,128)(2,1)S(1)} %collective-permute-done.14.refs_2_, bf16[1,3584,1024]{2,1,0:T(8,128)(2,1)S(1)} %load.2.refs_1_.refs_3_, ...), custom_call_target="tpu_custom_call" | custom-call | flops 1 | bytes 1 | tf_op jit(solution)/shard_map/expert/pallas_call | solution.py:80
  44.0 3.3 %expert.5 = (bf16[64,3584]{1,0:T(8,128)(2,1)S(1)}, bf16[64,3584]{1,0:T(8,128)(2,1)S(1)}) custom-call(s32[1]{0:T(128)} %bitcast.refs_0_, bf16[64,3712]{1,0:T(8,128)(2,1)S(1)} %get-tuple-element.44.refs_6_.refs_1_, bf16[64,3712]{1,0:T(8,128)(2,1)S(1)} %collective-permute-done.13.refs_2_, bf16[1,3584,1024]{2,1,0:T(8,128)(2,1)S(1)} %load.2.refs_1_.refs_3_, ...), custom_call_target="tpu_custom_call" | custom-call | flops 1 | bytes 1 | tf_op jit(solution)/shard_map/expert/pallas_call | solution.py:80
  47.3 1.7 %collective-permute-done.11.refs_2_ = bf16[64,3712]{1,0:T(8,128)(2,1)S(1)} collective-permute-done((bf16[64,3712]{1,0:T(8,128)(2,1)S(1)}, bf16[64,3712]{1,0:T(8,128)(2,1)S(1)}, u32[]{:S(2)}, u32[]{:S(2)}) %collective-permute-start.11) | collective-permute-done | bytes 475168 | tf_op jit(solution)/shard_map/ppermute | solution.py:21
  50.8 1.5 %collective-permute-done.17.refs_4_ = bf16[64,3584]{1,0:T(8,128)(2,1)S(1)} collective-permute-done((bf16[64,3584]{1,0:T(8,128)(2,1)S(1)}, bf16[64,3584]{1,0:T(8,128)(2,1)S(1)}, u32[]{:S(2)}, u32[]{:S(2)}) %collective-permute-start.17) | collective-permute-done | bytes 458784 | tf_op jit(solution)/shard_map/ppermute | solution.py:21
  53.4 0.9 combine1.5
  54.3 3.3 %expert.6 = (bf16[64,3584]{1,0:T(8,128)(2,1)S(1)}, bf16[64,3584]{1,0:T(8,128)(2,1)S(1)}) custom-call(s32[1]{0:T(128)} %bitcast.refs_0_, bf16[64,3712]{1,0:T(8,128)(2,1)S(1)} %get-tuple-element.49.refs_5_.refs_1_, bf16[64,3712]{1,0:T(8,128)(2,1)S(1)} %collective-permute-done.15.refs_2_, bf16[1,3584,1024]{2,1,0:T(8,128)(2,1)S(1)} %load.2.refs_1_.refs_3_, ...), custom_call_target="tpu_custom_call" | custom-call | flops 1 | bytes 1 | tf_op jit(solution)/shard_map/expert/pallas_call | solution.py:80
  57.7 1.7 %collective-permute-start.21 = (bf16[64,3584]{1,0:T(8,128)(2,1)S(1)}, bf16[64,3584]{1,0:T(8,128)(2,1)S(1)}, u32[]{:S(2)}, u32[]{:S(2)}) collective-permute-start(bf16[64,3584]{1,0:T(8,128)(2,1)S(1)} %get-tuple-element.61), channel_id=1, source_target_pairs={{0,4},{1,3},{2,6},{3,1},{4,0},{5,7},{6,2},{7,5},{8,12},{9,11},{10,... | collective-permute-start | bytes 1376264 | tf_op jit(solution)/shard_map/ppermute | solution.py:21
  59.4 3.3 %expert.7 = (bf16[64,3584]{1,0:T(8,128)(2,1)S(1)}, bf16[64,3584]{1,0:T(8,128)(2,1)S(1)}) custom-call(s32[1]{0:T(128)} %bitcast.refs_0_, bf16[64,3712]{1,0:T(8,128)(2,1)S(1)} %get-tuple-element.40.refs_1_, bf16[64,3712]{1,0:T(8,128)(2,1)S(1)} %collective-permute-done.8.refs_2_, bf16[1,3584,1024]{2,1,0:T(8,128)(2,1)S(1)} %load.2.refs_1_.refs_3_, ...), custom_call_target="tpu_custom_call" | custom-call | flops 1 | bytes 1 | tf_op jit(solution)/shard_map/expert/pallas_call | solution.py:80
  64.1 1.7 %collective-permute-start.20 = (bf16[32,3584]{1,0:T(8,128)(2,1)S(1)}, bf16[32,3584]{1,0:T(8,128)(2,1)S(1)}, u32[]{:S(2)}, u32[]{:S(2)}) collective-permute-start(bf16[32,3584]{1,0:T(8,128)(2,1)S(1)} %get-tuple-element.60), channel_id=1, source_target_pairs={{0,2},{1,5},{2,0},{3,7},{4,6},{5,1},{6,4},{7,3},{8,10},{9,13},{10,... | collective-permute-start | bytes 688136 | tf_op jit(solution)/shard_map/ppermute | solution.py:21
  66.6 6.0 %collective-permute-done.20.refs_1_ = bf16[32,3584]{1,0:T(8,128)(2,1)S(1)} collective-permute-done((bf16[32,3584]{1,0:T(8,128)(2,1)S(1)}, bf16[32,3584]{1,0:T(8,128)(2,1)S(1)}, u32[]{:S(2)}, u32[]{:S(2)}) %collective-permute-start.20) | collective-permute-done | bytes 229408 | tf_op jit(solution)/shard_map/ppermute | solution.py:21
  73.4 1.9 %collective-permute-start.23 = (bf16[64,3584]{1,0:T(8,128)(2,1)S(1)}, bf16[64,3584]{1,0:T(8,128)(2,1)S(1)}, u32[]{:S(2)}, u32[]{:S(2)}) collective-permute-start(bf16[64,3584]{1,0:T(8,128)(2,1)S(1)} %get-tuple-element.65), channel_id=1, source_target_pairs={{0,4},{1,3},{2,6},{3,1},{4,0},{5,7},{6,2},{7,5},{8,12},{9,11},{10,... | collective-permute-start | bytes 1376264 | tf_op jit(solution)/shard_map/ppermute | solution.py:21
  75.7 1.2 %collective-permute-start.28 = (bf16[32,3584]{1,0:T(8,128)(2,1)S(1)}, bf16[32,3584]{1,0:T(8,128)(2,1)S(1)}, u32[]{:S(2)}, u32[]{:S(2)}) collective-permute-start(bf16[32,3584]{1,0:T(8,128)(2,1)S(1)} %leave.2.refs_6_), channel_id=1, source_target_pairs={{0,16},{1,17},{2,18},{3,19},{4,20},{5,21},{6,22},{7,23},{8,24},{9,... | collective-permute-start | bytes 688136 | tf_op jit(solution)/shard_map/ppermute | solution.py:21
  76.8 5.9 %collective-permute-done.26.refs_1_ = bf16[32,3584]{1,0:T(8,128)(2,1)S(1)} collective-permute-done((bf16[32,3584]{1,0:T(8,128)(2,1)S(1)}, bf16[32,3584]{1,0:T(8,128)(2,1)S(1)}, u32[]{:S(2)}, u32[]{:S(2)}) %collective-permute-start.26) | collective-permute-done | bytes 229408 | tf_op jit(solution)/shard_map/ppermute | solution.py:21
  82.7 1.6 %collective-permute-done.23.refs_1_ = bf16[64,3584]{1,0:T(8,128)(2,1)S(1)} collective-permute-done((bf16[64,3584]{1,0:T(8,128)(2,1)S(1)}, bf16[64,3584]{1,0:T(8,128)(2,1)S(1)}, u32[]{:S(2)}, u32[]{:S(2)}) %collective-permute-start.23) | collective-permute-done | bytes 458784 | tf_op jit(solution)/shard_map/ppermute | solution.py:21
  85.2 2.9 %collective-permute-start.29 = (bf16[32,3584]{1,0:T(8,128)(2,1)S(1)}, bf16[32,3584]{1,0:T(8,128)(2,1)S(1)}, u32[]{:S(2)}, u32[]{:S(2)}) collective-permute-start(bf16[32,3584]{1,0:T(8,128)(2,1)S(1)} %leave.3.refs_3_), channel_id=1, source_target_pairs={{0,24},{1,25},{2,26},{3,27},{4,28},{5,29},{6,30},{7,31},{8,16},{9,... | collective-permute-start | bytes 688136 | tf_op jit(solution)/shard_map/ppermute | solution.py:21
  88.1 5.9 %collective-permute-done.28.refs_2_ = bf16[32,3584]{1,0:T(8,128)(2,1)S(1)} collective-permute-done((bf16[32,3584]{1,0:T(8,128)(2,1)S(1)}, bf16[32,3584]{1,0:T(8,128)(2,1)S(1)}, u32[]{:S(2)}, u32[]{:S(2)}) %collective-permute-start.28) | collective-permute-done | bytes 229408 | tf_op jit(solution)/shard_map/ppermute | solution.py:21
  (60 shorter events, 12.2 us)
Async XLA Ops:
  1.1 26.4 %collective-permute-start.5 = (bf16[3,3584,128]{2,1,0:T(8,128)(2,1)}, bf16[3,3584,128]{2,1,0:T(8,128)(2,1)S(1)}, u32[]{:S(2)}, u32[]{:S(2)}) collective-permute-start(bf16[3,3584,128]{2,1,0:T(8,128)(2,1)} %refs_2_.1), channel_id=1, source_target_pairs={{0,1},{1,0},{2,3},{3,2},{4,5},{5,4},{6,7},{7,6},{8,9},{9,8},{10,11... | collective-permute-start | bytes 8257544 | tf_op jit(solution)/shard_map/ppermute | solution.py:21
  1.6 6.7 %collective-permute-start = (bf16[32,3712]{1,0:T(8,128)(2,1)S(1)}, bf16[32,3712]{1,0:T(8,128)(2,1)S(1)}, u32[]{:S(2)}, u32[]{:S(2)}) collective-permute-start(bf16[32,3712]{1,0:T(8,128)(2,1)S(1)} %own.1.refs_0_.refs_2_), channel_id=1, source_target_pairs={{0,2},{1,5},{2,0},{3,7},{4,6},{5,1},{6,4},{7,3},{8,10},{9,13},{10,... | collective-permute-start | bytes 712712 | tf_op jit(solution)/shard_map/ppermute | solution.py:21
  4.1 12.8 %collective-permute-start.3 = (bf16[32,3712]{1,0:T(8,128)(2,1)S(1)}, bf16[32,3712]{1,0:T(8,128)(2,1)S(1)}, u32[]{:S(2)}, u32[]{:S(2)}) collective-permute-start(bf16[32,3712]{1,0:T(8,128)(2,1)S(1)} %own.1.refs_0_.refs_2_), channel_id=1, source_target_pairs={{0,8},{1,9},{2,10},{3,11},{4,12},{5,13},{6,14},{7,15},{8,0},{9,1},... | collective-permute-start | bytes 712712 | tf_op jit(solution)/shard_map/ppermute | solution.py:21
  5.7 13.6 %collective-permute-start.2 = (bf16[32,3712]{1,0:T(8,128)(2,1)S(1)}, bf16[32,3712]{1,0:T(8,128)(2,1)S(1)}, u32[]{:S(2)}, u32[]{:S(2)}) collective-permute-start(bf16[32,3712]{1,0:T(8,128)(2,1)S(1)} %own.1.refs_0_.refs_2_), channel_id=1, source_target_pairs={{0,16},{1,17},{2,18},{3,19},{4,20},{5,21},{6,22},{7,23},{8,24},{9,... | collective-permute-start | bytes 712712 | tf_op jit(solution)/shard_map/ppermute | solution.py:21
  8.4 19.1 %collective-permute-start.1 = (bf16[64,3712]{1,0:T(8,128)(2,1)S(1)}, bf16[64,3712]{1,0:T(8,128)(2,1)S(1)}, u32[]{:S(2)}, u32[]{:S(2)}) collective-permute-start(bf16[64,3712]{1,0:T(8,128)(2,1)S(1)} %pack.4.refs_1_.refs_0_), channel_id=1, source_target_pairs={{0,4},{1,3},{2,6},{3,1},{4,0},{5,7},{6,2},{7,5},{8,12},{9,11},{10,... | collective-permute-start | bytes 1425416 | tf_op jit(solution)/shard_map/ppermute | solution.py:21
  13.6 13.9 %copy-start = (bf16[3,3584,128]{2,1,0:T(8,128)(2,1)S(1)}, bf16[3,3584,128]{2,1,0:T(8,128)(2,1)}, u32[]{:S(2)}) copy-start(bf16[3,3584,128]{2,1,0:T(8,128)(2,1)} %refs_2_.1) | copy-start | bytes 8257540
  17.0 6.1 %collective-permute-start.7 = (bf16[32,3712]{1,0:T(8,128)(2,1)S(1)}, bf16[32,3712]{1,0:T(8,128)(2,1)S(1)}, u32[]{:S(2)}, u32[]{:S(2)}) collective-permute-start(bf16[32,3712]{1,0:T(8,128)(2,1)S(1)} %enter.3.refs_1_.refs_0_), channel_id=1, source_target_pairs={{0,2},{1,5},{2,0},{3,7},{4,6},{5,1},{6,4},{7,3},{8,10},{9,13},{10,... | collective-permute-start | bytes 712712 | tf_op jit(solution)/shard_map/ppermute | solution.py:21
  19.3 7.6 %collective-permute-start.6 = (bf16[32,3712]{1,0:T(8,128)(2,1)S(1)}, bf16[32,3712]{1,0:T(8,128)(2,1)S(1)}, u32[]{:S(2)}, u32[]{:S(2)}) collective-permute-start(bf16[32,3712]{1,0:T(8,128)(2,1)S(1)} %enter.4.refs_2_.refs_0_), channel_id=1, source_target_pairs={{0,2},{1,5},{2,0},{3,7},{4,6},{5,1},{6,4},{7,3},{8,10},{9,13},{10,... | collective-permute-start | bytes 712712 | tf_op jit(solution)/shard_map/ppermute | solution.py:21
  23.1 13.4 %collective-permute-start.10 = (bf16[64,3712]{1,0:T(8,128)(2,1)S(1)}, bf16[64,3712]{1,0:T(8,128)(2,1)S(1)}, u32[]{:S(2)}, u32[]{:S(2)}) collective-permute-start(bf16[64,3712]{1,0:T(8,128)(2,1)S(1)} %pack.5.refs_2_.refs_1_), channel_id=1, source_target_pairs={{0,4},{1,3},{2,6},{3,1},{4,0},{5,7},{6,2},{7,5},{8,12},{9,11},{10,... | collective-permute-start | bytes 1425416 | tf_op jit(solution)/shard_map/ppermute | solution.py:21
  23.5 7.3 %collective-permute-start.4 = (bf16[32,3712]{1,0:T(8,128)(2,1)S(1)}, bf16[32,3712]{1,0:T(8,128)(2,1)S(1)}, u32[]{:S(2)}, u32[]{:S(2)}) collective-permute-start(bf16[32,3712]{1,0:T(8,128)(2,1)S(1)} %enter.4.refs_2_.refs_0_), channel_id=1, source_target_pairs={{0,8},{1,9},{2,10},{3,11},{4,12},{5,13},{6,14},{7,15},{8,0},{9,1},... | collective-permute-start | bytes 712712 | tf_op jit(solution)/shard_map/ppermute | solution.py:21
  27.0 12.5 %collective-permute-start.12 = (bf16[64,3712]{1,0:T(8,128)(2,1)S(1)}, bf16[64,3712]{1,0:T(8,128)(2,1)S(1)}, u32[]{:S(2)}, u32[]{:S(2)}) collective-permute-start(bf16[64,3712]{1,0:T(8,128)(2,1)S(1)} %pack.6.refs_5_.refs_1_), channel_id=1, source_target_pairs={{0,4},{1,3},{2,6},{3,1},{4,0},{5,7},{6,2},{7,5},{8,12},{9,11},{10,... | collective-permute-start | bytes 1425416 | tf_op jit(solution)/shard_map/ppermute | solution.py:21
  30.9 7.5 %collective-permute-start.9 = (bf16[32,3712]{1,0:T(8,128)(2,1)S(1)}, bf16[32,3712]{1,0:T(8,128)(2,1)S(1)}, u32[]{:S(2)}, u32[]{:S(2)}) collective-permute-start(bf16[32,3712]{1,0:T(8,128)(2,1)S(1)} %enter.5.refs_3_.refs_0_), channel_id=1, source_target_pairs={{0,2},{1,5},{2,0},{3,7},{4,6},{5,1},{6,4},{7,3},{8,10},{9,13},{10,... | collective-permute-start | bytes 712712 | tf_op jit(solution)/shard_map/ppermute | solution.py:21
  37.2 3.5 %collective-permute-start.14 = (bf16[64,3712]{1,0:T(8,128)(2,1)S(1)}, bf16[64,3712]{1,0:T(8,128)(2,1)S(1)}, u32[]{:S(2)}, u32[]{:S(2)}) collective-permute-start(bf16[64,3712]{1,0:T(8,128)(2,1)S(1)} %get-tuple-element.46), channel_id=1, source_target_pairs={{0,1},{1,0},{2,3},{3,2},{4,5},{5,4},{6,7},{7,6},{8,9},{9,8},{10,11... | collective-permute-start | bytes 1425416 | tf_op jit(solution)/shard_map/ppermute | solution.py:21
  40.2 3.8 %collective-permute-start.13 = (bf16[64,3712]{1,0:T(8,128)(2,1)S(1)}, bf16[64,3712]{1,0:T(8,128)(2,1)S(1)}, u32[]{:S(2)}, u32[]{:S(2)}) collective-permute-start(bf16[64,3712]{1,0:T(8,128)(2,1)S(1)} %get-tuple-element.45), channel_id=1, source_target_pairs={{0,1},{1,0},{2,3},{3,2},{4,5},{5,4},{6,7},{7,6},{8,9},{9,8},{10,11... | collective-permute-start | bytes 1425416 | tf_op jit(solution)/shard_map/ppermute | solution.py:21
  40.3 8.7 %collective-permute-start.11 = (bf16[64,3712]{1,0:T(8,128)(2,1)S(1)}, bf16[64,3712]{1,0:T(8,128)(2,1)S(1)}, u32[]{:S(2)}, u32[]{:S(2)}) collective-permute-start(bf16[64,3712]{1,0:T(8,128)(2,1)S(1)} %pack.7.refs_3_.refs_1_), channel_id=1, source_target_pairs={{0,4},{1,3},{2,6},{3,1},{4,0},{5,7},{6,2},{7,5},{8,12},{9,11},{10,... | collective-permute-start | bytes 1425416 | tf_op jit(solution)/shard_map/ppermute | solution.py:21
  49.7 4.6 %collective-permute-start.15 = (bf16[64,3712]{1,0:T(8,128)(2,1)S(1)}, bf16[64,3712]{1,0:T(8,128)(2,1)S(1)}, u32[]{:S(2)}, u32[]{:S(2)}) collective-permute-start(bf16[64,3712]{1,0:T(8,128)(2,1)S(1)} %get-tuple-element.50), channel_id=1, source_target_pairs={{0,1},{1,0},{2,3},{3,2},{4,5},{5,4},{6,7},{7,6},{8,9},{9,8},{10,11... | collective-permute-start | bytes 1425416 | tf_op jit(solution)/shard_map/ppermute | solution.py:21
  49.8 2.5 %collective-permute-start.17 = (bf16[64,3584]{1,0:T(8,128)(2,1)S(1)}, bf16[64,3584]{1,0:T(8,128)(2,1)S(1)}, u32[]{:S(2)}, u32[]{:S(2)}) collective-permute-start(bf16[64,3584]{1,0:T(8,128)(2,1)S(1)} %get-tuple-element.52), channel_id=1, source_target_pairs={{0,1},{1,0},{2,3},{3,2},{4,5},{5,4},{6,7},{7,6},{8,9},{9,8},{10,11... | collective-permute-start | bytes 1376264 | tf_op jit(solution)/shard_map/ppermute | solution.py:21
  50.3 3.1 %collective-permute-start.16 = (bf16[64,3584]{1,0:T(8,128)(2,1)S(1)}, bf16[64,3584]{1,0:T(8,128)(2,1)S(1)}, u32[]{:S(2)}, u32[]{:S(2)}) collective-permute-start(bf16[64,3584]{1,0:T(8,128)(2,1)S(1)} %get-tuple-element.51), channel_id=1, source_target_pairs={{0,1},{1,0},{2,3},{3,2},{4,5},{5,4},{6,7},{7,6},{8,9},{9,8},{10,11... | collective-permute-start | bytes 1376264 | tf_op jit(solution)/shard_map/ppermute | solution.py:21
  50.3 9.1 %collective-permute-start.8 = (bf16[64,3712]{1,0:T(8,128)(2,1)S(1)}, bf16[64,3712]{1,0:T(8,128)(2,1)S(1)}, u32[]{:S(2)}, u32[]{:S(2)}) collective-permute-start(bf16[64,3712]{1,0:T(8,128)(2,1)S(1)} %get-tuple-element.41), channel_id=1, source_target_pairs={{0,1},{1,0},{2,3},{3,2},{4,5},{5,4},{6,7},{7,6},{8,9},{9,8},{10,11... | collective-permute-start | bytes 1425416 | tf_op jit(solution)/shard_map/ppermute | solution.py:21
  53.0 10.0 %collective-permute-start.19 = (bf16[64,3584]{1,0:T(8,128)(2,1)S(1)}, bf16[64,3584]{1,0:T(8,128)(2,1)S(1)}, u32[]{:S(2)}, u32[]{:S(2)}) collective-permute-start(bf16[64,3584]{1,0:T(8,128)(2,1)S(1)} %get-tuple-element.58), channel_id=1, source_target_pairs={{0,4},{1,3},{2,6},{3,1},{4,0},{5,7},{6,2},{7,5},{8,12},{9,11},{10,... | collective-permute-start | bytes 1376264 | tf_op jit(solution)/shard_map/ppermute | solution.py:21
  57.6 5.4 %collective-permute-start.22 = (bf16[64,3584]{1,0:T(8,128)(2,1)S(1)}, bf16[64,3584]{1,0:T(8,128)(2,1)S(1)}, u32[]{:S(2)}, u32[]{:S(2)}) collective-permute-start(bf16[64,3584]{1,0:T(8,128)(2,1)S(1)} %get-tuple-element.62), channel_id=1, source_target_pairs={{0,1},{1,0},{2,3},{3,2},{4,5},{5,4},{6,7},{7,6},{8,9},{9,8},{10,11... | collective-permute-start | bytes 1376264 | tf_op jit(solution)/shard_map/ppermute | solution.py:21
  57.7 8.8 %collective-permute-start.21 = (bf16[64,3584]{1,0:T(8,128)(2,1)S(1)}, bf16[64,3584]{1,0:T(8,128)(2,1)S(1)}, u32[]{:S(2)}, u32[]{:S(2)}) collective-permute-start(bf16[64,3584]{1,0:T(8,128)(2,1)S(1)} %get-tuple-element.61), channel_id=1, source_target_pairs={{0,4},{1,3},{2,6},{3,1},{4,0},{5,7},{6,2},{7,5},{8,12},{9,11},{10,... | collective-permute-start | bytes 1376264 | tf_op jit(solution)/shard_map/ppermute | solution.py:21
  62.7 9.9 %collective-permute-start.18 = (bf16[64,3584]{1,0:T(8,128)(2,1)S(1)}, bf16[64,3584]{1,0:T(8,128)(2,1)S(1)}, u32[]{:S(2)}, u32[]{:S(2)}) collective-permute-start(bf16[64,3584]{1,0:T(8,128)(2,1)S(1)} %get-tuple-element.57), channel_id=1, source_target_pairs={{0,1},{1,0},{2,3},{3,2},{4,5},{5,4},{6,7},{7,6},{8,9},{9,8},{10,11... | collective-permute-start | bytes 1376264 | tf_op jit(solution)/shard_map/ppermute | solution.py:21
  63.7 11.5 %collective-permute-start.25 = (bf16[64,3584]{1,0:T(8,128)(2,1)S(1)}, bf16[64,3584]{1,0:T(8,128)(2,1)S(1)}, u32[]{:S(2)}, u32[]{:S(2)}) collective-permute-start(bf16[64,3584]{1,0:T(8,128)(2,1)S(1)} %get-tuple-element.66), channel_id=1, source_target_pairs={{0,4},{1,3},{2,6},{3,1},{4,0},{5,7},{6,2},{7,5},{8,12},{9,11},{10,... | collective-permute-start | bytes 1376264 | tf_op jit(solution)/shard_map/ppermute | solution.py:21
  64.1 8.5 %collective-permute-start.20 = (bf16[32,3584]{1,0:T(8,128)(2,1)S(1)}, bf16[32,3584]{1,0:T(8,128)(2,1)S(1)}, u32[]{:S(2)}, u32[]{:S(2)}) collective-permute-start(bf16[32,3584]{1,0:T(8,128)(2,1)S(1)} %get-tuple-element.60), channel_id=1, source_target_pairs={{0,2},{1,5},{2,0},{3,7},{4,6},{5,1},{6,4},{7,3},{8,10},{9,13},{10,... | collective-permute-start | bytes 688136 | tf_op jit(solution)/shard_map/ppermute | solution.py:21
  66.5 16.2 %collective-permute-start.24 = (bf16[64,3584]{1,0:T(8,128)(2,1)S(1)}, bf16[64,3584]{1,0:T(8,128)(2,1)S(1)}, u32[]{:S(2)}, u32[]{:S(2)}) collective-permute-start(bf16[64,3584]{1,0:T(8,128)(2,1)S(1)} %sum.1.refs_2_), channel_id=1, source_target_pairs={{0,8},{1,9},{2,10},{3,11},{4,12},{5,13},{6,14},{7,15},{8,0},{9,1},... | collective-permute-start | bytes 1376264 | tf_op jit(solution)/shard_map/ppermute | solution.py:21
  73.4 11.0 %collective-permute-start.23 = (bf16[64,3584]{1,0:T(8,128)(2,1)S(1)}, bf16[64,3584]{1,0:T(8,128)(2,1)S(1)}, u32[]{:S(2)}, u32[]{:S(2)}) collective-permute-start(bf16[64,3584]{1,0:T(8,128)(2,1)S(1)} %get-tuple-element.65), channel_id=1, source_target_pairs={{0,4},{1,3},{2,6},{3,1},{4,0},{5,7},{6,2},{7,5},{8,12},{9,11},{10,... | collective-permute-start | bytes 1376264 | tf_op jit(solution)/shard_map/ppermute | solution.py:21
  75.3 7.4 %collective-permute-start.26 = (bf16[32,3584]{1,0:T(8,128)(2,1)S(1)}, bf16[32,3584]{1,0:T(8,128)(2,1)S(1)}, u32[]{:S(2)}, u32[]{:S(2)}) collective-permute-start(bf16[32,3584]{1,0:T(8,128)(2,1)S(1)} %get-tuple-element.68), channel_id=1, source_target_pairs={{0,2},{1,5},{2,0},{3,7},{4,6},{5,1},{6,4},{7,3},{8,10},{9,13},{10,... | collective-permute-start | bytes 688136 | tf_op jit(solution)/shard_map/ppermute | solution.py:21
  75.7 18.4 %collective-permute-start.28 = (bf16[32,3584]{1,0:T(8,128)(2,1)S(1)}, bf16[32,3584]{1,0:T(8,128)(2,1)S(1)}, u32[]{:S(2)}, u32[]{:S(2)}) collective-permute-start(bf16[32,3584]{1,0:T(8,128)(2,1)S(1)} %leave.2.refs_6_), channel_id=1, source_target_pairs={{0,16},{1,17},{2,18},{3,19},{4,20},{5,21},{6,22},{7,23},{8,24},{9,... | collective-permute-start | bytes 688136 | tf_op jit(solution)/shard_map/ppermute | solution.py:21
  84.6 9.5 %collective-permute-start.27 = (bf16[32,3584]{1,0:T(8,128)(2,1)S(1)}, bf16[32,3584]{1,0:T(8,128)(2,1)S(1)}, u32[]{:S(2)}, u32[]{:S(2)}) collective-permute-start(bf16[32,3584]{1,0:T(8,128)(2,1)S(1)} %get-tuple-element.70), channel_id=1, source_target_pairs={{0,2},{1,5},{2,0},{3,7},{4,6},{5,1},{6,4},{7,3},{8,10},{9,13},{10,... | collective-permute-start | bytes 688136 | tf_op jit(solution)/shard_map/ppermute | solution.py:21
  85.2 8.9 %collective-permute-start.29 = (bf16[32,3584]{1,0:T(8,128)(2,1)S(1)}, bf16[32,3584]{1,0:T(8,128)(2,1)S(1)}, u32[]{:S(2)}, u32[]{:S(2)}) collective-permute-start(bf16[32,3584]{1,0:T(8,128)(2,1)S(1)} %leave.3.refs_3_), channel_id=1, source_target_pairs={{0,24},{1,25},{2,26},{3,27},{4,28},{5,29},{6,30},{7,31},{8,16},{9,... | collective-permute-start | bytes 688136 | tf_op jit(solution)/shard_map/ppermute | solution.py:21
